TPU v7x, 256 devices: a whole 4x4x8 slice. The times are simulated.
256 devices in a mesh: blk: 64 (over y, z, x_hi), grp: 4 (over x_lo, core).
Axes of the slice: x: 4 (x_hi: 2, x_lo: 2; x = x_hi * 2 + x_lo), y: 4, z: 8, core: 2. Of those that a mesh axis runs over, the one named last changes fastest.
Arguments:
- users: float32 [65536, 256], P(('blk', 'grp')), may hold values from -1.5 to 1.5
- items: float32 [65536, 256], P('blk'), may hold values from -1.5 to 1.5
- noise_users: float32 [2, 65536, 256], P(None, ('blk', 'grp')), may hold values from -6 to 6
- noise_items: float32 [2, 65536, 256], P(None, 'blk'), may hold values from -6 to 6
- tile_index: int32 [2, 2048], P(None, ('blk', 'grp')), may hold values from 0 to 15, as said below
- counts: int32 [2, 256], P(None, ('blk', 'grp')), may hold values from 1 to 8, as said below
- ratings: bfloat16 [2, 2048, 128, 128], P(None, ('blk', 'grp')), may hold values from -6 to 6
- weights: bfloat16 [2, 2048, 128, 128], P(None, ('blk', 'grp')), may hold values from 0 to 2
Outputs:
- users_out: float32 [65536, 256], P(('blk', 'grp'))
- items_out: float32 [65536, 256], P(('blk', 'grp'))
Inputs may be any that keep to these rules, and one draw needn't show every extreme that they name: `tile_index`: slot t names user tile row t // 8 of the device's users and item tile column t % 8; the live slots of a device in a stratum name distinct tiles. `counts`: in every stratum some device has 8 live slots.
All inputs are finite; a program needn't handle non-finite values.
Results may differ from a plain program's by a relative error of at most 0.0003.
Values sent between devices are 32-bit elements; how exact they have to be, the bound alone decides.
No kernel may reach another device: no remote copies, remote signals or barrier semaphores. Data moves between devices by JAX's collectives and lax.ppermute only.
A program may use at most 64 MiB of HBM per device.

v0:
```python
import math

import jax
import jax.numpy as jnp
from jax import lax
from jax.sharding import PartitionSpec as P

STRATA = 2


STEP_SIZE = 0.001
LIKELIHOOD = 20.0
NOISE_SCALE = math.sqrt(0.002)
HIGHEST = lax.Precision.HIGHEST


def passed_along(value, axis, steps):
    count = lax.axis_size(axis)
    pairs = [(source, (source + steps) % count) for source in range(count)]
    return lax.ppermute(value, axis, pairs)


def slot_terms(user_rows, item_block, slot_index, live_slots, rating_tiles, weight_tiles):
    tile = rating_tiles.shape[-1]
    rank = user_rows.shape[1]
    user_tiles = user_rows.shape[0] // tile
    item_tiles = item_block.shape[0] // tile
    tile_row = slot_index // item_tiles
    tile_col = slot_index % item_tiles
    user_table = user_rows.reshape(user_tiles, tile, rank)
    item_table = item_block.reshape(item_tiles, tile, rank)
    user_part = jnp.take(user_table, tile_row, axis=0)
    item_part = jnp.take(item_table, tile_col, axis=0)
    predicted = jnp.einsum("mik,mjk->mij", user_part, item_part, precision=HIGHEST)
    errors = (
        live_slots[:, None, None]
        * weight_tiles.astype(jnp.float32)
        * (rating_tiles.astype(jnp.float32) - predicted)
    )
    user_grads = jnp.einsum("mij,mjk->mik", errors, item_part, precision=HIGHEST)
    item_grads = jnp.einsum("mij,mik->mjk", errors, user_part, precision=HIGHEST)
    pick_user = (tile_row[:, None] == jnp.arange(user_tiles)[None, :]).astype(jnp.float32)
    pick_item = (tile_col[:, None] == jnp.arange(item_tiles)[None, :]).astype(jnp.float32)
    grad_users = jnp.einsum("mq,mik->qik", pick_user, user_grads, precision=HIGHEST).reshape(
        user_tiles * tile, rank
    )
    grad_items = jnp.einsum("mq,mjk->qjk", pick_item, item_grads, precision=HIGHEST).reshape(
        item_tiles * tile, rank
    )
    return (grad_users, grad_items)


def stratum_grads(user_rows, item_block, slot_index, live_count, rating_tiles, weight_tiles):
    slot_total = slot_index.shape[0]
    live_slots = (jnp.arange(slot_total) < live_count).astype(jnp.float32)
    return slot_terms(user_rows, item_block, slot_index, live_slots, rating_tiles, weight_tiles)


def body(users, items, noise_users, noise_items, tile_index, counts, ratings, weights):
    user_now = users
    item_block = items
    item_share = items
    quarter = items.shape[0] // lax.axis_size("grp")
    member = lax.axis_index("grp")
    for stratum in range(STRATA):
        grad_users, grad_items = stratum_grads(
            user_now,
            item_block,
            tile_index[stratum],
            counts[stratum, 0],
            ratings[stratum],
            weights[stratum],
        )
        user_now = (
            user_now
            + STEP_SIZE * (LIKELIHOOD * grad_users - user_now)
            + NOISE_SCALE * noise_users[stratum]
        )
        summed = lax.psum(grad_items, "grp")
        updated = (
            item_block
            + STEP_SIZE * (LIKELIHOOD * summed - item_block)
            + NOISE_SCALE * noise_items[stratum]
        )
        item_block = passed_along(updated, "blk", 1)
        item_share = lax.dynamic_slice_in_dim(item_block, member * quarter, quarter, 0)
    return (user_now, item_share)


def solution(mesh):
    in_specs = (
        P(("blk", "grp"), None),
        P("blk", None),
        P(None, ("blk", "grp"), None),
        P(None, "blk", None),
        P(None, ("blk", "grp")),
        P(None, ("blk", "grp")),
        P(None, ("blk", "grp"), None, None),
        P(None, ("blk", "grp"), None, None),
    )
    out_specs = (P(("blk", "grp"), None), P(("blk", "grp"), None))
    return jax.shard_map(body, mesh=mesh, in_specs=in_specs, out_specs=out_specs, check_vma=False)
```

profile of v0, /device:TPU:1, one launch (start us, length us, event | category | flops | bytes accessed | tf_op | source)
XLA Modules:
  0.0 198.3 jit_solution(15313312942955038997)
XLA Ops:
  7.2 0.0 all-reduce.3.cloned.1.call-start
  7.2 0.8 compare_and_fusion.1
  8.0 1.3 fusion.58
  9.3 0.7 compare_and_fusion.2
  10.0 0.0 copy-start.3
  10.0 1.6 gather_fusion
  11.7 1.8 gather_fusion.1
  13.5 0.0 copy-done.3
  13.5 2.2 %fusion = f32[8,128,128]{2,1,0:T(8,128)S(1)} fusion(f32[8,128,256]{2,1,0:T(8,128)S(1)} %gather_fusion.1, f32[8,128,256]{2,1,0:T(8,128)S(1)} %gather_fusion, pred[8]{0:T(512)(128)(4,1)S(1)} %get-tuple-element.12, pred[8]{0:T(512)(128)(4,1)S(1)} %get-tuple-element.14, bf16[2,8,128,128]{3,2,1,0:T(8,128)(2,1)S(1)} %copy-done.3, ...), kind=kOutput, calls=%fused_computation.6 | convolution fusion | flops 403832832 | bytes 3145776 | tf_op jit(solution)/shard_map/mik,mjk->mij/dot_general | solution.py:34
  15.7 1.2 fusion.17
  16.9 1.2 fusion.5
  18.1 1.3 copy.11
  19.4 0.0 all-reduce.3.cloned.1.call-update
  19.4 0.0 all-reduce.5.cloned.1.call-start
  19.5 1.1 fusion.14
  20.6 0.0 copy-start
  20.6 49.7 %all-reduce.3.cloned.1.call-done = f32[1024,256]{1,0:T(8,128)} async-done(((f32[1024,256]{1,0:T(8,128)}), f32[1024,256]{1,0:T(8,128)}) %all-reduce.3.cloned.1.call-update) | async-done | bytes 1048592 | tf_op jit(solution)/shard_map/psum | solution.py:79
  70.3 0.0 copy-start.4
  70.4 3.1 %bitcast_add_fusion.1 = f32[1024,256]{1,0:T(8,128)} fusion(f32[2,1024,256]{2,1,0:T(8,128)} %param.15, f32[1024,256]{1,0:T(8,128)} %param.13, f32[1024,256]{1,0:T(8,128)} %all-reduce.3.cloned.1.call-done), kind=kLoop, calls=%fused_computation.11 | loop fusion | flops 1572864 | bytes 4194304 | tf_op jit(solution)/shard_map/add | solution.py:81
  73.5 2.4 %collective-permute-start = (f32[1024,256]{1,0:T(8,128)}, f32[1024,256]{1,0:T(8,128)S(1)}, u32[]{:S(2)}, u32[]{:S(2)}) collective-permute-start(f32[1024,256]{1,0:T(8,128)} %bitcast_add_fusion.1), channel_id=1, source_target_pairs={{0,4},{4,8},{8,12},{12,16},{16,20},{20,24},{24,28},{28,32},{32,36}... | collective-permute-start | bytes 3145736 | tf_op jit(solution)/shard_map/ppermute | solution.py:20
  75.9 1.2 convolution_multiply_fusion.1
  77.1 0.0 copy-done
  77.1 0.0 copy-done.4
  77.1 0.1 bitcast_add_fusion.3
  77.2 0.6 gather_fusion.2
  77.8 0.7 compare_and_fusion
  78.5 25.6 %collective-permute-done = f32[1024,256]{1,0:T(8,128)S(1)} collective-permute-done((f32[1024,256]{1,0:T(8,128)}, f32[1024,256]{1,0:T(8,128)S(1)}, u32[]{:S(2)}, u32[]{:S(2)}) %collective-permute-start) | collective-permute-done | bytes 1048608 | tf_op jit(solution)/shard_map/ppermute | solution.py:20
  104.1 0.0 copy-start.1
  104.1 1.0 copy-done.1
  105.1 1.8 gather_fusion.3
  107.0 2.2 %fusion.1 = f32[8,128,128]{2,1,0:T(8,128)S(1)} fusion(f32[8,128,256]{2,1,0:T(8,128)S(1)} %gather_fusion.3, f32[8,128,256]{2,1,0:T(8,128)S(1)} %gather_fusion.2, pred[8]{0:T(512)(128)(4,1)S(1)} %get-tuple-element.7, pred[8]{0:T(512)(128)(4,1)S(1)} %get-tuple-element.4, bf16[2,8,128,128]{3,2,1,0:T(8,128)(2,1)S(1)} %copy-done.3, ...), kind=kOutput, calls=%fused_computation.7 | convolution fusion | flops 403832832 | bytes 3145776 | tf_op jit(solution)/shard_map/mik,mjk->mij/dot_general | solution.py:34
  109.2 1.2 fusion.11
  110.4 1.2 fusion.2
  111.6 0.0 copy-start.2
  111.6 1.3 copy.13
  112.9 0.0 all-reduce.5.cloned.1.call-update
  112.9 44.4 %all-reduce.5.cloned.1.call-done = f32[1024,256]{1,0:T(8,128)} async-done(((f32[1024,256]{1,0:T(8,128)}), f32[1024,256]{1,0:T(8,128)}) %all-reduce.5.cloned.1.call-update) | async-done | bytes 1048592 | tf_op jit(solution)/shard_map/psum | solution.py:79
  157.3 0.0 copy-done.2
  157.3 2.8 %bitcast_add_fusion = f32[1024,256]{1,0:T(8,128)} fusion(f32[2,1024,256]{2,1,0:T(8,128)} %param.15, f32[1024,256]{1,0:T(8,128)S(1)} %copy-done.2, f32[1024,256]{1,0:T(8,128)} %all-reduce.5.cloned.1.call-done), kind=kLoop, calls=%fused_computation.10 | loop fusion | flops 1572864 | bytes 4194304 | tf_op jit(solution)/shard_map/add | solution.py:81
  160.1 2.4 %collective-permute-start.1 = (f32[1024,256]{1,0:T(8,128)}, f32[1024,256]{1,0:T(8,128)S(1)}, u32[]{:S(2)}, u32[]{:S(2)}) collective-permute-start(f32[1024,256]{1,0:T(8,128)} %bitcast_add_fusion), channel_id=1, source_target_pairs={{0,4},{4,8},{8,12},{12,16},{16,20},{20,24},{24,28},{28,32},{32,36}... | collective-permute-start | bytes 3145736 | tf_op jit(solution)/shard_map/ppermute | solution.py:20
  162.5 0.0 copy-start.5
  162.5 1.1 fusion.8
  163.6 1.2 convolution_multiply_fusion
  164.8 0.0 copy-done.5
  164.8 0.8 bitcast_add_fusion.2
  165.6 25.1 %collective-permute-done.1 = f32[1024,256]{1,0:T(8,128)S(1)} collective-permute-done((f32[1024,256]{1,0:T(8,128)}, f32[1024,256]{1,0:T(8,128)S(1)}, u32[]{:S(2)}, u32[]{:S(2)}) %collective-permute-start.1) | collective-permute-done | bytes 1048608 | tf_op jit(solution)/shard_map/ppermute | solution.py:20
  190.7 0.7 constant_dynamic-slice_fusion
  (9 shorter events, 0.1 us)
Async XLA Ops:
  7.2 63.2 %all-reduce.3.cloned.1.call-start = ((), (), s32[]{:S(2)}) async-start(), calls=%async_computation | async-start | bytes 2097152 | tf_op jit(solution)/shard_map/psum | solution.py:79
  10.0 3.5 %copy-start.3 = (bf16[2,8,128,128]{3,2,1,0:T(8,128)(2,1)S(1)}, bf16[2,8,128,128]{3,2,1,0:T(8,128)(2,1)}, u32[]{:S(2)}) copy-start(bf16[2,8,128,128]{3,2,1,0:T(8,128)(2,1)} %param.18) | copy-start | bytes 1572868
  19.4 137.9 %all-reduce.5.cloned.1.call-start = ((), (), s32[]{:S(2)}) async-start(), calls=%async_computation.1 | async-start | bytes 2097152 | tf_op jit(solution)/shard_map/psum | solution.py:79
  20.6 56.5 %copy-start = (f32[256,256]{1,0:T(8,128)S(1)}, f32[256,256]{1,0:T(8,128)}, u32[]{:S(2)}) copy-start(f32[256,256]{1,0:T(8,128)} %param.12) | copy-start | bytes 786436
  70.3 6.8 %copy-start.4 = (f32[2,256,256]{2,1,0:T(8,128)S(1)}, f32[2,256,256]{2,1,0:T(8,128)}, u32[]{:S(2)}) copy-start(f32[2,256,256]{2,1,0:T(8,128)} %param.14) | copy-start | bytes 1572868
  73.5 30.6 %collective-permute-start = (f32[1024,256]{1,0:T(8,128)}, f32[1024,256]{1,0:T(8,128)S(1)}, u32[]{:S(2)}, u32[]{:S(2)}) collective-permute-start(f32[1024,256]{1,0:T(8,128)} %bitcast_add_fusion.1), channel_id=1, source_target_pairs={{0,4},{4,8},{8,12},{12,16},{16,20},{20,24},{24,28},{28,32},{32,36}... | collective-permute-start | bytes 3145736 | tf_op jit(solution)/shard_map/ppermute | solution.py:20
  104.1 1.0 copy-start.1
  111.6 45.8 %copy-start.2 = (f32[1024,256]{1,0:T(8,128)S(1)}, f32[1024,256]{1,0:T(8,128)}, u32[]{:S(2)}) copy-start(f32[1024,256]{1,0:T(8,128)} %copy-done.1) | copy-start | bytes 3145732
  160.1 30.6 %collective-permute-start.1 = (f32[1024,256]{1,0:T(8,128)}, f32[1024,256]{1,0:T(8,128)S(1)}, u32[]{:S(2)}, u32[]{:S(2)}) collective-permute-start(f32[1024,256]{1,0:T(8,128)} %bitcast_add_fusion), channel_id=1, source_target_pairs={{0,4},{4,8},{8,12},{12,16},{16,20},{20,24},{24,28},{28,32},{32,36}... | collective-permute-start | bytes 3145736 | tf_op jit(solution)/shard_map/ppermute | solution.py:20
  162.5 2.3 %copy-start.5 = (f32[2,256,256]{2,1,0:T(8,128)S(1)}, f32[2,256,256]{2,1,0:T(8,128)}, u32[]{:S(2)}) copy-start(f32[2,256,256]{2,1,0:T(8,128)} %param.14) | copy-start | bytes 1572868
Sparse Core Ops, SparseCore 0:
  19.5 50.7 all-reduce.2
  113.0 44.2 all-reduce.4
where the time goes:
time: 199 us; the launch traced here: 198 us
  waiting for transfers between devices  145 us (73%)
  between operations  14.3 us (7%)
  matrix products  13.7 us (7%)
  local copies, waits for them, and re-layouts  11.6 us (6%)
  other arithmetic  8.85 us (4%)
  starting transfers between devices  4.89 us (2%)
    psum x2, waiting for transfers between devices, body(): summed = lax.psum(grad_items, 'grp')  94.2 us
    ppermute x2, waiting for transfers between devices, passed_along(): return lax.ppermute(value, axis, pairs)  50.8 us
    add x2, other arithmetic, body(): item_block + STEP_SIZE * (LIKELIHOOD * summed - item_block)  5.9 us
    ppermute x2, starting transfers between devices, passed_along(): return lax.ppermute(value, axis, pairs)  4.81 us
    dot_general x2, matrix products, slot_terms(): jnp.einsum('mik,mjk->mij', user_part, item_part, precision=HIGHEST)  4.38 us
  transfers between devices with their start and end apart: 4, of which 4 were waited for; matrix products, arithmetic and copies ran while one was open for 3% of the time, Pallas kernels for 0%

commit v1 on v0

v1 whole, which is shorter than its diff:
```python
import functools
import math

import jax
import jax.numpy as jnp
from jax import lax
from jax.experimental import pallas as pl
from jax.experimental.pallas import tpu as pltpu
from jax.sharding import PartitionSpec as P

STEP_SIZE = 0.001
LIKELIHOOD = 20.0
NOISE_SCALE = math.sqrt(0.002)
GAIN = STEP_SIZE * LIKELIHOOD
AXES = ("blk", "grp")
TILE = 128
CHUNKS = 2
VMEM_LIMIT = 16 * 1024 * 1024

NN = (((1,), (0,)), ((), ()))
NT = (((1,), (1,)), ((), ()))
TN = (((0,), (0,)), ((), ()))


def halves(value):
    high = value.astype(jnp.bfloat16)
    low = (value - high.astype(jnp.float32)).astype(jnp.bfloat16)
    return high, low


def product(left, right, dims):
    dot = functools.partial(
        lax.dot_general, dimension_numbers=dims, preferred_element_type=jnp.float32
    )
    return dot(left[0], right[0]) + (dot(left[0], right[1]) + dot(left[1], right[0]))


def spread(index_ref, count_ref, stratum, rating_ref, weight_ref, rating_out, weight_out):
    rating_out[...] = jnp.zeros_like(rating_out)
    weight_out[...] = jnp.zeros_like(weight_out)
    columns = rating_out.shape[0]
    for slot in range(rating_ref.shape[1]):

        @pl.when(slot < count_ref[stratum, 0])
        def _(slot=slot):
            tile = index_ref[stratum, slot]
            column = lax.rem(tile, columns)
            row = pl.multiple_of(lax.div(tile, columns) * TILE, TILE)
            rating_out[column, pl.ds(row, TILE), :] = rating_ref[0, slot]
            weight_out[column, pl.ds(row, TILE), :] = weight_ref[0, slot]


def tile_errors(user_halves, item_halves, rating, weight):
    predicted = product(user_halves, item_halves, NT)
    return halves(weight.astype(jnp.float32) * (rating.astype(jnp.float32) - predicted))


def item_rows(items_ref, column):
    return items_ref[pl.ds(pl.multiple_of(column * TILE, TILE), TILE), :]


def call(body, outs, operands, cost):
    specs = []
    for array, block, index in operands:
        if index is None:
            specs.append(pl.BlockSpec(memory_space=pltpu.SMEM))
        else:
            specs.append(pl.BlockSpec(block, functools.partial(lambda step, at: at, at=index)))
    out_specs = [
        pl.BlockSpec(shape, functools.partial(lambda step, n: (0,) * n, n=len(shape)))
        for shape, _ in outs
    ]
    return pl.pallas_call(
        body,
        grid=(1,),
        in_specs=specs,
        out_specs=out_specs,
        out_shape=[jax.ShapeDtypeStruct(shape, dtype) for shape, dtype in outs],
        compiler_params=pltpu.CompilerParams(vmem_limit_bytes=VMEM_LIMIT),
        cost_estimate=pl.CostEstimate(flops=cost, bytes_accessed=1 << 20, transcendentals=0),
    )(*[array for array, _, _ in operands])


def whole(array):
    return (array, array.shape, (0,) * array.ndim)


def scalars(array):
    return (array, None, None)


def of_stratum(array, stratum):
    return (array, (1,) + array.shape[1:], (stratum,) + (0,) * (array.ndim - 1))


def body(users, items, noise_users, noise_items, tile_index, counts, ratings, weights):
    f32, bf16 = jnp.float32, jnp.bfloat16
    n_blk, n_grp = lax.axis_size("blk"), lax.axis_size("grp")
    owned, rank = users.shape
    columns = items.shape[0] // TILE
    per_quarter = columns // n_grp
    quarter = per_quarter * TILE
    per_chunk = per_quarter // CHUNKS
    chunk = per_chunk * TILE
    member = lax.axis_index("grp")
    place = member.astype(jnp.int32).reshape(1)

    def swap(value, other):
        pairs = [
            (b * n_grp + g, b * n_grp + (g ^ other)) for b in range(n_blk) for g in range(n_grp)
        ]
        return lax.ppermute(value, AXES, pairs)

    def onward(value):
        pairs = [
            (b * n_grp + g, (b + 1) % n_blk * n_grp + (g ^ 2))
            for b in range(n_blk)
            for g in range(n_grp)
        ]
        return lax.ppermute(value, AXES, pairs)

    dense = (columns, owned, TILE)
    piece = (chunk, rank)

    def piece_grads(user_halves, items_ref, rating_ref, weight_ref, start, outs, user_total):
        for k in range(CHUNKS):
            for t in range(per_chunk):
                column = start + k * per_chunk + t
                item_halves = halves(item_rows(items_ref, column))
                errors = tile_errors(user_halves, item_halves, rating_ref[column], weight_ref[column])
                if outs is not None:
                    outs[k][t * TILE : (t + 1) * TILE, :] = product(errors, user_halves, TN)
                if user_total is not None:
                    user_total = user_total + product(errors, item_halves, NN)
        return user_total

    def first(place_ref, index_ref, count_ref, rating_ref, weight_ref, users_ref, items_ref,
              rating_out, weight_out, *outs):
        spread(index_ref, count_ref, 0, rating_ref, weight_ref, rating_out, weight_out)
        start = (place_ref[0] ^ 1) * per_quarter
        piece_grads(halves(users_ref[...]), items_ref, rating_out, weight_out, start, outs, None)

    unit = 2 * owned * quarter * rank * 3
    rating_0, weight_0, *to_sibling = call(
        first,
        [(dense, bf16)] * 2 + [(piece, f32)] * CHUNKS,
        [scalars(place), scalars(tile_index), scalars(counts), of_stratum(ratings, 0),
         of_stratum(weights, 0), whole(users), whole(items)],
        2 * unit,
    )
    from_sibling = [swap(value, 1) for value in to_sibling]

    def second(place_ref, rating_ref, weight_ref, users_ref, items_ref, *outs):
        start = place_ref[0] * per_quarter
        piece_grads(halves(users_ref[...]), items_ref, rating_ref, weight_ref, start, outs, None)

    mine = call(
        second,
        [(piece, f32)] * CHUNKS,
        [scalars(place), whole(rating_0), whole(weight_0), whole(users), whole(items)],
        2 * unit,
    )
    from_chip = [swap(a + b, 2) for a, b in zip(mine, from_sibling)]

    def third(place_ref, rating_ref, weight_ref, users_ref, items_ref, noise_ref, users_out, *outs):
        user_halves = halves(users_ref[...])
        total = jnp.zeros((owned, rank), f32)
        for flip, target in ((3, outs[:CHUNKS]), (2, outs[CHUNKS:]), (0, None), (1, None)):
            start = (place_ref[0] ^ flip) * per_quarter
            total = piece_grads(
                user_halves, items_ref, rating_ref, weight_ref, start, target, total
            )
        now = users_ref[...]
        users_out[...] = now + STEP_SIZE * (LIKELIHOOD * total - now) + NOISE_SCALE * noise_ref[0]

    users_1, *pieces = call(
        third,
        [(users.shape, f32)] + [(piece, f32)] * (2 * CHUNKS),
        [scalars(place), whole(rating_0), whole(weight_0), whole(users), whole(items),
         of_stratum(noise_users, 0)],
        10 * unit,
    )
    kept = pieces[CHUNKS:]
    from_sibling = [swap(value, 1) for value in pieces[:CHUNKS]]

    def row_chunk(array, flip, k):
        return lax.dynamic_slice_in_dim(array, (member ^ flip) * quarter + k * chunk, chunk, 0)

    def noise_chunk(stratum, flip, k):
        at = (stratum, (member ^ flip) * quarter + k * chunk, 0)
        return lax.dynamic_slice(noise_items, at, (1, chunk, rank))[0]

    ahead = []
    for k in range(CHUNKS):
        rows = row_chunk(items, 2, k)
        base = rows - STEP_SIZE * rows + NOISE_SCALE * noise_chunk(0, 2, k)
        base = lax.optimization_barrier(base + GAIN * (kept[k] + from_sibling[k]))
        ahead.append(onward(base + GAIN * from_chip[k]))

    half = (columns // 2, owned, TILE)

    def layout(place_ref, index_ref, count_ref, rating_ref, weight_ref,
               rating_out, weight_out, rating_send, weight_send):
        spread(index_ref, count_ref, 1, rating_ref, weight_ref, rating_out, weight_out)
        for n, flip in enumerate((1, 3)):
            for t in range(per_quarter):
                column = (place_ref[0] ^ flip) * per_quarter + t
                rating_send[n * per_quarter + t] = rating_out[column].astype(f32)
                weight_send[n * per_quarter + t] = weight_out[column].astype(f32)

    rating_1, weight_1, rating_send, weight_send = call(
        layout,
        [(dense, bf16)] * 2 + [(half, f32)] * 2,
        [scalars(place), scalars(tile_index), scalars(counts), of_stratum(ratings, 1),
         of_stratum(weights, 1)],
        unit,
    )
    rating_s, weight_s, users_s = swap(rating_send, 1), swap(weight_send, 1), swap(users_1, 1)

    def late(k, slot, place_ref, items_ref, users_ref, users_s_ref, rating_ref, weight_ref,
             rating_s_ref, weight_s_ref, *rest):
        own, other = halves(users_ref[...]), halves(users_s_ref[...])
        out = rest[-1]
        for t in range(per_chunk):
            offset = k * per_chunk + t
            column = (place_ref[0] ^ (2 * slot)) * per_quarter + offset
            rows = slice(t * TILE, (t + 1) * TILE)
            now = items_ref[rows, :]
            item_halves = halves(now)
            errors = tile_errors(own, item_halves, rating_ref[column], weight_ref[column])
            total = product(errors, own, TN)
            at = slot * per_quarter + offset
            errors = tile_errors(other, item_halves, rating_s_ref[at], weight_s_ref[at])
            total = total + product(errors, other, TN)
            if slot == 1:
                total = now + STEP_SIZE * (LIKELIHOOD * total - now) + NOISE_SCALE * rest[0][rows, :]
            out[rows, :] = total

    near, far, near_s, far_s, final = [], [], [], [], []
    for k in range(CHUNKS):
        common = [whole(users_1), whole(users_s), whole(rating_1), whole(weight_1),
                  whole(rating_s), whole(weight_s)]
        here = ahead[k]
        there = swap(here, 2)
        [send] = call(
            functools.partial(late, k, 0), [(piece, f32)],
            [scalars(place), whole(here)] + common, 4 * unit // CHUNKS,
        )
        received = swap(send, 2)
        noise = lax.optimization_barrier(noise_chunk(1, 2, k))
        [base] = call(
            functools.partial(late, k, 1), [(piece, f32)],
            [scalars(place), whole(there)] + common + [whole(noise)], 4 * unit // CHUNKS,
        )
        final.append(onward(base + GAIN * received))
        near.append(here)
        far.append(there)
        near_s.append(swap(here, 1))
        far_s.append(swap(there, 1))

    def last(place_ref, rating_ref, weight_ref, users_ref, noise_ref, *rest):
        blocks, users_out = rest[:-1], rest[-1]
        user_halves = halves(users_ref[...])
        total = jnp.zeros((owned, rank), f32)
        for n, flip in enumerate((0, 1, 2, 3)):
            for k in range(CHUNKS):
                for t in range(per_chunk):
                    column = (place_ref[0] ^ flip) * per_quarter + k * per_chunk + t
                    item_halves = halves(blocks[n * CHUNKS + k][t * TILE : (t + 1) * TILE, :])
                    errors = tile_errors(user_halves, item_halves, rating_ref[column], weight_ref[column])
                    total = total + product(errors, item_halves, NN)
        now = users_ref[...]
        users_out[...] = now + STEP_SIZE * (LIKELIHOOD * total - now) + NOISE_SCALE * noise_ref[0]

    [users_out] = call(
        last,
        [(users.shape, f32)],
        [scalars(place), whole(rating_1), whole(weight_1), whole(users_1), of_stratum(noise_users, 1)]
        + [whole(v) for v in near + near_s + far + far_s],
        8 * unit,
    )
    return (users_out, jnp.concatenate(final, 0))


def solution(mesh):
    in_specs = (
        P(("blk", "grp"), None),
        P("blk", None),
        P(None, ("blk", "grp"), None),
        P(None, "blk", None),
        P(None, ("blk", "grp")),
        P(None, ("blk", "grp")),
        P(None, ("blk", "grp"), None, None),
        P(None, ("blk", "grp"), None, None),
    )
    out_specs = (P(("blk", "grp"), None), P(("blk", "grp"), None))
    return jax.shard_map(body, mesh=mesh, in_specs=in_specs, out_specs=out_specs, check_vma=False)
```

time: 199 us -> 66.7 us (0.34)
  waiting for transfers between devices: 145 us -> 23.8 us
  Pallas kernels: 0 us -> 14.6 us
  matrix products: 13.7 us -> 0 us
  between operations: 14.3 us -> 0.88 us
  starting transfers between devices: 4.89 us -> 13.3 us
  other arithmetic: 8.85 us -> 2.92 us
    psum x2 -> x0, waiting for transfers between devices: 94.2 us -> none  [body(): summed = lax.psum(grad_items, 'grp')]
    ppermute x2 -> x21, waiting for transfers between devices: 50.8 us -> 23.8 us  [the longest x4 18.4 us: onward(): return lax.ppermute(value, AXES, pairs)]
    pallas_call x0 -> x9, Pallas kernels: none -> 14.6 us  [call(): pl.pallas_call(body, grid=(1,), in_specs=specs, out_specs=out_specs, out_...]
    dot_general x10 -> x0, matrix products: 13.7 us -> none  [the longest x2 4.38 us: slot_terms(): jnp.einsum('mik,mjk->mij', user_part, item_part, precision=HIGHEST)]
    ppermute x2 -> x21, starting transfers between devices: 4.81 us -> 13.3 us  [the longest x17 11.5 us: swap(): return lax.ppermute(value, AXES, pairs)]
    unnamed x12 -> x41, local copies, waits for them, and re-layouts: 1.03 us -> 9.25 us
    gather x4 -> x0, local copies, waits for them, and re-layouts: 5.91 us -> none  [the longest x2 3.68 us: slot_terms(): item_part = jnp.take(item_table, tile_col, axis=0)]
    add x4 -> x7, other arithmetic: 6.73 us -> 2.2 us  [the longest x1 1.18 us: body(): base = lax.optimization_barrier(base + GAIN * (kept[k] + from_sibling[k]))]
  transfers between devices with their start and end apart: 4 -> 21, of which waited for: 4 -> 8; matrix products, arithmetic and copies ran while one was open for 3% -> 5% of each run, Pallas kernels for 0% -> 19%
where the time goes in v1:
time: 66.7 us; the launch traced here: 65.7 us
  waiting for transfers between devices  23.8 us (36%)
  Pallas kernels  14.6 us (22%)
  starting transfers between devices  13.3 us (20%)
  local copies, waits for them, and re-layouts  10.2 us (15%)
  other arithmetic  2.92 us (4%)
  between operations  0.88 us (1%)
    ppermute x4, waiting for transfers between devices, onward(): return lax.ppermute(value, AXES, pairs)  18.4 us
    pallas_call x9, Pallas kernels, call(): pl.pallas_call(body, grid=(1,), in_specs=specs, out_specs=out_specs, out_...  14.6 us
    ppermute x17, starting transfers between devices, swap(): return lax.ppermute(value, AXES, pairs)  11.5 us
    unnamed x41, local copies, waits for them, and re-layouts  9.25 us
    ppermute x17, waiting for transfers between devices, swap(): return lax.ppermute(value, AXES, pairs)  5.44 us
    ppermute x4, starting transfers between devices, onward(): return lax.ppermute(value, AXES, pairs)  1.72 us
  transfers between devices with their start and end apart: 21, of which 8 were waited for; matrix products, arithmetic and copies ran while one was open for 5% of the time, Pallas kernels for 19%

profile of v1, /device:TPU:1, one launch (start us, length us, event | category | flops | bytes accessed | tf_op | source)
XLA Modules:
  0.0 65.7 jit_solution(16578840160137749321)
XLA Ops:
  0.6 0.7 %copy.10.count_ref = s32[2,1]{1,0:T(2,128)S(1)} copy(s32[2,1]{0,1:T(1,128)} %param.13) | data formatting | bytes 16 | tf_op args[5]
  1.4 1.2 %copy-done = f32[1024,256]{1,0:T(8,128)S(1)} copy-done((f32[1024,256]{1,0:T(8,128)S(1)}, f32[1024,256]{1,0:T(8,128)}, u32[]{:S(2)}) %copy-start) | copy-done | bytes 1048600
  2.6 1.0 %copy-done.2 = bf16[2,8,128,128]{3,2,1,0:T(8,128)(2,1)S(1)} copy-done((bf16[2,8,128,128]{3,2,1,0:T(8,128)(2,1)S(1)}, bf16[2,8,128,128]{3,2,1,0:T(8,128)(2,1)}, u32[]{:S(2)}) %copy-start.2) | copy-done | bytes 524312
  3.6 1.0 %copy-done.4 = bf16[2,8,128,128]{3,2,1,0:T(8,128)(2,1)S(1)} copy-done((bf16[2,8,128,128]{3,2,1,0:T(8,128)(2,1)S(1)}, bf16[2,8,128,128]{3,2,1,0:T(8,128)(2,1)}, u32[]{:S(2)}) %copy-start.4) | copy-done | bytes 524312
  4.7 0.9 %copy-done.5 = f32[256,256]{1,0:T(8,128)S(1)} copy-done((f32[256,256]{1,0:T(8,128)S(1)}, f32[256,256]{1,0:T(8,128)}, u32[]{:S(2)}) %copy-start.5) | copy-done | bytes 262168
  5.6 0.7 %copy-done.15 = s32[2,8]{1,0:T(2,128)S(1)} copy-done((s32[2,8]{1,0:T(2,128)S(1)}, s32[2,8]{1,0:T(2,128)}, u32[]{:S(2)}) %copy-start.15) | copy-done | bytes 88
  6.3 2.1 %shard_map.96 = (bf16[8,256,128]{2,1,0:T(8,128)(2,1)S(1)}, bf16[8,256,128]{2,1,0:T(8,128)(2,1)S(1)}, f32[128,256]{1,0:T(8,128)}, f32[128,256]{1,0:T(8,128)S(1)}) custom-call(s32[1]{0:T(128)} %bitcast.place_ref, s32[2,8]{1,0:T(2,128)S(1)} %copy-done.15, s32[2,1]{1,0:T(2,128)S(1)} %copy.10.count_ref, bf16[2,8,128,128]{3,2,1,0:T(8,128)(2,1)S(1)} %copy-done.2, ...), custom_call_target="tpu_custom_call" | custom-call | flops 201326592 | bytes 1048576 | tf_op jit(solution)/shard_map/pallas_call | solution.py:73
  8.4 3.3 %collective-permute-start.1 = (f32[128,256]{1,0:T(8,128)}, f32[128,256]{1,0:T(8,128)}, u32[]{:S(2)}, u32[]{:S(2)}) collective-permute-start(f32[128,256]{1,0:T(8,128)} %get-tuple-element.25), channel_id=1, source_target_pairs={{0,1},{1,0},{2,3},{3,2},{4,5},{5,4},{6,7},{7,6},{8,9},{9,8},{10,11... | collective-permute-start | bytes 393224 | tf_op jit(solution)/shard_map/ppermute | solution.py:112
  11.7 3.0 %shard_map.97 = (f32[256,256]{1,0:T(8,128)S(1)}, f32[128,256]{1,0:T(8,128)}, f32[128,256]{1,0:T(8,128)}, f32[128,256]{1,0:T(8,128)S(1)}, f32[128,256]{1,0:T(8,128)S(1)}) custom-call(s32[1]{0:T(128)} %bitcast.place_ref, bf16[8,256,128]{2,1,0:T(8,128)(2,1)S(1)} %get-tuple-element.19.rating_ref, bf16[8,256,128]{2,1,0:T(8,128)(2,1)S(1)} %get-tuple-element.20.weight_ref, ...), custom_call_target="tpu_custom_call" | custom-call | flops 1006632960 | bytes 1048576 | tf_op jit(solution)/shard_map/pallas_call | solution.py:73
  14.8 0.7 %copy-done.13 = f32[128,256]{1,0:T(8,128)} copy-done((f32[128,256]{1,0:T(8,128)}, f32[128,256]{1,0:T(8,128)S(1)}, u32[]{:S(2)}) %copy-start.13) | copy-done | bytes 131096
  15.4 0.0 collective-permute-start
  15.5 0.5 collective-permute-start.4
  15.9 0.0 collective-permute-start.14
  16.0 1.7 %shard_map.95 = (bf16[8,256,128]{2,1,0:T(8,128)(2,1)S(1)}, bf16[8,256,128]{2,1,0:T(8,128)(2,1)S(1)}, f32[4,256,128]{2,1,0:T(8,128)}, f32[4,256,128]{2,1,0:T(8,128)S(1)}) custom-call(s32[1]{0:T(128)} %bitcast.place_ref, s32[2,8]{1,0:T(2,128)S(1)} %copy-done.15, s32[2,1]{1,0:T(2,128)S(1)} %copy.10.count_ref, bf16[2,8,128,128]{3,2,1,0:T(8,128)(2,1)S(1)} %copy-done.3, ...), custom_call_target="tpu_custom_call" | custom-call | flops 100663296 | bytes 1048576 | tf_op jit(solution)/shard_map/pallas_call | solution.py:73
  17.7 0.8 %copy-done.16 = f32[4,256,128]{2,1,0:T(8,128)} copy-done((f32[4,256,128]{2,1,0:T(8,128)}, f32[4,256,128]{2,1,0:T(8,128)S(1)}, u32[]{:S(2)}) %copy-start.16) | copy-done | bytes 524312
  18.5 0.5 collective-permute-start.15
  18.9 1.0 %copy-done.8 = bf16[8,256,128]{2,1,0:T(8,128)(2,1)S(1)} copy-done((bf16[8,256,128]{2,1,0:T(8,128)(2,1)S(1)}, bf16[8,256,128]{2,1,0:T(8,128)(2,1)}, u32[]{:S(2)}) %copy-start.8) | copy-done | bytes 524312
  20.0 1.0 %copy-done.10 = bf16[8,256,128]{2,1,0:T(8,128)(2,1)S(1)} copy-done((bf16[8,256,128]{2,1,0:T(8,128)(2,1)S(1)}, bf16[8,256,128]{2,1,0:T(8,128)(2,1)}, u32[]{:S(2)}) %copy-start.10) | copy-done | bytes 524312
  21.0 1.1 %shard_map.98 = (f32[128,256]{1,0:T(8,128)S(1)}, f32[128,256]{1,0:T(8,128)S(1)}) custom-call(s32[1]{0:T(128)} %bitcast.place_ref, bf16[8,256,128]{2,1,0:T(8,128)(2,1)S(1)} %copy-done.8, bf16[8,256,128]{2,1,0:T(8,128)(2,1)S(1)} %copy-done.10, f32[256,256]{1,0:T(8,128)S(1)} %copy-done.6, f32[1024,256]{1,0:T(8,128)S(1)} %copy-done.1), custom_call_target="tpu_custom_call" | custom-call | flops 201326592 | bytes 1048576 | tf_op jit(solution)/shard_map/pallas_call | solution.py:73
  22.1 0.1 collective-permute-start.16
  22.2 0.9 %add.57 = f32[128,256]{1,0:T(8,128)S(1)} add(f32[128,256]{1,0:T(8,128)S(1)} %get-tuple-element.24, f32[128,256]{1,0:T(8,128)} %collective-permute-done.1) | non-fusion elementwise | flops 32768 | bytes 393216 | tf_op jit(solution)/shard_map/add | solution.py:163
  23.2 0.5 collective-permute-start.5
  23.8 1.2 %fusion.3 = (f32[128,256]{1,0:T(8,128)S(1)}, f32[128,256]{1,0:T(8,128)S(1)}) fusion(f32[128,256]{1,0:T(8,128)S(1)} %copy-done.14, f32[128,256]{1,0:T(8,128)} %collective-permute-done.4, f32[2,1024,256]{2,1,0:T(8,128)} %param.11, s32[]{:T(128)S(6)} %select_n.5, f32[1024,256]{1,0:T(8,128)S(1)} %copy-done.1, f32[128,256]{1,0:T(8,128)S(1)} %get-tuple-element.22, ...), kind=kLoop, calls=%fused_computation.6 | loop fusion | flops 458752 | bytes 1310728 | tf_op jit(solution)/shard_map/add | solution.py:197
  25.0 1.6 %collective-permute-start.6 = (f32[128,256]{1,0:T(8,128)S(1)}, f32[128,256]{1,0:T(8,128)S(1)}, u32[]{:S(2)}, u32[]{:S(2)}) collective-permute-start(f32[128,256]{1,0:T(8,128)S(1)} %add.64), channel_id=1, source_target_pairs={{0,2},{1,3},{2,0},{3,1},{4,6},{5,7},{6,4},{7,5},{8,10},{9,11},{10,... | collective-permute-start | bytes 393224 | tf_op jit(solution)/shard_map/ppermute | solution.py:112
  26.5 2.3 %collective-permute-done.2 = f32[128,256]{1,0:T(8,128)S(1)} collective-permute-done((f32[128,256]{1,0:T(8,128)S(1)}, f32[128,256]{1,0:T(8,128)S(1)}, u32[]{:S(2)}, u32[]{:S(2)}) %collective-permute-start.2) | collective-permute-done | bytes 131104 | tf_op jit(solution)/shard_map/ppermute | solution.py:112
  28.8 0.8 %collective-permute-start.3 = (f32[128,256]{1,0:T(8,128)S(1)}, f32[128,256]{1,0:T(8,128)S(1)}, u32[]{:S(2)}, u32[]{:S(2)}) collective-permute-start(f32[128,256]{1,0:T(8,128)S(1)} %multiply_add_fusion.3), channel_id=1, source_target_pairs={{0,6},{1,7},{2,4},{3,5},{4,10},{5,11},{6,8},{7,9},{8,14},{9,15},{1... | collective-permute-start | bytes 393224 | tf_op jit(solution)/shard_map/ppermute | solution.py:120
  29.6 2.0 %collective-permute-done.6 = f32[128,256]{1,0:T(8,128)S(1)} collective-permute-done((f32[128,256]{1,0:T(8,128)S(1)}, f32[128,256]{1,0:T(8,128)S(1)}, u32[]{:S(2)}, u32[]{:S(2)}) %collective-permute-start.6) | collective-permute-done | bytes 131104 | tf_op jit(solution)/shard_map/ppermute | solution.py:112
  31.6 0.8 %collective-permute-start.7 = (f32[128,256]{1,0:T(8,128)S(1)}, f32[128,256]{1,0:T(8,128)S(1)}, u32[]{:S(2)}, u32[]{:S(2)}) collective-permute-start(f32[128,256]{1,0:T(8,128)S(1)} %multiply_add_fusion.2), channel_id=1, source_target_pairs={{0,6},{1,7},{2,4},{3,5},{4,10},{5,11},{6,8},{7,9},{8,14},{9,15},{1... | collective-permute-start | bytes 393224 | tf_op jit(solution)/shard_map/ppermute | solution.py:120
  32.5 7.3 %collective-permute-done.3.rest_0_.items_ref = f32[128,256]{1,0:T(8,128)S(1)} collective-permute-done((f32[128,256]{1,0:T(8,128)S(1)}, f32[128,256]{1,0:T(8,128)S(1)}, u32[]{:S(2)}, u32[]{:S(2)}) %collective-permute-start.3) | collective-permute-done | bytes 131104 | tf_op jit(solution)/shard_map/ppermute | solution.py:120
  39.8 3.7 %collective-permute-done.7.rest_1_.items_ref = f32[128,256]{1,0:T(8,128)S(1)} collective-permute-done((f32[128,256]{1,0:T(8,128)S(1)}, f32[128,256]{1,0:T(8,128)S(1)}, u32[]{:S(2)}, u32[]{:S(2)}) %collective-permute-start.7) | collective-permute-done | bytes 131104 | tf_op jit(solution)/shard_map/ppermute | solution.py:120
  43.5 1.0 %shard_map.101 = f32[128,256]{1,0:T(8,128)S(1)} custom-call(s32[1]{0:T(128)} %bitcast.place_ref, f32[128,256]{1,0:T(8,128)S(1)} %collective-permute-done.3.rest_0_.items_ref, f32[256,256]{1,0:T(8,128)S(1)} %get-tuple-element.21.users_ref, f32[256,256]{1,0:T(8,128)S(1)} %collective-permute-done.14.users_s_ref, ...), custom_call_target="tpu_custom_call" | custom-call | flops 201326592 | bytes 1048576 | tf_op jit(solution)/shard_map/pallas_call | solution.py:73
  44.5 1.5 %collective-permute-start.17 = (f32[128,256]{1,0:T(8,128)S(1)}, f32[128,256]{1,0:T(8,128)S(1)}, u32[]{:S(2)}, u32[]{:S(2)}) collective-permute-start(f32[128,256]{1,0:T(8,128)S(1)} %shard_map.101), channel_id=1, source_target_pairs={{0,2},{1,3},{2,0},{3,1},{4,6},{5,7},{6,4},{7,5},{8,10},{9,11},{10,... | collective-permute-start | bytes 393224 | tf_op jit(solution)/shard_map/ppermute | solution.py:112
  46.0 1.0 %dynamic-slice_bitcast_fusion.1 = (f32[128,256]{1,0:T(8,128)S(1)}, f32[128,256]{1,0:T(8,128)S(1)}) fusion(f32[2,1024,256]{2,1,0:T(8,128)} %param.11, s32[]{:T(128)S(6)} %select_n.4, s32[]{:T(128)S(6)} %select_n.5), kind=kLoop, calls=%fused_computation.10 | loop fusion | bytes 524296 | tf_op jit(solution)/shard_map/squeeze | solution.py:191
  47.0 2.0 %collective-permute-start.9 = (f32[128,256]{1,0:T(8,128)S(1)}, f32[128,256]{1,0:T(8,128)S(1)}, u32[]{:S(2)}, u32[]{:S(2)}) collective-permute-start(f32[128,256]{1,0:T(8,128)S(1)} %collective-permute-done.7.rest_1_.items_ref), channel_id=1, source_target_pairs={{0,1},{1,0},{2,3},{3,2},{4,5},{5,4},{6,7},{7,6},{8,9},{9,8},{10,11... | collective-permute-start | bytes 393224 | tf_op jit(solution)/shard_map/ppermute | solution.py:112
  49.0 0.1 collective-permute-start.8
  49.1 1.0 %shard_map.103 = f32[128,256]{1,0:T(8,128)S(1)} custom-call(s32[1]{0:T(128)} %bitcast.place_ref, f32[128,256]{1,0:T(8,128)S(1)} %collective-permute-done.7.rest_1_.items_ref, f32[256,256]{1,0:T(8,128)S(1)} %get-tuple-element.21.users_ref, f32[256,256]{1,0:T(8,128)S(1)} %collective-permute-done.14.users_s_ref, ...), custom_call_target="tpu_custom_call" | custom-call | flops 201326592 | bytes 1048576 | tf_op jit(solution)/shard_map/pallas_call | solution.py:73
  50.1 0.1 collective-permute-start.19
  50.2 1.0 %shard_map.102 = f32[128,256]{1,0:T(8,128)S(1)} custom-call(s32[1]{0:T(128)} %bitcast.place_ref, f32[128,256]{1,0:T(8,128)S(1)} %collective-permute-done.11.rest_5_.items_ref, f32[256,256]{1,0:T(8,128)S(1)} %get-tuple-element.21.users_ref, f32[256,256]{1,0:T(8,128)S(1)} %collective-permute-done.14.users_s_ref, ...), custom_call_target="tpu_custom_call" | custom-call | flops 201326592 | bytes 1048576 | tf_op jit(solution)/shard_map/pallas_call | solution.py:73
  51.2 1.1 %collective-permute-start.13 = (f32[128,256]{1,0:T(8,128)S(1)}, f32[128,256]{1,0:T(8,128)S(1)}, u32[]{:S(2)}, u32[]{:S(2)}) collective-permute-start(f32[128,256]{1,0:T(8,128)S(1)} %collective-permute-done.11.rest_5_.items_ref), channel_id=1, source_target_pairs={{0,1},{1,0},{2,3},{3,2},{4,5},{5,4},{6,7},{7,6},{8,9},{9,8},{10,11... | collective-permute-start | bytes 393224 | tf_op jit(solution)/shard_map/ppermute | solution.py:112
  52.3 1.0 %shard_map.100 = f32[128,256]{1,0:T(8,128)S(1)} custom-call(s32[1]{0:T(128)} %bitcast.place_ref, f32[128,256]{1,0:T(8,128)S(1)} %collective-permute-done.10.rest_4_.items_ref, f32[256,256]{1,0:T(8,128)S(1)} %get-tuple-element.21.users_ref, f32[256,256]{1,0:T(8,128)S(1)} %collective-permute-done.14.users_s_ref, ...), custom_call_target="tpu_custom_call" | custom-call | flops 201326592 | bytes 1048576 | tf_op jit(solution)/shard_map/pallas_call | solution.py:73
  53.4 0.1 collective-permute-start.12
  53.5 0.5 collective-permute-done.19
  54.0 0.1 collective-permute-start.20
  54.1 0.6 collective-permute-done.12.rest_6_
  54.8 2.9 %shard_map.99 = f32[256,256]{1,0:T(8,128)} custom-call(s32[1]{0:T(128)} %bitcast.place_ref, bf16[8,256,128]{2,1,0:T(8,128)(2,1)S(1)} %get-tuple-element.17.rating_ref, bf16[8,256,128]{2,1,0:T(8,128)(2,1)S(1)} %get-tuple-element.18.weight_ref, f32[256,256]{1,0:T(8,128)S(1)} %get-tuple-element.21.users_ref, f32[2,256,256]{2,1,0:T(8,128)S(1)} %copy-done.12, ...), custom_call_target="tpu_custom_call" | custom-call | flops 805306368 | bytes 1048576 | tf_op jit(solution)/shard_map/pallas_call | solution.py:73
  57.6 5.6 %collective-permute-done.18 = f32[128,256]{1,0:T(8,128)S(1)} collective-permute-done((f32[128,256]{1,0:T(8,128)S(1)}, f32[128,256]{1,0:T(8,128)S(1)}, u32[]{:S(2)}, u32[]{:S(2)}) %collective-permute-start.18) | collective-permute-done | bytes 131104 | tf_op jit(solution)/shard_map/ppermute | solution.py:120
  63.2 1.8 %collective-permute-done.20 = f32[128,256]{1,0:T(8,128)S(1)} collective-permute-done((f32[128,256]{1,0:T(8,128)S(1)}, f32[128,256]{1,0:T(8,128)S(1)}, u32[]{:S(2)}, u32[]{:S(2)}) %collective-permute-start.20) | collective-permute-done | bytes 131104 | tf_op jit(solution)/shard_map/ppermute | solution.py:120
  65.0 0.7 %pad_maximum_fusion = f32[256,256]{1,0:T(8,128)} fusion(f32[128,256]{1,0:T(8,128)S(1)} %collective-permute-done.20, f32[128,256]{1,0:T(8,128)S(1)} %collective-permute-done.18), kind=kLoop, calls=%fused_computation | loop fusion | flops 65536 | bytes 524288 | tf_op jit(solution)/shard_map/concatenate | solution.py:282
  (53 shorter events, 0.2 us)
Async XLA Ops:
  1.4 1.2 %copy-start = (f32[1024,256]{1,0:T(8,128)S(1)}, f32[1024,256]{1,0:T(8,128)}, u32[]{:S(2)}) copy-start(f32[1024,256]{1,0:T(8,128)} %items_ref.5) | copy-start | bytes 3145732
  2.6 1.0 %copy-start.2 = (bf16[2,8,128,128]{3,2,1,0:T(8,128)(2,1)S(1)}, bf16[2,8,128,128]{3,2,1,0:T(8,128)(2,1)}, u32[]{:S(2)}) copy-start(bf16[2,8,128,128]{3,2,1,0:T(8,128)(2,1)} %rating_ref.3) | copy-start | bytes 1572868
  3.6 1.0 %copy-start.4 = (bf16[2,8,128,128]{3,2,1,0:T(8,128)(2,1)S(1)}, bf16[2,8,128,128]{3,2,1,0:T(8,128)(2,1)}, u32[]{:S(2)}) copy-start(bf16[2,8,128,128]{3,2,1,0:T(8,128)(2,1)} %weight_ref.3) | copy-start | bytes 1572868
  4.7 0.9 %copy-start.5 = (f32[256,256]{1,0:T(8,128)S(1)}, f32[256,256]{1,0:T(8,128)}, u32[]{:S(2)}) copy-start(f32[256,256]{1,0:T(8,128)} %users_ref.5) | copy-start | bytes 786436
  5.6 0.7 %copy-start.15 = (s32[2,8]{1,0:T(2,128)S(1)}, s32[2,8]{1,0:T(2,128)}, u32[]{:S(2)}) copy-start(s32[2,8]{1,0:T(2,128)} %index_ref.3) | copy-start | bytes 196
  6.3 5.4 %copy-start.1 = (f32[1024,256]{1,0:T(8,128)S(1)}, f32[1024,256]{1,0:T(8,128)}, u32[]{:S(2)}) copy-start(f32[1024,256]{1,0:T(8,128)} %items_ref.5) | copy-start | bytes 3145732
  6.3 5.4 %copy-start.6 = (f32[256,256]{1,0:T(8,128)S(1)}, f32[256,256]{1,0:T(8,128)}, u32[]{:S(2)}) copy-start(f32[256,256]{1,0:T(8,128)} %users_ref.5) | copy-start | bytes 786436
  6.3 5.4 %copy-start.11 = (f32[2,256,256]{2,1,0:T(8,128)S(1)}, f32[2,256,256]{2,1,0:T(8,128)}, u32[]{:S(2)}) copy-start(f32[2,256,256]{2,1,0:T(8,128)} %noise_ref.3) | copy-start | bytes 1572868
  8.4 9.3 %copy-start.7 = (bf16[8,256,128]{2,1,0:T(8,128)(2,1)}, bf16[8,256,128]{2,1,0:T(8,128)(2,1)S(1)}, u32[]{:S(2)}) copy-start(bf16[8,256,128]{2,1,0:T(8,128)(2,1)S(1)} %get-tuple-element.19.rating_ref) | copy-start | bytes 1572868
  8.4 9.3 %copy-start.9 = (bf16[8,256,128]{2,1,0:T(8,128)(2,1)}, bf16[8,256,128]{2,1,0:T(8,128)(2,1)S(1)}, u32[]{:S(2)}) copy-start(bf16[8,256,128]{2,1,0:T(8,128)(2,1)S(1)} %get-tuple-element.20.weight_ref) | copy-start | bytes 1572868
  8.4 9.3 %copy-start.18 = (f32[128,256]{1,0:T(8,128)}, f32[128,256]{1,0:T(8,128)S(1)}, u32[]{:S(2)}) copy-start(f32[128,256]{1,0:T(8,128)S(1)} %get-tuple-element.29) | copy-start | bytes 393220
  8.4 7.6 %copy-start.3 = (bf16[2,8,128,128]{3,2,1,0:T(8,128)(2,1)S(1)}, bf16[2,8,128,128]{3,2,1,0:T(8,128)(2,1)}, u32[]{:S(2)}) copy-start(bf16[2,8,128,128]{3,2,1,0:T(8,128)(2,1)} %rating_ref.3) | copy-start | bytes 1572868
  8.4 13.7 %collective-permute-start.1 = (f32[128,256]{1,0:T(8,128)}, f32[128,256]{1,0:T(8,128)}, u32[]{:S(2)}, u32[]{:S(2)}) collective-permute-start(f32[128,256]{1,0:T(8,128)} %get-tuple-element.25), channel_id=1, source_target_pairs={{0,1},{1,0},{2,3},{3,2},{4,5},{5,4},{6,7},{7,6},{8,9},{9,8},{10,11... | collective-permute-start | bytes 393224 | tf_op jit(solution)/shard_map/ppermute | solution.py:112
  14.8 0.7 %copy-start.13 = (f32[128,256]{1,0:T(8,128)}, f32[128,256]{1,0:T(8,128)S(1)}, u32[]{:S(2)}) copy-start(f32[128,256]{1,0:T(8,128)S(1)} %get-tuple-element.26) | copy-start | bytes 393220
  15.4 7.7 %collective-permute-start = (f32[128,256]{1,0:T(8,128)}, f32[128,256]{1,0:T(8,128)}, u32[]{:S(2)}, u32[]{:S(2)}) collective-permute-start(f32[128,256]{1,0:T(8,128)} %get-tuple-element.23), channel_id=1, source_target_pairs={{0,1},{1,0},{2,3},{3,2},{4,5},{5,4},{6,7},{7,6},{8,9},{9,8},{10,11... | collective-permute-start | bytes 393224 | tf_op jit(solution)/shard_map/ppermute | solution.py:112
  15.5 8.3 %collective-permute-start.4 = (f32[128,256]{1,0:T(8,128)}, f32[128,256]{1,0:T(8,128)}, u32[]{:S(2)}, u32[]{:S(2)}) collective-permute-start(f32[128,256]{1,0:T(8,128)} %get-tuple-element.27), channel_id=1, source_target_pairs={{0,1},{1,0},{2,3},{3,2},{4,5},{5,4},{6,7},{7,6},{8,9},{9,8},{10,11... | collective-permute-start | bytes 393224 | tf_op jit(solution)/shard_map/ppermute | solution.py:112
  15.9 27.5 %collective-permute-start.14 = (f32[256,256]{1,0:T(8,128)S(1)}, f32[256,256]{1,0:T(8,128)S(1)}, u32[]{:S(2)}, u32[]{:S(2)}) collective-permute-start(f32[256,256]{1,0:T(8,128)S(1)} %get-tuple-element.21.users_ref), channel_id=1, source_target_pairs={{0,1},{1,0},{2,3},{3,2},{4,5},{5,4},{6,7},{7,6},{8,9},{9,8},{10,11... | collective-permute-start | bytes 786440 | tf_op jit(solution)/shard_map/ppermute | solution.py:112
  17.7 0.8 %copy-start.16 = (f32[4,256,128]{2,1,0:T(8,128)}, f32[4,256,128]{2,1,0:T(8,128)S(1)}, u32[]{:S(2)}) copy-start(f32[4,256,128]{2,1,0:T(8,128)S(1)} %get-tuple-element.31) | copy-start | bytes 1572868
  18.5 25.0 %collective-permute-start.15 = (f32[4,256,128]{2,1,0:T(8,128)}, f32[4,256,128]{2,1,0:T(8,128)S(1)}, u32[]{:S(2)}, u32[]{:S(2)}) collective-permute-start(f32[4,256,128]{2,1,0:T(8,128)} %get-tuple-element.30), channel_id=1, source_target_pairs={{0,1},{1,0},{2,3},{3,2},{4,5},{5,4},{6,7},{7,6},{8,9},{9,8},{10,11... | collective-permute-start | bytes 1572872 | tf_op jit(solution)/shard_map/ppermute | solution.py:112
  18.9 1.0 %copy-start.8 = (bf16[8,256,128]{2,1,0:T(8,128)(2,1)S(1)}, bf16[8,256,128]{2,1,0:T(8,128)(2,1)}, u32[]{:S(2)}) copy-start(bf16[8,256,128]{2,1,0:T(8,128)(2,1)} %copy-done.7) | copy-start | bytes 1572868
  20.0 1.0 %copy-start.10 = (bf16[8,256,128]{2,1,0:T(8,128)(2,1)S(1)}, bf16[8,256,128]{2,1,0:T(8,128)(2,1)}, u32[]{:S(2)}) copy-start(bf16[8,256,128]{2,1,0:T(8,128)(2,1)} %copy-done.9) | copy-start | bytes 1572868
  21.0 1.1 %copy-start.17 = (f32[4,256,128]{2,1,0:T(8,128)S(1)}, f32[4,256,128]{2,1,0:T(8,128)}, u32[]{:S(2)}) copy-start(f32[4,256,128]{2,1,0:T(8,128)} %copy-done.16) | copy-start | bytes 1572868
  21.0 2.2 %copy-start.19 = (f32[128,256]{1,0:T(8,128)S(1)}, f32[128,256]{1,0:T(8,128)}, u32[]{:S(2)}) copy-start(f32[128,256]{1,0:T(8,128)} %copy-done.18) | copy-start | bytes 393220
  21.0 2.7 %copy-start.14 = (f32[128,256]{1,0:T(8,128)S(1)}, f32[128,256]{1,0:T(8,128)}, u32[]{:S(2)}) copy-start(f32[128,256]{1,0:T(8,128)} %copy-done.13) | copy-start | bytes 393220
  22.1 21.4 %collective-permute-start.16 = (f32[4,256,128]{2,1,0:T(8,128)S(1)}, f32[4,256,128]{2,1,0:T(8,128)S(1)}, u32[]{:S(2)}, u32[]{:S(2)}) collective-permute-start(f32[4,256,128]{2,1,0:T(8,128)S(1)} %copy-done.17), channel_id=1, source_target_pairs={{0,1},{1,0},{2,3},{3,2},{4,5},{5,4},{6,7},{7,6},{8,9},{9,8},{10,11... | collective-permute-start | bytes 1572872 | tf_op jit(solution)/shard_map/ppermute | solution.py:112
  23.2 1.7 %collective-permute-start.5 = (f32[128,256]{1,0:T(8,128)S(1)}, f32[128,256]{1,0:T(8,128)S(1)}, u32[]{:S(2)}, u32[]{:S(2)}) collective-permute-start(f32[128,256]{1,0:T(8,128)S(1)} %copy-done.19), channel_id=1, source_target_pairs={{0,1},{1,0},{2,3},{3,2},{4,5},{5,4},{6,7},{7,6},{8,9},{9,8},{10,11... | collective-permute-start | bytes 393224 | tf_op jit(solution)/shard_map/ppermute | solution.py:112
  23.7 5.1 %collective-permute-start.2 = (f32[128,256]{1,0:T(8,128)S(1)}, f32[128,256]{1,0:T(8,128)S(1)}, u32[]{:S(2)}, u32[]{:S(2)}) collective-permute-start(f32[128,256]{1,0:T(8,128)S(1)} %add.57), channel_id=1, source_target_pairs={{0,2},{1,3},{2,0},{3,1},{4,6},{5,7},{6,4},{7,5},{8,10},{9,11},{10,... | collective-permute-start | bytes 393224 | tf_op jit(solution)/shard_map/ppermute | solution.py:112
  25.0 6.6 %collective-permute-start.6 = (f32[128,256]{1,0:T(8,128)S(1)}, f32[128,256]{1,0:T(8,128)S(1)}, u32[]{:S(2)}, u32[]{:S(2)}) collective-permute-start(f32[128,256]{1,0:T(8,128)S(1)} %add.64), channel_id=1, source_target_pairs={{0,2},{1,3},{2,0},{3,1},{4,6},{5,7},{6,4},{7,5},{8,10},{9,11},{10,... | collective-permute-start | bytes 393224 | tf_op jit(solution)/shard_map/ppermute | solution.py:112
  28.8 10.9 %collective-permute-start.3 = (f32[128,256]{1,0:T(8,128)S(1)}, f32[128,256]{1,0:T(8,128)S(1)}, u32[]{:S(2)}, u32[]{:S(2)}) collective-permute-start(f32[128,256]{1,0:T(8,128)S(1)} %multiply_add_fusion.3), channel_id=1, source_target_pairs={{0,6},{1,7},{2,4},{3,5},{4,10},{5,11},{6,8},{7,9},{8,14},{9,15},{1... | collective-permute-start | bytes 393224 | tf_op jit(solution)/shard_map/ppermute | solution.py:120
  31.6 11.8 %collective-permute-start.7 = (f32[128,256]{1,0:T(8,128)S(1)}, f32[128,256]{1,0:T(8,128)S(1)}, u32[]{:S(2)}, u32[]{:S(2)}) collective-permute-start(f32[128,256]{1,0:T(8,128)S(1)} %multiply_add_fusion.2), channel_id=1, source_target_pairs={{0,6},{1,7},{2,4},{3,5},{4,10},{5,11},{6,8},{7,9},{8,14},{9,15},{1... | collective-permute-start | bytes 393224 | tf_op jit(solution)/shard_map/ppermute | solution.py:120
  39.8 11.4 %collective-permute-start.10 = (f32[128,256]{1,0:T(8,128)S(1)}, f32[128,256]{1,0:T(8,128)S(1)}, u32[]{:S(2)}, u32[]{:S(2)}) collective-permute-start(f32[128,256]{1,0:T(8,128)S(1)} %collective-permute-done.3.rest_0_.items_ref), channel_id=1, source_target_pairs={{0,2},{1,3},{2,0},{3,1},{4,6},{5,7},{6,4},{7,5},{8,10},{9,11},{10,... | collective-permute-start | bytes 393224 | tf_op jit(solution)/shard_map/ppermute | solution.py:112
  43.5 6.6 %collective-permute-start.11 = (f32[128,256]{1,0:T(8,128)S(1)}, f32[128,256]{1,0:T(8,128)S(1)}, u32[]{:S(2)}, u32[]{:S(2)}) collective-permute-start(f32[128,256]{1,0:T(8,128)S(1)} %collective-permute-done.7.rest_1_.items_ref), channel_id=1, source_target_pairs={{0,2},{1,3},{2,0},{3,1},{4,6},{5,7},{6,4},{7,5},{8,10},{9,11},{10,... | collective-permute-start | bytes 393224 | tf_op jit(solution)/shard_map/ppermute | solution.py:112
  44.5 8.9 %collective-permute-start.17 = (f32[128,256]{1,0:T(8,128)S(1)}, f32[128,256]{1,0:T(8,128)S(1)}, u32[]{:S(2)}, u32[]{:S(2)}) collective-permute-start(f32[128,256]{1,0:T(8,128)S(1)} %shard_map.101), channel_id=1, source_target_pairs={{0,2},{1,3},{2,0},{3,1},{4,6},{5,7},{6,4},{7,5},{8,10},{9,11},{10,... | collective-permute-start | bytes 393224 | tf_op jit(solution)/shard_map/ppermute | solution.py:112
  47.0 7.0 %collective-permute-start.9 = (f32[128,256]{1,0:T(8,128)S(1)}, f32[128,256]{1,0:T(8,128)S(1)}, u32[]{:S(2)}, u32[]{:S(2)}) collective-permute-start(f32[128,256]{1,0:T(8,128)S(1)} %collective-permute-done.7.rest_1_.items_ref), channel_id=1, source_target_pairs={{0,1},{1,0},{2,3},{3,2},{4,5},{5,4},{6,7},{7,6},{8,9},{9,8},{10,11... | collective-permute-start | bytes 393224 | tf_op jit(solution)/shard_map/ppermute | solution.py:112
  49.0 5.1 %collective-permute-start.8 = (f32[128,256]{1,0:T(8,128)S(1)}, f32[128,256]{1,0:T(8,128)S(1)}, u32[]{:S(2)}, u32[]{:S(2)}) collective-permute-start(f32[128,256]{1,0:T(8,128)S(1)} %collective-permute-done.3.rest_0_.items_ref), channel_id=1, source_target_pairs={{0,1},{1,0},{2,3},{3,2},{4,5},{5,4},{6,7},{7,6},{8,9},{9,8},{10,11... | collective-permute-start | bytes 393224 | tf_op jit(solution)/shard_map/ppermute | solution.py:112
  50.1 3.9 %collective-permute-start.19 = (f32[128,256]{1,0:T(8,128)S(1)}, f32[128,256]{1,0:T(8,128)S(1)}, u32[]{:S(2)}, u32[]{:S(2)}) collective-permute-start(f32[128,256]{1,0:T(8,128)S(1)} %shard_map.103), channel_id=1, source_target_pairs={{0,2},{1,3},{2,0},{3,1},{4,6},{5,7},{6,4},{7,5},{8,10},{9,11},{10,... | collective-permute-start | bytes 393224 | tf_op jit(solution)/shard_map/ppermute | solution.py:112
  51.2 3.6 %copy-start.12 = (f32[2,256,256]{2,1,0:T(8,128)S(1)}, f32[2,256,256]{2,1,0:T(8,128)}, u32[]{:S(2)}) copy-start(f32[2,256,256]{2,1,0:T(8,128)} %noise_ref.3) | copy-start | bytes 1572868
  51.2 2.9 %collective-permute-start.13 = (f32[128,256]{1,0:T(8,128)S(1)}, f32[128,256]{1,0:T(8,128)S(1)}, u32[]{:S(2)}, u32[]{:S(2)}) collective-permute-start(f32[128,256]{1,0:T(8,128)S(1)} %collective-permute-done.11.rest_5_.items_ref), channel_id=1, source_target_pairs={{0,1},{1,0},{2,3},{3,2},{4,5},{5,4},{6,7},{7,6},{8,9},{9,8},{10,11... | collective-permute-start | bytes 393224 | tf_op jit(solution)/shard_map/ppermute | solution.py:112
  53.4 1.4 %collective-permute-start.12 = (f32[128,256]{1,0:T(8,128)S(1)}, f32[128,256]{1,0:T(8,128)S(1)}, u32[]{:S(2)}, u32[]{:S(2)}) collective-permute-start(f32[128,256]{1,0:T(8,128)S(1)} %collective-permute-done.10.rest_4_.items_ref), channel_id=1, source_target_pairs={{0,1},{1,0},{2,3},{3,2},{4,5},{5,4},{6,7},{7,6},{8,9},{9,8},{10,11... | collective-permute-start | bytes 393224 | tf_op jit(solution)/shard_map/ppermute | solution.py:112
  54.0 9.2 %collective-permute-start.18 = (f32[128,256]{1,0:T(8,128)S(1)}, f32[128,256]{1,0:T(8,128)S(1)}, u32[]{:S(2)}, u32[]{:S(2)}) collective-permute-start(f32[128,256]{1,0:T(8,128)S(1)} %multiply_add_fusion.1), channel_id=1, source_target_pairs={{0,6},{1,7},{2,4},{3,5},{4,10},{5,11},{6,8},{7,9},{8,14},{9,15},{1... | collective-permute-start | bytes 393224 | tf_op jit(solution)/shard_map/ppermute | solution.py:120
  54.0 11.0 %collective-permute-start.20 = (f32[128,256]{1,0:T(8,128)S(1)}, f32[128,256]{1,0:T(8,128)S(1)}, u32[]{:S(2)}, u32[]{:S(2)}) collective-permute-start(f32[128,256]{1,0:T(8,128)S(1)} %multiply_add_fusion), channel_id=1, source_target_pairs={{0,6},{1,7},{2,4},{3,5},{4,10},{5,11},{6,8},{7,9},{8,14},{9,15},{1... | collective-permute-start | bytes 393224 | tf_op jit(solution)/shard_map/ppermute | solution.py:120

commit v2 on v0

v2 whole, which is shorter than its diff:
```python
import functools
import math

import jax
import jax.numpy as jnp
from jax import lax
from jax.experimental import pallas as pl
from jax.experimental.pallas import tpu as pltpu
from jax.sharding import PartitionSpec as P

STEP_SIZE = 0.001
LIKELIHOOD = 20.0
NOISE_SCALE = math.sqrt(0.002)
GAIN = STEP_SIZE * LIKELIHOOD
AXES = ("blk", "grp")
TILE = 128
CHUNKS = 2
WEIGHT = 8
THIRD = 64
SHORT = 4
MOVE = 64
VMEM_LIMIT = 16 * 1024 * 1024

NN = (((1,), (0,)), ((), ()))
NT = (((1,), (1,)), ((), ()))
TN = (((0,), (0,)), ((), ()))


def halves(value):
    high = value.astype(jnp.bfloat16)
    low = (value - high.astype(jnp.float32)).astype(jnp.bfloat16)
    return high, low


def product(left, right, dims):
    dot = functools.partial(
        lax.dot_general, dimension_numbers=dims, preferred_element_type=jnp.float32
    )
    return dot(left[0], right[0]) + (dot(left[0], right[1]) + dot(left[1], right[0]))


def errors_of(item_halves, user_halves, rating, weight):
    predicted = product(item_halves, user_halves, NT)
    return halves(weight.astype(jnp.float32) * (rating.astype(jnp.float32) - predicted))


def stepped(now, total, noise):
    return now + STEP_SIZE * (LIKELIHOOD * total - now) + NOISE_SCALE * noise


SCALARS = pl.BlockSpec(memory_space=pltpu.SMEM)
LOCAL = pl.BlockSpec(memory_space=pltpu.VMEM)
DISTANT = pl.BlockSpec(memory_space=pltpu.HBM)
AFTER = pl.BlockSpec(memory_space=pl.ANY)


def call(body, outs, operands, cost, scratch=(), after=()):
    unread = len(after)

    def kernel(*refs):
        body(*refs[unread:])

    return pl.pallas_call(
        kernel,
        in_specs=[AFTER] * unread + [spec for spec, _ in operands],
        out_specs=[LOCAL] * len(outs),
        out_shape=[jax.ShapeDtypeStruct(shape, dtype) for shape, dtype in outs],
        scratch_shapes=list(scratch),
        compiler_params=pltpu.CompilerParams(vmem_limit_bytes=VMEM_LIMIT),
        cost_estimate=pl.CostEstimate(
            flops=WEIGHT * cost, bytes_accessed=1 << 18, transcendentals=0
        ),
        name=body.__name__ if hasattr(body, "__name__") else body.func.__name__,
    )(*after, *[held(spec, array) for spec, array in operands])


def held(spec, array):
    return pltpu.with_memory_space_constraint(array, pltpu.HBM) if spec is DISTANT else array


def local(array):
    return (LOCAL, array)


def body(users, items, noise_users, noise_items, tile_index, counts, ratings, weights):
    f32, bf16 = jnp.float32, jnp.bfloat16
    n_blk, n_grp = lax.axis_size("blk"), lax.axis_size("grp")
    owned, rank = users.shape
    slots = ratings.shape[1]
    columns = items.shape[0] // TILE
    per_quarter = columns // n_grp
    quarter = per_quarter * TILE
    chunk = quarter // CHUNKS
    place = (SCALARS, lax.axis_index("grp").astype(jnp.int32).reshape(1))

    def swap(value, other):
        pairs = [
            (b * n_grp + g, b * n_grp + (g ^ other)) for b in range(n_blk) for g in range(n_grp)
        ]
        with jax.named_scope("core_swap" if other == 1 else "chip_swap"):
            return lax.ppermute(value, AXES, pairs)

    def onward(value):
        pairs = [
            (b * n_grp + g, (b + 1) % n_blk * n_grp + (g ^ 2))
            for b in range(n_blk)
            for g in range(n_grp)
        ]
        with jax.named_scope("onward"):
            return lax.ppermute(value, AXES, pairs)

    dense = (columns, owned, TILE)
    piece = (chunk, rank)
    square = (quarter, owned)
    unit = 2 * owned * quarter * rank * 3

    def rows_of(place_ref, flip):
        return pl.ds(pl.multiple_of((place_ref[0] ^ flip) * quarter, quarter), quarter)

    def side_by_side(dense_ref, start):
        return jnp.concatenate([dense_ref[start + t] for t in range(per_quarter)], 1)

    def quarter_terms(place_ref, flip, rating_ref, weight_ref, users_ref, items_ref, high_ref, low_ref):
        start = (place_ref[0] ^ flip) * per_quarter
        user_halves = halves(users_ref[...])
        item_halves = halves(items_ref[rows_of(place_ref, flip), :])
        rating = side_by_side(rating_ref, start).astype(f32).T
        weight = side_by_side(weight_ref, start).astype(f32).T
        errors = errors_of(item_halves, user_halves, rating, weight)
        high_ref[...], low_ref[...] = errors
        return product(errors, user_halves, NN)

    def put(value, outs):
        for k, out in enumerate(outs):
            out[...] = value[k * chunk : (k + 1) * chunk, :]

    def fetch(pairs, sems):
        copies = [pltpu.make_async_copy(a, b, sems.at[n]) for n, (a, b) in enumerate(pairs)]
        for copy in copies:
            copy.start()
        return copies

    live = counts.reshape(-1)
    tables = [(DISTANT, tile_index), (DISTANT, live), (DISTANT, ratings), (DISTANT, weights)]
    landing = [
        pltpu.SMEM(tile_index.shape, jnp.int32),
        pltpu.SMEM(live.shape, jnp.int32),
        pltpu.VMEM(ratings.shape[1:], bf16),
        pltpu.VMEM(weights.shape[1:], bf16),
    ]

    def first(place_ref, index_hbm, count_hbm, rating_hbm, weight_hbm, users_hbm, items_hbm,
              rating_out, weight_out, users_out, items_out, high_out, low_out, *rest):
        outs, (index_ref, count_ref, rating_in, weight_in, sems) = rest[:CHUNKS], rest[CHUNKS:]
        copies = fetch(
            [(index_hbm, index_ref), (count_hbm, count_ref),
             (rating_hbm.at[0], rating_in), (weight_hbm.at[0], weight_in),
             (users_hbm, users_out), (items_hbm, items_out)],
            sems,
        )
        rating_out[...] = jnp.zeros_like(rating_out)
        weight_out[...] = jnp.zeros_like(weight_out)
        for copy in copies[:4]:
            copy.wait()
        for slot in range(slots):

            @pl.when(slot < count_ref[0])
            def _(slot=slot):
                tile = index_ref[0, slot]
                column = lax.rem(tile, columns)
                row = pl.multiple_of(lax.div(tile, columns) * TILE, TILE)
                rating_out[column, pl.ds(row, TILE), :] = rating_in[slot]
                weight_out[column, pl.ds(row, TILE), :] = weight_in[slot]

        copies[4].wait()
        copies[5].wait()
        put(quarter_terms(place_ref, 1, rating_out, weight_out, users_out, items_out,
                          high_out, low_out), outs)

    rating_0, weight_0, users_0, items_0, *rest = call(
        first,
        [(dense, bf16)] * 2 + [(users.shape, f32), (items.shape, f32)] + [(square, bf16)] * 2
        + [(piece, f32)] * CHUNKS,
        [place] + tables + [(DISTANT, users), (DISTANT, items)],
        2 * unit,
        landing + [pltpu.SemaphoreType.DMA((6,))],
    )
    errors_1, to_sibling = rest[:2], rest[2:]
    from_sibling = [swap(value, 1) for value in to_sibling]
    stage_0 = [local(rating_0), local(weight_0), local(users_0), local(items_0)]

    def second(place_ref, rating_ref, weight_ref, users_ref, items_ref, high_out, low_out, *outs):
        put(quarter_terms(place_ref, 0, rating_ref, weight_ref, users_ref, items_ref,
                          high_out, low_out), outs)

    high_0, low_0, *mine = call(
        second, [(square, bf16)] * 2 + [(piece, f32)] * CHUNKS, [place] + stage_0, 2 * unit
    )
    errors_0 = [high_0, low_0]

    def join(a_ref, b_ref, out):
        out[...] = a_ref[...] + b_ref[...]

    def add_scaled(base_ref, *rest):
        total = rest[0][...]
        for ref in rest[1:-1]:
            total = total + ref[...]
        rest[-1][...] = base_ref[...] + GAIN * total

    to_chip = []
    for k in range(CHUNKS):
        [value] = call(join, [(piece, f32)], [local(mine[k]), local(from_sibling[k])], 1, after=to_chip[-1:])
        to_chip.append(value)
    from_chip = [swap(value, 2) for value in to_chip]

    def third(place_ref, rating_ref, weight_ref, users_ref, items_ref, noise_hbm,
              high_3, low_3, high_2, low_2, *rest):
        outs, bases, (noise, sems) = rest[:CHUNKS], rest[CHUNKS : 2 * CHUNKS], rest[2 * CHUNKS :]
        [copy] = fetch([(noise_hbm.at[0, rows_of(place_ref, 2), :], noise)], sems)
        args = (rating_ref, weight_ref, users_ref, items_ref)
        put(quarter_terms(place_ref, 3, *args, high_3, low_3), outs)
        total = quarter_terms(place_ref, 2, *args, high_2, low_2)
        copy.wait()
        put(stepped(items_ref[rows_of(place_ref, 2), :], total, noise[...]), bases)

    *rest, = call(
        third,
        [(square, bf16)] * 4 + [(piece, f32)] * (2 * CHUNKS),
        [place] + stage_0 + [(DISTANT, noise_items)],
        THIRD * unit,
        [pltpu.VMEM((quarter, rank), f32), pltpu.SemaphoreType.DMA((1,))],
        after=to_chip,
    )
    errors_3, errors_2, to_sibling, base = rest[:2], rest[2:4], rest[4 : 4 + CHUNKS], rest[4 + CHUNKS :]
    from_sibling = [swap(value, 1) for value in to_sibling]

    def user_step(place_ref, users_ref, items_ref, noise_hbm, *rest):
        errors, (users_out, noise, sems) = rest[:-3], rest[-3:]
        [copy] = fetch([(noise_hbm.at[0], noise)], sems)
        total = jnp.zeros((owned, rank), f32)
        for flip in range(n_grp):
            item_halves = halves(items_ref[rows_of(place_ref, flip), :])
            kept = (errors[2 * flip][...], errors[2 * flip + 1][...])
            total = total + product(kept, item_halves, TN)
        copy.wait()
        users_out[...] = stepped(users_ref[...], total, noise[...])

    [users_1] = call(
        user_step,
        [(users.shape, f32)],
        [place, local(users_0), local(items_0), (DISTANT, noise_users)]
        + [local(v) for v in errors_0 + errors_1 + errors_2 + errors_3],
        SHORT * unit,
        [pltpu.VMEM(users.shape, f32), pltpu.SemaphoreType.DMA((1,))],
        after=to_sibling,
    )
    users_s = swap(users_1, 1)

    flat = (columns * TILE, owned)
    half = (columns * TILE // 2, owned)

    def layout(place_ref, index_hbm, count_hbm, rating_hbm, weight_hbm, noise_hbm,
               rating_out, weight_out, rating_send, weight_send, noise_out,
               index_ref, count_ref, rating_in, weight_in, sems):
        copies = fetch(
            [(index_hbm, index_ref), (count_hbm, count_ref),
             (rating_hbm.at[1], rating_in), (weight_hbm.at[1], weight_in),
             (noise_hbm.at[1, rows_of(place_ref, 2), :], noise_out)],
            sems,
        )
        rating_out[...] = jnp.zeros_like(rating_out)
        weight_out[...] = jnp.zeros_like(weight_out)
        for copy in copies[:4]:
            copy.wait()
        for slot in range(slots):

            @pl.when(slot < count_ref[1])
            def _(slot=slot):
                tile = index_ref[1, slot]
                at = pl.ds(pl.multiple_of(lax.rem(tile, columns) * TILE, TILE), TILE)
                turned = (rating_in[slot].astype(f32).T, weight_in[slot].astype(f32).T)
                for row in range(owned // TILE):

                    @pl.when(lax.div(tile, columns) == row)
                    def _(row=row):
                        across = slice(row * TILE, (row + 1) * TILE)
                        rating_out[at, across] = turned[0]
                        weight_out[at, across] = turned[1]

        for n, flip in enumerate((1, 3)):
            rows = slice(n * quarter, (n + 1) * quarter)
            rating_send[rows, :] = rating_out[rows_of(place_ref, flip), :]
            weight_send[rows, :] = weight_out[rows_of(place_ref, flip), :]
        copies[4].wait()

    rating_1, weight_1, rating_send, weight_send, noise_1 = call(
        layout,
        [(flat, f32)] * 2 + [(half, f32)] * 2 + [((quarter, rank), f32)],
        [place] + tables + [(DISTANT, noise_items)],
        SHORT * unit,
        landing + [pltpu.SemaphoreType.DMA((5,))],
        after=[users_1],
    )
    rating_s, weight_s = swap(rating_send, 1), swap(weight_send, 1)

    moved = []
    for k in range(CHUNKS):
        [value] = call(
            add_scaled, [(piece, f32)],
            [local(v) for v in (base[k], from_sibling[k], from_chip[k])], MOVE * unit,
            after=[rating_send, *moved[-1:]],
        )
        moved.append(value)
    ahead = [onward(value) for value in moved]

    def late(k, slot, place_ref, items_ref, users_ref, users_s_ref, rating_ref, weight_ref,
             rating_s_ref, weight_s_ref, *rest):
        high_out, low_out, copy_out, out = rest[-4:]
        own, other = halves(users_ref[...]), halves(users_s_ref[...])
        now = items_ref[...]
        copy_out[...] = now
        item_halves = halves(now)
        at = pl.ds(pl.multiple_of((place_ref[0] ^ (2 * slot)) * quarter + k * chunk, chunk), chunk)
        errors = errors_of(item_halves, own, rating_ref[at, :], weight_ref[at, :])
        high_out[...], low_out[...] = errors
        total = product(errors, own, NN)
        at = slice(slot * quarter + k * chunk, slot * quarter + (k + 1) * chunk)
        errors = errors_of(item_halves, other, rating_s_ref[at, :], weight_s_ref[at, :])
        total = total + product(errors, other, NN)
        if slot == 1:
            total = stepped(now, total, rest[0][k * chunk : (k + 1) * chunk, :])
        out[...] = total

    common = [local(v) for v in (users_1, users_s, rating_1, weight_1, rating_s, weight_s)]
    errors_shape = (chunk, owned)
    late_outs = [(errors_shape, bf16)] * 2 + [(piece, f32)] * 2
    here = ahead
    there = [swap(value, 2) for value in here]
    errors_here, here_copy, sent = [], [], []
    for k in range(CHUNKS):
        high, low, rows, value = call(
            functools.partial(late, k, 0), late_outs, [place, local(here[k])] + common,
            4 * unit // CHUNKS, after=sent[-1:],
        )
        errors_here.append((high, low))
        here_copy.append(rows)
        sent.append(value)
    received = [swap(value, 2) for value in sent]
    errors_there, there_copy, finished = [], [], []
    for k in range(CHUNKS):
        high, low, rows, step = call(
            functools.partial(late, k, 1), late_outs,
            [place, local(there[k])] + common + [local(noise_1)], 4 * unit // CHUNKS,
            after=[sent[-1], *finished[-1:]],
        )
        [value] = call(add_scaled, [(piece, f32)], [local(step), local(received[k])], 1)
        errors_there.append((high, low))
        there_copy.append(rows)
        finished.append(value)
    final = [onward(value) for value in finished]
    here_s = [swap(value, 1) for value in here_copy]
    there_s = [swap(value, 1) for value in there_copy]

    def last(place_ref, rating_ref, weight_ref, users_ref, noise_hbm, *rest):
        known, blocks = rest[: 6 * CHUNKS], rest[6 * CHUNKS : 8 * CHUNKS]
        users_out, token, noise, sems = rest[8 * CHUNKS :]
        token[...] = jnp.zeros_like(token)
        [copy] = fetch([(noise_hbm.at[1], noise)], sems)
        user_halves = halves(users_ref[...])
        total = jnp.zeros((owned, rank), f32)
        for n in range(2 * CHUNKS):
            errors = (known[3 * n][...], known[3 * n + 1][...])
            total = total + product(errors, halves(known[3 * n + 2][...]), TN)
        for n, block in enumerate(blocks):
            flip, k = (1, 3)[n // CHUNKS], n % CHUNKS
            at = pl.ds(pl.multiple_of((place_ref[0] ^ flip) * quarter + k * chunk, chunk), chunk)
            item_halves = halves(block[...])
            errors = errors_of(item_halves, user_halves, rating_ref[at, :], weight_ref[at, :])
            total = total + product(errors, item_halves, TN)
        copy.wait()
        users_out[...] = stepped(users_ref[...], total, noise[...])

    known = [
        local(v)
        for errors, rows in zip(errors_here + errors_there, here + there)
        for v in (*errors, rows)
    ]
    users_out, token = call(
        last,
        [(users.shape, f32), ((8, 128), f32)],
        [place, local(rating_1), local(weight_1), local(users_1), (DISTANT, noise_users)]
        + known + [local(v) for v in here_s + there_s],
        6 * unit,
        [pltpu.VMEM(users.shape, f32), pltpu.SemaphoreType.DMA((1,))],
        after=finished,
    )

    def gather(*refs):
        for k in range(CHUNKS):
            refs[-1][k * chunk : (k + 1) * chunk, :] = refs[k][...]

    [items_out] = call(
        gather, [((quarter, rank), f32)], [local(v) for v in final], 1, after=[token]
    )
    return (users_out, items_out)


def solution(mesh):
    in_specs = (
        P(("blk", "grp"), None),
        P("blk", None),
        P(None, ("blk", "grp"), None),
        P(None, "blk", None),
        P(None, ("blk", "grp")),
        P(None, ("blk", "grp")),
        P(None, ("blk", "grp"), None, None),
        P(None, ("blk", "grp"), None, None),
    )
    out_specs = (P(("blk", "grp"), None), P(("blk", "grp"), None))
    return jax.shard_map(body, mesh=mesh, in_specs=in_specs, out_specs=out_specs, check_vma=False)
```

time: 199 us -> 55.9 us (0.28)
  waiting for transfers between devices: 145 us -> 23.9 us
  Pallas kernels: 0 us -> 14.8 us
  matrix products: 13.7 us -> 0 us
  between operations: 14.3 us -> 0.83 us
  local copies, waits for them, and re-layouts: 11.6 us -> 0 us
  starting transfers between devices: 4.89 us -> 16.1 us
  other arithmetic: 8.85 us -> 0 us
    psum x2 -> x0, waiting for transfers between devices: 94.2 us -> none  [body(): summed = lax.psum(grad_items, 'grp')]
    ppermute x2 -> x21, waiting for transfers between devices: 50.8 us -> 23.9 us  [the longest x4 21.3 us: onward(): return lax.ppermute(value, AXES, pairs)]
    pallas_call x0 -> x17, Pallas kernels: none -> 14.8 us  [call(): pl.pallas_call(kernel, in_specs=[AFTER] * unread + [spec for spec, _ in o...]
    dot_general x10 -> x0, matrix products: 13.7 us -> none  [the longest x2 4.38 us: slot_terms(): jnp.einsum('mik,mjk->mij', user_part, item_part, precision=HIGHEST)]
    ppermute x2 -> x21, starting transfers between devices: 4.81 us -> 16.1 us  [the longest x17 13.6 us: swap(): return lax.ppermute(value, AXES, pairs)]
    add x4 -> x0, other arithmetic: 6.73 us -> none  [the longest x2 5.9 us: body(): item_block + STEP_SIZE * (LIKELIHOOD * summed - item_block)]
    gather x4 -> x0, local copies, waits for them, and re-layouts: 5.91 us -> none  [the longest x2 3.68 us: slot_terms(): item_part = jnp.take(item_table, tile_col, axis=0)]
    dot_general x2 -> x0, local copies, waits for them, and re-layouts: 2.62 us -> none  [slot_terms(): jnp.einsum('mq,mjk->qjk', pick_item, item_grads, precision=HIGHEST)]
  transfers between devices with their start and end apart: 4 -> 21, of which waited for: 4 -> 7; matrix products, arithmetic and copies ran while one was open for 3% -> 0% of each run, Pallas kernels for 0% -> 21%
where the time goes in v2:
time: 55.9 us; the launch traced here: 55.6 us
  waiting for transfers between devices  23.9 us (43%)
  starting transfers between devices  16.1 us (29%)
  Pallas kernels  14.8 us (26%)
  between operations  0.83 us (1%)
    ppermute x4, waiting for transfers between devices, onward(): return lax.ppermute(value, AXES, pairs)  21.3 us
    pallas_call x17, Pallas kernels, call(): pl.pallas_call(kernel, in_specs=[AFTER] * unread + [spec for spec, _ in o...  14.8 us
    ppermute x17, starting transfers between devices, swap(): return lax.ppermute(value, AXES, pairs)  13.6 us
    ppermute x17, waiting for transfers between devices, swap(): return lax.ppermute(value, AXES, pairs)  2.61 us
    ppermute x4, starting transfers between devices, onward(): return lax.ppermute(value, AXES, pairs)  2.45 us
  transfers between devices with their start and end apart: 21, of which 7 were waited for; matrix products, arithmetic and copies ran while one was open for 0% of the time, Pallas kernels for 21%

profile of v2, /device:TPU:1, one launch (start us, length us, event | category | flops | bytes accessed | tf_op | source)
XLA Modules:
  0.0 55.6 jit_solution(11684794324249691444)
XLA Ops:
  0.6 2.2 %first.1 = (bf16[8,256,128]{2,1,0:T(8,128)(2,1)S(1)}, bf16[8,256,128]{2,1,0:T(8,128)(2,1)S(1)}, f32[256,256]{1,0:T(8,128)S(1)}, f32[1024,256]{1,0:T(8,128)S(1)},...) custom-call(s32[1]{0:T(128)} %bitcast.refs_0_.refs_2_.refs_1_, ...), custom_call_target="tpu_custom_call" | custom-call | flops 1610612736 | bytes 262144 | tf_op jit(solution)/shard_map/first/pallas_call | solution.py:63
  2.8 3.3 %collective-permute-start = (f32[128,256]{1,0:T(8,128)S(1)}, f32[128,256]{1,0:T(8,128)S(1)}, u32[]{:S(2)}, u32[]{:S(2)}) collective-permute-start(f32[128,256]{1,0:T(8,128)S(1)} %get-tuple-element.50), channel_id=1, source_target_pairs={{0,1},{1,0},{2,3},{3,2},{4,5},{5,4},{6,7},{7,6},{8,9},{9,8},{10,11... | collective-permute-start | bytes 393224 | tf_op jit(solution)/shard_map/core_swap/ppermute | solution.py:101
  6.1 0.1 collective-permute-start.1
  6.2 0.6 %second.1 = (bf16[256,256]{1,0:T(8,128)(2,1)S(1)}, bf16[256,256]{1,0:T(8,128)(2,1)S(1)}, f32[128,256]{1,0:T(8,128)S(1)}, f32[128,256]{1,0:T(8,128)S(1)}) custom-call(s32[1]{0:T(128)} %bitcast.refs_0_.refs_2_.refs_1_, bf16[8,256,128]{2,1,0:T(8,128)(2,1)S(1)} %get-tuple-element.45.refs_1_.refs_3_, bf16[8,256,128]{2,1,0:T(8,128)(2,1)S(1)} %get-tuple-element.46.refs_2_.refs_4_, ...), custom_call_target="tpu_custom_call" | custom-call | flops 1610612736 | bytes 262144 | tf_op jit(solution)/shard_map/second/pallas_call | solution.py:63
  6.9 0.2 collective-permute-done.refs_1_
  7.2 0.1 collective-permute-start.3
  7.3 0.2 collective-permute-done.1.refs_2_
  7.5 1.3 %collective-permute-start.9 = (f32[128,256]{1,0:T(8,128)S(1)}, f32[128,256]{1,0:T(8,128)S(1)}, u32[]{:S(2)}, u32[]{:S(2)}) collective-permute-start(f32[128,256]{1,0:T(8,128)S(1)} %join.3.refs_1_), channel_id=1, source_target_pairs={{0,2},{1,3},{2,0},{3,1},{4,6},{5,7},{6,4},{7,5},{8,10},{9,11},{10,... | collective-permute-start | bytes 393224 | tf_op jit(solution)/shard_map/chip_swap/ppermute | solution.py:101
  8.8 1.9 %third.1 = (bf16[256,256]{1,0:T(8,128)(2,1)S(1)}, bf16[256,256]{1,0:T(8,128)(2,1)S(1)}, bf16[256,256]{1,0:T(8,128)(2,1)S(1)}, bf16[256,256]{1,0:T(8,128)(2,1)S(1...) custom-call(f32[128,256]{1,0:T(8,128)S(1)} %join.2.refs_0_, ...), custom_call_target="tpu_custom_call" | custom-call | flops 51539607552 | bytes 262144 | tf_op jit(solution)/shard_map/third/pallas_call | solution.py:63
  10.7 1.0 %collective-permute-start.2 = (f32[128,256]{1,0:T(8,128)S(1)}, f32[128,256]{1,0:T(8,128)S(1)}, u32[]{:S(2)}, u32[]{:S(2)}) collective-permute-start(f32[128,256]{1,0:T(8,128)S(1)} %get-tuple-element.53.refs_0_), channel_id=1, source_target_pairs={{0,1},{1,0},{2,3},{3,2},{4,5},{5,4},{6,7},{7,6},{8,9},{9,8},{10,11... | collective-permute-start | bytes 393224 | tf_op jit(solution)/shard_map/core_swap/ppermute | solution.py:101
  11.7 0.1 collective-permute-start.8
  11.8 1.4 %user_step.1.refs_0_.refs_2_.refs_3_.refs_4_.refs_5_ = f32[256,256]{1,0:T(8,128)S(1)} custom-call(f32[128,256]{1,0:T(8,128)S(1)} %get-tuple-element.53.refs_0_, f32[128,256]{1,0:T(8,128)S(1)} %get-tuple-element.54.refs_1_, s32[1]{0:T(128)} %bitcast.refs_0_.refs_2_.refs_1_, f32[256,256]{1,0:T(8,128)S(1)} %get-tuple-element.47.refs_3_.refs_5_, ...), custom_call_target="tpu_custom_call" | custom-call | flops 3221225472 | bytes 262144 | tf_op jit(solution)/shard_map/user_step/pallas_call | solution.py:63
  13.2 1.7 %layout.1 = (f32[1024,256]{1,0:T(8,128)S(1)}, f32[1024,256]{1,0:T(8,128)S(1)}, f32[512,256]{1,0:T(8,128)S(1)}, f32[512,256]{1,0:T(8,128)S(1)}, f32[256,256]{1,0:T(8,128)S(1)}) custom-call(f32[256,256]{1,0:T(8,128)S(1)} %user_step.1.refs_0_.refs_2_.refs_3_.refs_4_.refs_5_, s32[1]{0:T(128)} %bitcast.refs_0_.refs_2_.refs_1_, s32[2,8]{1,0:T(2,128)} %refs_2_.1, ...), custom_call_target="tpu_custom_call" | custom-call | flops 3221225472 | bytes 262144 | tf_op jit(solution)/shard_map/layout/pallas_call | solution.py:63
  15.0 0.8 %collective-permute-start.5 = (f32[256,256]{1,0:T(8,128)S(1)}, f32[256,256]{1,0:T(8,128)S(1)}, u32[]{:S(2)}, u32[]{:S(2)}) collective-permute-start(f32[256,256]{1,0:T(8,128)S(1)} %user_step.1.refs_0_.refs_2_.refs_3_.refs_4_.refs_5_), channel_id=1, source_target_pairs={{0,1},{1,0},{2,3},{3,2},{4,5},{5,4},{6,7},{7,6},{8,9},{9,8},{10,11... | collective-permute-start | bytes 786440 | tf_op jit(solution)/shard_map/core_swap/ppermute | solution.py:101
  15.8 0.0 collective-permute-done.2.refs_2_
  15.8 0.1 collective-permute-start.6
  15.9 0.0 collective-permute-done.3.refs_3_
  15.9 0.4 collective-permute-start.7
  16.3 0.0 collective-permute-done.8.refs_3_
  16.3 0.5 collective-permute-start.4
  16.8 0.0 collective-permute-done.9.refs_4_
  16.9 1.8 %collective-permute-start.10 = (f32[128,256]{1,0:T(8,128)S(1)}, f32[128,256]{1,0:T(8,128)S(1)}, u32[]{:S(2)}, u32[]{:S(2)}) collective-permute-start(f32[128,256]{1,0:T(8,128)S(1)} %add_scaled.5), channel_id=1, source_target_pairs={{0,6},{1,7},{2,4},{3,5},{4,10},{5,11},{6,8},{7,9},{8,14},{9,15},{1... | collective-permute-start | bytes 393224 | tf_op jit(solution)/shard_map/onward/ppermute | solution.py:110
  18.6 9.7 %collective-permute-done.4.refs_1_.refs_9_ = f32[128,256]{1,0:T(8,128)S(1)} collective-permute-done((f32[128,256]{1,0:T(8,128)S(1)}, f32[128,256]{1,0:T(8,128)S(1)}, u32[]{:S(2)}, u32[]{:S(2)}) %collective-permute-start.4) | collective-permute-done | bytes 131104 | tf_op jit(solution)/shard_map/onward/ppermute | solution.py:110
  28.3 0.0 collective-permute-start.11
  28.4 2.8 %collective-permute-done.10.refs_2_.refs_12_ = f32[128,256]{1,0:T(8,128)S(1)} collective-permute-done((f32[128,256]{1,0:T(8,128)S(1)}, f32[128,256]{1,0:T(8,128)S(1)}, u32[]{:S(2)}, u32[]{:S(2)}) %collective-permute-start.10) | collective-permute-done | bytes 131104 | tf_op jit(solution)/shard_map/onward/ppermute | solution.py:110
  31.2 0.0 collective-permute-start.13
  31.2 0.0 collective-permute-done.5.refs_3_.refs_4_.refs_5_
  31.2 0.0 collective-permute-done.6.refs_6_.refs_7_.refs_8_
  31.2 0.9 %late.4 = (bf16[128,256]{1,0:T(8,128)(2,1)S(1)}, bf16[128,256]{1,0:T(8,128)(2,1)S(1)}, f32[128,256]{1,0:T(8,128)S(1)}, f32[128,256]{1,0:T(8,128)S(1)}) custom-call(s32[1]{0:T(128)} %bitcast.refs_0_.refs_2_.refs_1_, f32[128,256]{1,0:T(8,128)S(1)} %collective-permute-done.4.refs_1_.refs_9_, f32[256,256]{1,0:T(8,128)S(1)} %user_step.1.refs_0_.refs_2_.refs_3_.refs_4_.refs_5_, ...), custom_call_target="tpu_custom_call" | custom-call | flops 1610612736 | bytes 262144 | tf_op jit(solution)/shard_map/late/pallas_call | solution.py:63
  32.1 1.7 %collective-permute-start.12 = (f32[128,256]{1,0:T(8,128)S(1)}, f32[128,256]{1,0:T(8,128)S(1)}, u32[]{:S(2)}, u32[]{:S(2)}) collective-permute-start(f32[128,256]{1,0:T(8,128)S(1)} %get-tuple-element.68.refs_0_), channel_id=1, source_target_pairs={{0,2},{1,3},{2,0},{3,1},{4,6},{5,7},{6,4},{7,5},{8,10},{9,11},{10,... | collective-permute-start | bytes 393224 | tf_op jit(solution)/shard_map/chip_swap/ppermute | solution.py:101
  33.8 0.9 %late.5 = (bf16[128,256]{1,0:T(8,128)(2,1)S(1)}, bf16[128,256]{1,0:T(8,128)(2,1)S(1)}, f32[128,256]{1,0:T(8,128)S(1)}, f32[128,256]{1,0:T(8,128)S(1)}) custom-call(f32[128,256]{1,0:T(8,128)S(1)} %get-tuple-element.68.refs_0_, s32[1]{0:T(128)} %bitcast.refs_0_.refs_2_.refs_1_, f32[128,256]{1,0:T(8,128)S(1)} %collective-permute-done.10.refs_2_.refs_12_, ...), custom_call_target="tpu_custom_call" | custom-call | flops 1610612736 | bytes 262144 | tf_op jit(solution)/shard_map/late/pallas_call | solution.py:63
  34.6 0.1 collective-permute-start.14
  34.8 0.0 collective-permute-done.11.refs_2_.refs_15_
  34.8 0.9 %late.6 = (bf16[128,256]{1,0:T(8,128)(2,1)S(1)}, bf16[128,256]{1,0:T(8,128)(2,1)S(1)}, f32[128,256]{1,0:T(8,128)S(1)}, f32[128,256]{1,0:T(8,128)S(1)}) custom-call(f32[128,256]{1,0:T(8,128)S(1)} %get-tuple-element.70.refs_0_, s32[1]{0:T(128)} %bitcast.refs_0_.refs_2_.refs_1_, f32[128,256]{1,0:T(8,128)S(1)} %collective-permute-done.11.refs_2_.refs_15_, ...), custom_call_target="tpu_custom_call" | custom-call | flops 1610612736 | bytes 262144 | tf_op jit(solution)/shard_map/late/pallas_call | solution.py:63
  35.6 1.6 %collective-permute-start.17 = (f32[128,256]{1,0:T(8,128)S(1)}, f32[128,256]{1,0:T(8,128)S(1)}, u32[]{:S(2)}, u32[]{:S(2)}) collective-permute-start(f32[128,256]{1,0:T(8,128)S(1)} %get-tuple-element.84), channel_id=1, source_target_pairs={{0,1},{1,0},{2,3},{3,2},{4,5},{5,4},{6,7},{7,6},{8,9},{9,8},{10,11... | collective-permute-start | bytes 393224 | tf_op jit(solution)/shard_map/core_swap/ppermute | solution.py:101
  37.3 0.1 collective-permute-start.16
  37.4 1.0 %collective-permute-done.12.refs_1_ = f32[128,256]{1,0:T(8,128)S(1)} collective-permute-done((f32[128,256]{1,0:T(8,128)S(1)}, f32[128,256]{1,0:T(8,128)S(1)}, u32[]{:S(2)}, u32[]{:S(2)}) %collective-permute-start.12) | collective-permute-done | bytes 131104 | tf_op jit(solution)/shard_map/chip_swap/ppermute | solution.py:101
  38.4 2.7 %collective-permute-start.15 = (f32[128,256]{1,0:T(8,128)S(1)}, f32[128,256]{1,0:T(8,128)S(1)}, u32[]{:S(2)}, u32[]{:S(2)}) collective-permute-start(f32[128,256]{1,0:T(8,128)S(1)} %get-tuple-element.82), channel_id=1, source_target_pairs={{0,1},{1,0},{2,3},{3,2},{4,5},{5,4},{6,7},{7,6},{8,9},{9,8},{10,11... | collective-permute-start | bytes 393224 | tf_op jit(solution)/shard_map/core_swap/ppermute | solution.py:101
  41.1 0.0 collective-permute-done.13.refs_3_.refs_18_
  41.1 0.9 %late.7 = (bf16[128,256]{1,0:T(8,128)(2,1)S(1)}, bf16[128,256]{1,0:T(8,128)(2,1)S(1)}, f32[128,256]{1,0:T(8,128)S(1)}, f32[128,256]{1,0:T(8,128)S(1)}) custom-call(f32[128,256]{1,0:T(8,128)S(1)} %get-tuple-element.70.refs_0_, f32[128,256]{1,0:T(8,128)S(1)} %add_scaled.6.refs_1_.refs_0_, s32[1]{0:T(128)} %bitcast.refs_0_.refs_2_.refs_1_, ...), custom_call_target="tpu_custom_call" | custom-call | flops 1610612736 | bytes 262144 | tf_op jit(solution)/shard_map/late/pallas_call | solution.py:63
  42.0 0.1 collective-permute-start.18
  42.1 0.1 collective-permute-start.19
  42.2 0.1 collective-permute-start.20
  42.3 0.0 collective-permute-done.15.refs_19_
  42.3 1.1 %collective-permute-done.18.refs_22_ = f32[128,256]{1,0:T(8,128)S(1)} collective-permute-done((f32[128,256]{1,0:T(8,128)S(1)}, f32[128,256]{1,0:T(8,128)S(1)}, u32[]{:S(2)}, u32[]{:S(2)}) %collective-permute-start.18) | collective-permute-done | bytes 131104 | tf_op jit(solution)/shard_map/core_swap/ppermute | solution.py:101
  43.4 2.7 %last.1 = (f32[256,256]{1,0:T(8,128)}, f32[8,128]{1,0:T(8,128)S(1)}) custom-call(f32[128,256]{1,0:T(8,128)S(1)} %add_scaled.6.refs_1_.refs_0_, f32[128,256]{1,0:T(8,128)S(1)} %add_scaled.7.refs_1_, s32[1]{0:T(128)} %bitcast.refs_0_.refs_2_.refs_1_, f32[1024,256]{1,0:T(8,128)S(1)} %get-tuple-element.65.refs_4_.refs_5_.refs_6_.refs_3_, ...), custom_call_target="tpu_custom_call" | custom-call | flops 4831838208 | bytes 262144 | tf_op jit(solution)/shard_map/last/pallas_call | solution.py:63
  46.1 8.8 %collective-permute-done.20.refs_2_ = f32[128,256]{1,0:T(8,128)S(1)} collective-permute-done((f32[128,256]{1,0:T(8,128)S(1)}, f32[128,256]{1,0:T(8,128)S(1)}, u32[]{:S(2)}, u32[]{:S(2)}) %collective-permute-start.20) | collective-permute-done | bytes 131104 | tf_op jit(solution)/shard_map/onward/ppermute | solution.py:110
  54.9 0.7 %gather.1 = f32[256,256]{1,0:T(8,128)} custom-call(f32[8,128]{1,0:T(8,128)S(1)} %get-tuple-element.87.refs_0_, f32[128,256]{1,0:T(8,128)S(1)} %collective-permute-done.19.refs_1_, f32[128,256]{1,0:T(8,128)S(1)} %collective-permute-done.20.refs_2_), custom_call_target="tpu_custom_call" | custom-call | flops 8 | bytes 262144 | tf_op jit(solution)/shard_map/gather/pallas_call | solution.py:63
  (11 shorter events, 0.1 us)
Async XLA Ops:
  2.8 4.3 %collective-permute-start = (f32[128,256]{1,0:T(8,128)S(1)}, f32[128,256]{1,0:T(8,128)S(1)}, u32[]{:S(2)}, u32[]{:S(2)}) collective-permute-start(f32[128,256]{1,0:T(8,128)S(1)} %get-tuple-element.50), channel_id=1, source_target_pairs={{0,1},{1,0},{2,3},{3,2},{4,5},{5,4},{6,7},{7,6},{8,9},{9,8},{10,11... | collective-permute-start | bytes 393224 | tf_op jit(solution)/shard_map/core_swap/ppermute | solution.py:101
  6.1 1.3 %collective-permute-start.1 = (f32[128,256]{1,0:T(8,128)S(1)}, f32[128,256]{1,0:T(8,128)S(1)}, u32[]{:S(2)}, u32[]{:S(2)}) collective-permute-start(f32[128,256]{1,0:T(8,128)S(1)} %get-tuple-element.52), channel_id=1, source_target_pairs={{0,1},{1,0},{2,3},{3,2},{4,5},{5,4},{6,7},{7,6},{8,9},{9,8},{10,11... | collective-permute-start | bytes 393224 | tf_op jit(solution)/shard_map/core_swap/ppermute | solution.py:101
  7.2 8.7 %collective-permute-start.3 = (f32[128,256]{1,0:T(8,128)S(1)}, f32[128,256]{1,0:T(8,128)S(1)}, u32[]{:S(2)}, u32[]{:S(2)}) collective-permute-start(f32[128,256]{1,0:T(8,128)S(1)} %join.2.refs_0_), channel_id=1, source_target_pairs={{0,2},{1,3},{2,0},{3,1},{4,6},{5,7},{6,4},{7,5},{8,10},{9,11},{10,... | collective-permute-start | bytes 393224 | tf_op jit(solution)/shard_map/chip_swap/ppermute | solution.py:101
  7.5 9.3 %collective-permute-start.9 = (f32[128,256]{1,0:T(8,128)S(1)}, f32[128,256]{1,0:T(8,128)S(1)}, u32[]{:S(2)}, u32[]{:S(2)}) collective-permute-start(f32[128,256]{1,0:T(8,128)S(1)} %join.3.refs_1_), channel_id=1, source_target_pairs={{0,2},{1,3},{2,0},{3,1},{4,6},{5,7},{6,4},{7,5},{8,10},{9,11},{10,... | collective-permute-start | bytes 393224 | tf_op jit(solution)/shard_map/chip_swap/ppermute | solution.py:101
  10.7 5.1 %collective-permute-start.2 = (f32[128,256]{1,0:T(8,128)S(1)}, f32[128,256]{1,0:T(8,128)S(1)}, u32[]{:S(2)}, u32[]{:S(2)}) collective-permute-start(f32[128,256]{1,0:T(8,128)S(1)} %get-tuple-element.53.refs_0_), channel_id=1, source_target_pairs={{0,1},{1,0},{2,3},{3,2},{4,5},{5,4},{6,7},{7,6},{8,9},{9,8},{10,11... | collective-permute-start | bytes 393224 | tf_op jit(solution)/shard_map/core_swap/ppermute | solution.py:101
  11.7 4.6 %collective-permute-start.8 = (f32[128,256]{1,0:T(8,128)S(1)}, f32[128,256]{1,0:T(8,128)S(1)}, u32[]{:S(2)}, u32[]{:S(2)}) collective-permute-start(f32[128,256]{1,0:T(8,128)S(1)} %get-tuple-element.54.refs_1_), channel_id=1, source_target_pairs={{0,1},{1,0},{2,3},{3,2},{4,5},{5,4},{6,7},{7,6},{8,9},{9,8},{10,11... | collective-permute-start | bytes 393224 | tf_op jit(solution)/shard_map/core_swap/ppermute | solution.py:101
  15.0 16.2 %collective-permute-start.5 = (f32[256,256]{1,0:T(8,128)S(1)}, f32[256,256]{1,0:T(8,128)S(1)}, u32[]{:S(2)}, u32[]{:S(2)}) collective-permute-start(f32[256,256]{1,0:T(8,128)S(1)} %user_step.1.refs_0_.refs_2_.refs_3_.refs_4_.refs_5_), channel_id=1, source_target_pairs={{0,1},{1,0},{2,3},{3,2},{4,5},{5,4},{6,7},{7,6},{8,9},{9,8},{10,11... | collective-permute-start | bytes 786440 | tf_op jit(solution)/shard_map/core_swap/ppermute | solution.py:101
  15.8 15.4 %collective-permute-start.6 = (f32[512,256]{1,0:T(8,128)S(1)}, f32[512,256]{1,0:T(8,128)S(1)}, u32[]{:S(2)}, u32[]{:S(2)}) collective-permute-start(f32[512,256]{1,0:T(8,128)S(1)} %get-tuple-element.63.refs_0_), channel_id=1, source_target_pairs={{0,1},{1,0},{2,3},{3,2},{4,5},{5,4},{6,7},{7,6},{8,9},{9,8},{10,11... | collective-permute-start | bytes 1572872 | tf_op jit(solution)/shard_map/core_swap/ppermute | solution.py:101
  15.9 15.3 %collective-permute-start.7 = (f32[512,256]{1,0:T(8,128)S(1)}, f32[512,256]{1,0:T(8,128)S(1)}, u32[]{:S(2)}, u32[]{:S(2)}) collective-permute-start(f32[512,256]{1,0:T(8,128)S(1)} %get-tuple-element.67), channel_id=1, source_target_pairs={{0,1},{1,0},{2,3},{3,2},{4,5},{5,4},{6,7},{7,6},{8,9},{9,8},{10,11... | collective-permute-start | bytes 1572872 | tf_op jit(solution)/shard_map/core_swap/ppermute | solution.py:101
  16.3 12.0 %collective-permute-start.4 = (f32[128,256]{1,0:T(8,128)S(1)}, f32[128,256]{1,0:T(8,128)S(1)}, u32[]{:S(2)}, u32[]{:S(2)}) collective-permute-start(f32[128,256]{1,0:T(8,128)S(1)} %add_scaled.4.refs_1_), channel_id=1, source_target_pairs={{0,6},{1,7},{2,4},{3,5},{4,10},{5,11},{6,8},{7,9},{8,14},{9,15},{1... | collective-permute-start | bytes 393224 | tf_op jit(solution)/shard_map/onward/ppermute | solution.py:110
  16.9 14.3 %collective-permute-start.10 = (f32[128,256]{1,0:T(8,128)S(1)}, f32[128,256]{1,0:T(8,128)S(1)}, u32[]{:S(2)}, u32[]{:S(2)}) collective-permute-start(f32[128,256]{1,0:T(8,128)S(1)} %add_scaled.5), channel_id=1, source_target_pairs={{0,6},{1,7},{2,4},{3,5},{4,10},{5,11},{6,8},{7,9},{8,14},{9,15},{1... | collective-permute-start | bytes 393224 | tf_op jit(solution)/shard_map/onward/ppermute | solution.py:110
  28.3 6.4 %collective-permute-start.11 = (f32[128,256]{1,0:T(8,128)S(1)}, f32[128,256]{1,0:T(8,128)S(1)}, u32[]{:S(2)}, u32[]{:S(2)}) collective-permute-start(f32[128,256]{1,0:T(8,128)S(1)} %collective-permute-done.4.refs_1_.refs_9_), channel_id=1, source_target_pairs={{0,2},{1,3},{2,0},{3,1},{4,6},{5,7},{6,4},{7,5},{8,10},{9,11},{10,... | collective-permute-start | bytes 393224 | tf_op jit(solution)/shard_map/chip_swap/ppermute | solution.py:101
  31.2 9.9 %collective-permute-start.13 = (f32[128,256]{1,0:T(8,128)S(1)}, f32[128,256]{1,0:T(8,128)S(1)}, u32[]{:S(2)}, u32[]{:S(2)}) collective-permute-start(f32[128,256]{1,0:T(8,128)S(1)} %collective-permute-done.10.refs_2_.refs_12_), channel_id=1, source_target_pairs={{0,2},{1,3},{2,0},{3,1},{4,6},{5,7},{6,4},{7,5},{8,10},{9,11},{10,... | collective-permute-start | bytes 393224 | tf_op jit(solution)/shard_map/chip_swap/ppermute | solution.py:101
  32.1 6.3 %collective-permute-start.12 = (f32[128,256]{1,0:T(8,128)S(1)}, f32[128,256]{1,0:T(8,128)S(1)}, u32[]{:S(2)}, u32[]{:S(2)}) collective-permute-start(f32[128,256]{1,0:T(8,128)S(1)} %get-tuple-element.68.refs_0_), channel_id=1, source_target_pairs={{0,2},{1,3},{2,0},{3,1},{4,6},{5,7},{6,4},{7,5},{8,10},{9,11},{10,... | collective-permute-start | bytes 393224 | tf_op jit(solution)/shard_map/chip_swap/ppermute | solution.py:101
  34.6 7.4 %collective-permute-start.14 = (f32[128,256]{1,0:T(8,128)S(1)}, f32[128,256]{1,0:T(8,128)S(1)}, u32[]{:S(2)}, u32[]{:S(2)}) collective-permute-start(f32[128,256]{1,0:T(8,128)S(1)} %get-tuple-element.70.refs_0_), channel_id=1, source_target_pairs={{0,2},{1,3},{2,0},{3,1},{4,6},{5,7},{6,4},{7,5},{8,10},{9,11},{10,... | collective-permute-start | bytes 393224 | tf_op jit(solution)/shard_map/chip_swap/ppermute | solution.py:101
  35.6 6.5 %collective-permute-start.17 = (f32[128,256]{1,0:T(8,128)S(1)}, f32[128,256]{1,0:T(8,128)S(1)}, u32[]{:S(2)}, u32[]{:S(2)}) collective-permute-start(f32[128,256]{1,0:T(8,128)S(1)} %get-tuple-element.84), channel_id=1, source_target_pairs={{0,1},{1,0},{2,3},{3,2},{4,5},{5,4},{6,7},{7,6},{8,9},{9,8},{10,11... | collective-permute-start | bytes 393224 | tf_op jit(solution)/shard_map/core_swap/ppermute | solution.py:101
  37.3 5.0 %collective-permute-start.16 = (f32[128,256]{1,0:T(8,128)S(1)}, f32[128,256]{1,0:T(8,128)S(1)}, u32[]{:S(2)}, u32[]{:S(2)}) collective-permute-start(f32[128,256]{1,0:T(8,128)S(1)} %get-tuple-element.83), channel_id=1, source_target_pairs={{0,1},{1,0},{2,3},{3,2},{4,5},{5,4},{6,7},{7,6},{8,9},{9,8},{10,11... | collective-permute-start | bytes 393224 | tf_op jit(solution)/shard_map/core_swap/ppermute | solution.py:101
  38.4 3.9 %collective-permute-start.15 = (f32[128,256]{1,0:T(8,128)S(1)}, f32[128,256]{1,0:T(8,128)S(1)}, u32[]{:S(2)}, u32[]{:S(2)}) collective-permute-start(f32[128,256]{1,0:T(8,128)S(1)} %get-tuple-element.82), channel_id=1, source_target_pairs={{0,1},{1,0},{2,3},{3,2},{4,5},{5,4},{6,7},{7,6},{8,9},{9,8},{10,11... | collective-permute-start | bytes 393224 | tf_op jit(solution)/shard_map/core_swap/ppermute | solution.py:101
  42.0 1.4 %collective-permute-start.18 = (f32[128,256]{1,0:T(8,128)S(1)}, f32[128,256]{1,0:T(8,128)S(1)}, u32[]{:S(2)}, u32[]{:S(2)}) collective-permute-start(f32[128,256]{1,0:T(8,128)S(1)} %get-tuple-element.85), channel_id=1, source_target_pairs={{0,1},{1,0},{2,3},{3,2},{4,5},{5,4},{6,7},{7,6},{8,9},{9,8},{10,11... | collective-permute-start | bytes 393224 | tf_op jit(solution)/shard_map/core_swap/ppermute | solution.py:101
  42.1 12.8 %collective-permute-start.19 = (f32[128,256]{1,0:T(8,128)S(1)}, f32[128,256]{1,0:T(8,128)S(1)}, u32[]{:S(2)}, u32[]{:S(2)}) collective-permute-start(f32[128,256]{1,0:T(8,128)S(1)} %add_scaled.6.refs_1_.refs_0_), channel_id=1, source_target_pairs={{0,6},{1,7},{2,4},{3,5},{4,10},{5,11},{6,8},{7,9},{8,14},{9,15},{1... | collective-permute-start | bytes 393224 | tf_op jit(solution)/shard_map/onward/ppermute | solution.py:110
  42.2 12.7 %collective-permute-start.20 = (f32[128,256]{1,0:T(8,128)S(1)}, f32[128,256]{1,0:T(8,128)S(1)}, u32[]{:S(2)}, u32[]{:S(2)}) collective-permute-start(f32[128,256]{1,0:T(8,128)S(1)} %add_scaled.7.refs_1_), channel_id=1, source_target_pairs={{0,6},{1,7},{2,4},{3,5},{4,10},{5,11},{6,8},{7,9},{8,14},{9,15},{1... | collective-permute-start | bytes 393224 | tf_op jit(solution)/shard_map/onward/ppermute | solution.py:110

commit v3 on v2

--- a/solution.py
+++ b/solution.py
@@ -19,6 +19,9 @@
 THIRD = 64
 SHORT = 4
 MOVE = 64
+FAR = (2, 8)
+LAST = 6
+FIN = 8
 VMEM_LIMIT = 16 * 1024 * 1024
 
 NN = (((1,), (0,)), ((), ()))
@@ -214,103 +217,103 @@
     from_chip = [swap(value, 2) for value in to_chip]
 
     def third(place_ref, rating_ref, weight_ref, users_ref, items_ref, noise_hbm,
+              rating_hbm, weight_hbm, noise_users_hbm,
+              rating_out, weight_out, noise_out, noise_users_out,
               high_3, low_3, high_2, low_2, *rest):
         outs, bases, (noise, sems) = rest[:CHUNKS], rest[CHUNKS : 2 * CHUNKS], rest[2 * CHUNKS :]
-        [copy] = fetch([(noise_hbm.at[0, rows_of(place_ref, 2), :], noise)], sems)
+        copies = fetch(
+            [(noise_hbm.at[0, rows_of(place_ref, 2), :], noise),
+             (rating_hbm.at[1], rating_out), (weight_hbm.at[1], weight_out),
+             (noise_hbm.at[1, rows_of(place_ref, 2), :], noise_out),
+             (noise_users_hbm.at[0], noise_users_out)],
+            sems,
+        )
         args = (rating_ref, weight_ref, users_ref, items_ref)
         put(quarter_terms(place_ref, 3, *args, high_3, low_3), outs)
         total = quarter_terms(place_ref, 2, *args, high_2, low_2)
-        copy.wait()
+        for copy in copies:
+            copy.wait()
         put(stepped(items_ref[rows_of(place_ref, 2), :], total, noise[...]), bases)
 
-    *rest, = call(
+    tiles_shape = (ratings.shape[1:], bf16)
+    rating_in, weight_in, noise_1, noise_users_0, *rest = call(
         third,
-        [(square, bf16)] * 4 + [(piece, f32)] * (2 * CHUNKS),
-        [place] + stage_0 + [(DISTANT, noise_items)],
+        [tiles_shape] * 2 + [((quarter, rank), f32), (users.shape, f32)]
+        + [(square, bf16)] * 4 + [(piece, f32)] * (2 * CHUNKS),
+        [place] + stage_0
+        + [(DISTANT, v) for v in (noise_items, ratings, weights, noise_users)],
         THIRD * unit,
-        [pltpu.VMEM((quarter, rank), f32), pltpu.SemaphoreType.DMA((1,))],
+        [pltpu.VMEM((quarter, rank), f32), pltpu.SemaphoreType.DMA((5,))],
         after=to_chip,
     )
     errors_3, errors_2, to_sibling, base = rest[:2], rest[2:4], rest[4 : 4 + CHUNKS], rest[4 + CHUNKS :]
     from_sibling = [swap(value, 1) for value in to_sibling]
 
-    def user_step(place_ref, users_ref, items_ref, noise_hbm, *rest):
-        errors, (users_out, noise, sems) = rest[:-3], rest[-3:]
-        [copy] = fetch([(noise_hbm.at[0], noise)], sems)
+    flat = (columns * TILE, owned)
+    half = (columns * TILE // 2, owned)
+
+    def layout(place_ref, index_hbm, count_hbm, rating_ref, weight_ref,
+               rating_out, weight_out, rating_send, weight_send, index_ref, count_ref, sems):
+        copies = fetch([(index_hbm, index_ref), (count_hbm, count_ref)], sems)
+        rating_out[...] = jnp.zeros_like(rating_out)
+        weight_out[...] = jnp.zeros_like(weight_out)
+        for copy in copies:
+            copy.wait()
+        for slot in range(slots):
+
+            @pl.when(slot < count_ref[1])
+            def _(slot=slot):
+                tile = index_ref[1, slot]
+                at = pl.ds(pl.multiple_of(lax.rem(tile, columns) * TILE, TILE), TILE)
+                turned = (rating_ref[slot].astype(f32).T, weight_ref[slot].astype(f32).T)
+                for row in range(owned // TILE):
+
+                    @pl.when(lax.div(tile, columns) == row)
+                    def _(row=row):
+                        across = slice(row * TILE, (row + 1) * TILE)
+                        rating_out[at, across] = turned[0]
+                        weight_out[at, across] = turned[1]
+
+        for n, flip in enumerate((1, 3)):
+            rows = slice(n * quarter, (n + 1) * quarter)
+            rating_send[rows, :] = rating_out[rows_of(place_ref, flip), :]
+            weight_send[rows, :] = weight_out[rows_of(place_ref, flip), :]
+    rating_1, weight_1, rating_send, weight_send = call(
+        layout,
+        [(flat, f32)] * 2 + [(half, f32)] * 2,
+        [place] + tables[:2] + [local(rating_in), local(weight_in)],
+        SHORT * unit,
+        landing[:2] + [pltpu.SemaphoreType.DMA((2,))],
+        after=to_sibling,
+    )
+    rating_s, weight_s = swap(rating_send, 1), swap(weight_send, 1)
+
+    def move(k, after):
+        terms = [local(v) for v in (base[k], from_sibling[k], from_chip[k])]
+        return call(add_scaled, [(piece, f32)], terms, MOVE * unit, after=after)
+
+    moved = move(0, [rating_send])
+
+    def user_step(place_ref, users_ref, items_ref, noise_ref, *rest):
+        errors, users_out = rest[:-1], rest[-1]
         total = jnp.zeros((owned, rank), f32)
         for flip in range(n_grp):
             item_halves = halves(items_ref[rows_of(place_ref, flip), :])
             kept = (errors[2 * flip][...], errors[2 * flip + 1][...])
             total = total + product(kept, item_halves, TN)
-        copy.wait()
-        users_out[...] = stepped(users_ref[...], total, noise[...])
+        users_out[...] = stepped(users_ref[...], total, noise_ref[...])
 
     [users_1] = call(
         user_step,
         [(users.shape, f32)],
-        [place, local(users_0), local(items_0), (DISTANT, noise_users)]
+        [place, local(users_0), local(items_0), local(noise_users_0)]
         + [local(v) for v in errors_0 + errors_1 + errors_2 + errors_3],
         SHORT * unit,
-        [pltpu.VMEM(users.shape, f32), pltpu.SemaphoreType.DMA((1,))],
-        after=to_sibling,
+        after=moved,
     )
     users_s = swap(users_1, 1)
 
-    flat = (columns * TILE, owned)
-    half = (columns * TILE // 2, owned)
-
-    def layout(place_ref, index_hbm, count_hbm, rating_hbm, weight_hbm, noise_hbm,
-               rating_out, weight_out, rating_send, weight_send, noise_out,
-               index_ref, count_ref, rating_in, weight_in, sems):
-        copies = fetch(
-            [(index_hbm, index_ref), (count_hbm, count_ref),
-             (rating_hbm.at[1], rating_in), (weight_hbm.at[1], weight_in),
-             (noise_hbm.at[1, rows_of(place_ref, 2), :], noise_out)],
-            sems,
-        )
-        rating_out[...] = jnp.zeros_like(rating_out)
-        weight_out[...] = jnp.zeros_like(weight_out)
-        for copy in copies[:4]:
-            copy.wait()
-        for slot in range(slots):
-
-            @pl.when(slot < count_ref[1])
-            def _(slot=slot):
-                tile = index_ref[1, slot]
-                at = pl.ds(pl.multiple_of(lax.rem(tile, columns) * TILE, TILE), TILE)
-                turned = (rating_in[slot].astype(f32).T, weight_in[slot].astype(f32).T)
-                for row in range(owned // TILE):
-
-                    @pl.when(lax.div(tile, columns) == row)
-                    def _(row=row):
-                        across = slice(row * TILE, (row + 1) * TILE)
-                        rating_out[at, across] = turned[0]
-                        weight_out[at, across] = turned[1]
-
-        for n, flip in enumerate((1, 3)):
-            rows = slice(n * quarter, (n + 1) * quarter)
-            rating_send[rows, :] = rating_out[rows_of(place_ref, flip), :]
-            weight_send[rows, :] = weight_out[rows_of(place_ref, flip), :]
-        copies[4].wait()
-
-    rating_1, weight_1, rating_send, weight_send, noise_1 = call(
-        layout,
-        [(flat, f32)] * 2 + [(half, f32)] * 2 + [((quarter, rank), f32)],
-        [place] + tables + [(DISTANT, noise_items)],
-        SHORT * unit,
-        landing + [pltpu.SemaphoreType.DMA((5,))],
-        after=[users_1],
-    )
-    rating_s, weight_s = swap(rating_send, 1), swap(weight_send, 1)
-
-    moved = []
-    for k in range(CHUNKS):
-        [value] = call(
-            add_scaled, [(piece, f32)],
-            [local(v) for v in (base[k], from_sibling[k], from_chip[k])], MOVE * unit,
-            after=[rating_send, *moved[-1:]],
-        )
-        moved.append(value)
+    moved += move(1, [users_1])
     ahead = [onward(value) for value in moved]
 
     def late(k, slot, place_ref, items_ref, users_ref, users_s_ref, rating_ref, weight_ref,
@@ -334,10 +337,15 @@
     common = [local(v) for v in (users_1, users_s, rating_1, weight_1, rating_s, weight_s)]
     errors_shape = (chunk, owned)
     late_outs = [(errors_shape, bf16)] * 2 + [(piece, f32)] * 2
-    here = ahead
-    there = [swap(value, 2) for value in here]
+    def relay(value_ref, out):
+        out[...] = value_ref[...]
+
+    here, there = list(ahead), []
     errors_here, here_copy, sent = [], [], []
     for k in range(CHUNKS):
+        if k:
+            [here[k]] = call(relay, [(piece, f32)], [local(here[k])], 1, after=sent)
+        there.append(swap(here[k], 2))
         high, low, rows, value = call(
             functools.partial(late, k, 0), late_outs, [place, local(here[k])] + common,
             4 * unit // CHUNKS, after=sent[-1:],
@@ -350,10 +358,10 @@
     for k in range(CHUNKS):
         high, low, rows, step = call(
             functools.partial(late, k, 1), late_outs,
-            [place, local(there[k])] + common + [local(noise_1)], 4 * unit // CHUNKS,
+            [place, local(there[k])] + common + [local(noise_1)], FAR[k] * unit,
             after=[sent[-1], *finished[-1:]],
         )
-        [value] = call(add_scaled, [(piece, f32)], [local(step), local(received[k])], 1)
+        [value] = call(add_scaled, [(piece, f32)], [local(step), local(received[k])], FIN * unit)
         errors_there.append((high, low))
         there_copy.append(rows)
         finished.append(value)
@@ -390,7 +398,7 @@
         [(users.shape, f32), ((8, 128), f32)],
         [place, local(rating_1), local(weight_1), local(users_1), (DISTANT, noise_users)]
         + known + [local(v) for v in here_s + there_s],
-        6 * unit,
+        LAST * unit,
         [pltpu.VMEM(users.shape, f32), pltpu.SemaphoreType.DMA((1,))],
         after=finished,
     )

time: 55.9 us -> 52.7 us (0.943)
  waiting for transfers between devices: 23.9 us -> 17.4 us
  starting transfers between devices: 16.1 us -> 20 us
  Pallas kernels: 14.8 us -> 14.1 us
    ppermute x4, waiting for transfers between devices: 21.3 us -> 15.8 us  [onward(): return lax.ppermute(value, AXES, pairs)]
    ppermute x17, starting transfers between devices: 13.6 us -> 17.3 us  [swap(): return lax.ppermute(value, AXES, pairs)]
    ppermute x17, waiting for transfers between devices: 2.61 us -> 1.65 us  [swap(): return lax.ppermute(value, AXES, pairs)]
    pallas_call x17 -> x18, Pallas kernels: 14.8 us -> 14.1 us  [call(): pl.pallas_call(kernel, in_specs=[AFTER] * unread + [spec for spec, _ in o...]
where the time goes in v3:
time: 52.7 us; the launch traced here: 52.4 us
  starting transfers between devices  20 us (38%)
  waiting for transfers between devices  17.4 us (33%)
  Pallas kernels  14.1 us (27%)
  between operations  0.83 us (2%)
    ppermute x17, starting transfers between devices, swap(): return lax.ppermute(value, AXES, pairs)  17.3 us
    ppermute x4, waiting for transfers between devices, onward(): return lax.ppermute(value, AXES, pairs)  15.8 us
    pallas_call x18, Pallas kernels, call(): pl.pallas_call(kernel, in_specs=[AFTER] * unread + [spec for spec, _ in o...  14.1 us
    ppermute x4, starting transfers between devices, onward(): return lax.ppermute(value, AXES, pairs)  2.72 us
    ppermute x17, waiting for transfers between devices, swap(): return lax.ppermute(value, AXES, pairs)  1.65 us
  transfers between devices with their start and end apart: 21, of which 7 were waited for; matrix products, arithmetic and copies ran while one was open for 0% of the time, Pallas kernels for 21%

profile of v3, /device:TPU:1, one launch (start us, length us, event | category | flops | bytes accessed | tf_op | source)
XLA Modules:
  0.0 52.4 jit_solution(14123207045807478504)
XLA Ops:
  0.6 2.2 %first.1 = (bf16[8,256,128]{2,1,0:T(8,128)(2,1)S(1)}, bf16[8,256,128]{2,1,0:T(8,128)(2,1)S(1)}, f32[256,256]{1,0:T(8,128)S(1)}, f32[1024,256]{1,0:T(8,128)S(1)},...) custom-call(s32[1]{0:T(128)} %bitcast.refs_0_.refs_2_.refs_1_, ...), custom_call_target="tpu_custom_call" | custom-call | flops 1610612736 | bytes 262144 | tf_op jit(solution)/shard_map/first/pallas_call | solution.py:66
  2.8 3.3 %collective-permute-start = (f32[128,256]{1,0:T(8,128)S(1)}, f32[128,256]{1,0:T(8,128)S(1)}, u32[]{:S(2)}, u32[]{:S(2)}) collective-permute-start(f32[128,256]{1,0:T(8,128)S(1)} %get-tuple-element.53), channel_id=1, source_target_pairs={{0,1},{1,0},{2,3},{3,2},{4,5},{5,4},{6,7},{7,6},{8,9},{9,8},{10,11... | collective-permute-start | bytes 393224 | tf_op jit(solution)/shard_map/core_swap/ppermute | solution.py:104
  6.1 0.1 collective-permute-start.1
  6.2 0.6 %second.1 = (bf16[256,256]{1,0:T(8,128)(2,1)S(1)}, bf16[256,256]{1,0:T(8,128)(2,1)S(1)}, f32[128,256]{1,0:T(8,128)S(1)}, f32[128,256]{1,0:T(8,128)S(1)}) custom-call(s32[1]{0:T(128)} %bitcast.refs_0_.refs_2_.refs_1_, bf16[8,256,128]{2,1,0:T(8,128)(2,1)S(1)} %get-tuple-element.48.refs_1_.refs_3_, bf16[8,256,128]{2,1,0:T(8,128)(2,1)S(1)} %get-tuple-element.49.refs_2_.refs_4_, ...), custom_call_target="tpu_custom_call" | custom-call | flops 1610612736 | bytes 262144 | tf_op jit(solution)/shard_map/second/pallas_call | solution.py:66
  6.9 0.2 collective-permute-done.refs_1_
  7.2 0.1 collective-permute-start.3
  7.3 0.2 collective-permute-done.1.refs_2_
  7.5 1.3 %collective-permute-start.9 = (f32[128,256]{1,0:T(8,128)S(1)}, f32[128,256]{1,0:T(8,128)S(1)}, u32[]{:S(2)}, u32[]{:S(2)}) collective-permute-start(f32[128,256]{1,0:T(8,128)S(1)} %join.3.refs_1_), channel_id=1, source_target_pairs={{0,2},{1,3},{2,0},{3,1},{4,6},{5,7},{6,4},{7,5},{8,10},{9,11},{10,... | collective-permute-start | bytes 393224 | tf_op jit(solution)/shard_map/chip_swap/ppermute | solution.py:104
  8.8 2.2 %third.1 = (bf16[8,128,128]{2,1,0:T(8,128)(2,1)S(1)}, bf16[8,128,128]{2,1,0:T(8,128)(2,1)S(1)}, f32[256,256]{1,0:T(8,128)S(1)}, f32[256,256]{1,0:T(8,128)S(1)}, ...) custom-call(f32[128,256]{1,0:T(8,128)S(1)} %join.2.refs_0_, ...), custom_call_target="tpu_custom_call" | custom-call | flops 51539607552 | bytes 262144 | tf_op jit(solution)/shard_map/third/pallas_call | solution.py:66
  11.1 1.0 %collective-permute-start.2 = (f32[128,256]{1,0:T(8,128)S(1)}, f32[128,256]{1,0:T(8,128)S(1)}, u32[]{:S(2)}, u32[]{:S(2)}) collective-permute-start(f32[128,256]{1,0:T(8,128)S(1)} %get-tuple-element.56.refs_0_), channel_id=1, source_target_pairs={{0,1},{1,0},{2,3},{3,2},{4,5},{5,4},{6,7},{7,6},{8,9},{9,8},{10,11... | collective-permute-start | bytes 393224 | tf_op jit(solution)/shard_map/core_swap/ppermute | solution.py:104
  12.1 0.1 collective-permute-start.8
  12.2 1.4 %layout.1 = (f32[1024,256]{1,0:T(8,128)S(1)}, f32[1024,256]{1,0:T(8,128)S(1)}, f32[512,256]{1,0:T(8,128)S(1)}, f32[512,256]{1,0:T(8,128)S(1)}) custom-call(f32[128,256]{1,0:T(8,128)S(1)} %get-tuple-element.56.refs_0_, f32[128,256]{1,0:T(8,128)S(1)} %get-tuple-element.57.refs_1_, s32[1]{0:T(128)} %bitcast.refs_0_.refs_2_.refs_1_, s32[2,8]{1,0:T(2,128)} %refs_3_.3, ...), custom_call_target="tpu_custom_call" | custom-call | flops 3221225472 | bytes 262144 | tf_op jit(solution)/shard_map/layout/pallas_call | solution.py:66
  13.5 0.5 collective-permute-start.6
  14.0 0.0 collective-permute-done.2.refs_2_
  14.0 0.1 collective-permute-start.7
  14.1 0.0 collective-permute-done.3.refs_3_
  14.2 1.0 %collective-permute-start.4 = (f32[128,256]{1,0:T(8,128)S(1)}, f32[128,256]{1,0:T(8,128)S(1)}, u32[]{:S(2)}, u32[]{:S(2)}) collective-permute-start(f32[128,256]{1,0:T(8,128)S(1)} %add_scaled.4.refs_0_), channel_id=1, source_target_pairs={{0,6},{1,7},{2,4},{3,5},{4,10},{5,11},{6,8},{7,9},{8,14},{9,15},{1... | collective-permute-start | bytes 393224 | tf_op jit(solution)/shard_map/onward/ppermute | solution.py:113
  15.2 0.7 %user_step.1.refs_2_.refs_0_.refs_3_.refs_4_.refs_5_ = f32[256,256]{1,0:T(8,128)S(1)} custom-call(f32[128,256]{1,0:T(8,128)S(1)} %add_scaled.4.refs_0_, s32[1]{0:T(128)} %bitcast.refs_0_.refs_2_.refs_1_, f32[256,256]{1,0:T(8,128)S(1)} %get-tuple-element.50.refs_3_.refs_5_.refs_2_, f32[1024,256]{1,0:T(8,128)S(1)} %get-tuple-element.51.refs_4_.refs_6_.refs_3_, ...), custom_call_target="tpu_custom_call" | custom-call | flops 3221225472 | bytes 262144 | tf_op jit(solution)/shard_map/user_step/pallas_call | solution.py:66
  15.9 0.0 collective-permute-done.8.refs_2_
  15.9 0.8 %collective-permute-start.5 = (f32[256,256]{1,0:T(8,128)S(1)}, f32[256,256]{1,0:T(8,128)S(1)}, u32[]{:S(2)}, u32[]{:S(2)}) collective-permute-start(f32[256,256]{1,0:T(8,128)S(1)} %user_step.1.refs_2_.refs_0_.refs_3_.refs_4_.refs_5_), channel_id=1, source_target_pairs={{0,1},{1,0},{2,3},{3,2},{4,5},{5,4},{6,7},{7,6},{8,9},{9,8},{10,11... | collective-permute-start | bytes 786440 | tf_op jit(solution)/shard_map/core_swap/ppermute | solution.py:104
  16.6 0.0 collective-permute-done.9.refs_3_
  16.7 1.5 %collective-permute-start.10 = (f32[128,256]{1,0:T(8,128)S(1)}, f32[128,256]{1,0:T(8,128)S(1)}, u32[]{:S(2)}, u32[]{:S(2)}) collective-permute-start(f32[128,256]{1,0:T(8,128)S(1)} %add_scaled.5), channel_id=1, source_target_pairs={{0,6},{1,7},{2,4},{3,5},{4,10},{5,11},{6,8},{7,9},{8,14},{9,15},{1... | collective-permute-start | bytes 393224 | tf_op jit(solution)/shard_map/onward/ppermute | solution.py:113
  18.2 8.0 %collective-permute-done.4.refs_1_.refs_9_ = f32[128,256]{1,0:T(8,128)S(1)} collective-permute-done((f32[128,256]{1,0:T(8,128)S(1)}, f32[128,256]{1,0:T(8,128)S(1)}, u32[]{:S(2)}, u32[]{:S(2)}) %collective-permute-start.4) | collective-permute-done | bytes 131104 | tf_op jit(solution)/shard_map/onward/ppermute | solution.py:113
  26.3 0.0 collective-permute-start.11
  26.3 0.0 collective-permute-done.5.refs_3_.refs_4_.refs_5_
  26.3 0.0 collective-permute-done.6.refs_6_.refs_7_.refs_8_
  26.3 0.9 %late.4 = (bf16[128,256]{1,0:T(8,128)(2,1)S(1)}, bf16[128,256]{1,0:T(8,128)(2,1)S(1)}, f32[128,256]{1,0:T(8,128)S(1)}, f32[128,256]{1,0:T(8,128)S(1)}) custom-call(s32[1]{0:T(128)} %bitcast.refs_0_.refs_2_.refs_1_, f32[128,256]{1,0:T(8,128)S(1)} %collective-permute-done.4.refs_1_.refs_9_, f32[256,256]{1,0:T(8,128)S(1)} %user_step.1.refs_2_.refs_0_.refs_3_.refs_4_.refs_5_, ...), custom_call_target="tpu_custom_call" | custom-call | flops 1610612736 | bytes 262144 | tf_op jit(solution)/shard_map/late/pallas_call | solution.py:66
  27.1 1.5 %collective-permute-start.12 = (f32[128,256]{1,0:T(8,128)S(1)}, f32[128,256]{1,0:T(8,128)S(1)}, u32[]{:S(2)}, u32[]{:S(2)}) collective-permute-start(f32[128,256]{1,0:T(8,128)S(1)} %get-tuple-element.74.refs_0_), channel_id=1, source_target_pairs={{0,2},{1,3},{2,0},{3,1},{4,6},{5,7},{6,4},{7,5},{8,10},{9,11},{10,... | collective-permute-start | bytes 393224 | tf_op jit(solution)/shard_map/chip_swap/ppermute | solution.py:104
  28.7 0.4 collective-permute-done.10.refs_1_
  29.1 0.3 collective-permute-start.13
  29.4 0.9 %late.5 = (bf16[128,256]{1,0:T(8,128)(2,1)S(1)}, bf16[128,256]{1,0:T(8,128)(2,1)S(1)}, f32[128,256]{1,0:T(8,128)S(1)}, f32[128,256]{1,0:T(8,128)S(1)}) custom-call(f32[128,256]{1,0:T(8,128)S(1)} %get-tuple-element.74.refs_0_, s32[1]{0:T(128)} %bitcast.refs_0_.refs_2_.refs_1_, f32[128,256]{1,0:T(8,128)S(1)} %relay.1.refs_2_.refs_12_, ...), custom_call_target="tpu_custom_call" | custom-call | flops 1610612736 | bytes 262144 | tf_op jit(solution)/shard_map/late/pallas_call | solution.py:66
  30.2 1.5 %collective-permute-start.14 = (f32[128,256]{1,0:T(8,128)S(1)}, f32[128,256]{1,0:T(8,128)S(1)}, u32[]{:S(2)}, u32[]{:S(2)}) collective-permute-start(f32[128,256]{1,0:T(8,128)S(1)} %get-tuple-element.76.refs_0_), channel_id=1, source_target_pairs={{0,2},{1,3},{2,0},{3,1},{4,6},{5,7},{6,4},{7,5},{8,10},{9,11},{10,... | collective-permute-start | bytes 393224 | tf_op jit(solution)/shard_map/chip_swap/ppermute | solution.py:104
  31.8 0.0 collective-permute-done.11.refs_2_.refs_15_
  31.8 0.9 %late.6 = (bf16[128,256]{1,0:T(8,128)(2,1)S(1)}, bf16[128,256]{1,0:T(8,128)(2,1)S(1)}, f32[128,256]{1,0:T(8,128)S(1)}, f32[128,256]{1,0:T(8,128)S(1)}) custom-call(f32[128,256]{1,0:T(8,128)S(1)} %get-tuple-element.76.refs_0_, s32[1]{0:T(128)} %bitcast.refs_0_.refs_2_.refs_1_, f32[128,256]{1,0:T(8,128)S(1)} %collective-permute-done.11.refs_2_.refs_15_, ...), custom_call_target="tpu_custom_call" | custom-call | flops 1610612736 | bytes 262144 | tf_op jit(solution)/shard_map/late/pallas_call | solution.py:66
  32.6 2.5 %collective-permute-start.17 = (f32[128,256]{1,0:T(8,128)S(1)}, f32[128,256]{1,0:T(8,128)S(1)}, u32[]{:S(2)}, u32[]{:S(2)}) collective-permute-start(f32[128,256]{1,0:T(8,128)S(1)} %get-tuple-element.90), channel_id=1, source_target_pairs={{0,1},{1,0},{2,3},{3,2},{4,5},{5,4},{6,7},{7,6},{8,9},{9,8},{10,11... | collective-permute-start | bytes 393224 | tf_op jit(solution)/shard_map/core_swap/ppermute | solution.py:104
  35.1 0.1 collective-permute-start.16
  35.2 1.7 %collective-permute-start.15 = (f32[128,256]{1,0:T(8,128)S(1)}, f32[128,256]{1,0:T(8,128)S(1)}, u32[]{:S(2)}, u32[]{:S(2)}) collective-permute-start(f32[128,256]{1,0:T(8,128)S(1)} %get-tuple-element.88), channel_id=1, source_target_pairs={{0,1},{1,0},{2,3},{3,2},{4,5},{5,4},{6,7},{7,6},{8,9},{9,8},{10,11... | collective-permute-start | bytes 393224 | tf_op jit(solution)/shard_map/core_swap/ppermute | solution.py:104
  37.0 0.0 collective-permute-done.13.refs_3_.refs_18_
  37.0 0.1 collective-permute-start.19
  37.1 0.9 %late.7 = (bf16[128,256]{1,0:T(8,128)(2,1)S(1)}, bf16[128,256]{1,0:T(8,128)(2,1)S(1)}, f32[128,256]{1,0:T(8,128)S(1)}, f32[128,256]{1,0:T(8,128)S(1)}) custom-call(f32[128,256]{1,0:T(8,128)S(1)} %get-tuple-element.76.refs_0_, f32[128,256]{1,0:T(8,128)S(1)} %add_scaled.6.refs_1_.refs_0_, s32[1]{0:T(128)} %bitcast.refs_0_.refs_2_.refs_1_, ...), custom_call_target="tpu_custom_call" | custom-call | flops 6442450944 | bytes 262144 | tf_op jit(solution)/shard_map/late/pallas_call | solution.py:66
  37.9 0.3 collective-permute-done.14.refs_1_
  38.2 2.4 %collective-permute-start.18 = (f32[128,256]{1,0:T(8,128)S(1)}, f32[128,256]{1,0:T(8,128)S(1)}, u32[]{:S(2)}, u32[]{:S(2)}) collective-permute-start(f32[128,256]{1,0:T(8,128)S(1)} %get-tuple-element.91), channel_id=1, source_target_pairs={{0,1},{1,0},{2,3},{3,2},{4,5},{5,4},{6,7},{7,6},{8,9},{9,8},{10,11... | collective-permute-start | bytes 393224 | tf_op jit(solution)/shard_map/core_swap/ppermute | solution.py:104
  40.6 0.1 collective-permute-start.20
  40.7 0.8 %collective-permute-done.18.refs_22_ = f32[128,256]{1,0:T(8,128)S(1)} collective-permute-done((f32[128,256]{1,0:T(8,128)S(1)}, f32[128,256]{1,0:T(8,128)S(1)}, u32[]{:S(2)}, u32[]{:S(2)}) %collective-permute-start.18) | collective-permute-done | bytes 131104 | tf_op jit(solution)/shard_map/core_swap/ppermute | solution.py:104
  41.6 2.7 %last.1 = (f32[256,256]{1,0:T(8,128)}, f32[8,128]{1,0:T(8,128)S(1)}) custom-call(f32[128,256]{1,0:T(8,128)S(1)} %add_scaled.6.refs_1_.refs_0_, f32[128,256]{1,0:T(8,128)S(1)} %add_scaled.7.refs_1_, s32[1]{0:T(128)} %bitcast.refs_0_.refs_2_.refs_1_, f32[1024,256]{1,0:T(8,128)S(1)} %get-tuple-element.71.refs_4_.refs_5_.refs_6_.refs_3_, ...), custom_call_target="tpu_custom_call" | custom-call | flops 4831838208 | bytes 262144 | tf_op jit(solution)/shard_map/last/pallas_call | solution.py:66
  44.3 7.4 %collective-permute-done.20.refs_2_ = f32[128,256]{1,0:T(8,128)S(1)} collective-permute-done((f32[128,256]{1,0:T(8,128)S(1)}, f32[128,256]{1,0:T(8,128)S(1)}, u32[]{:S(2)}, u32[]{:S(2)}) %collective-permute-start.20) | collective-permute-done | bytes 131104 | tf_op jit(solution)/shard_map/onward/ppermute | solution.py:113
  51.7 0.0 collective-permute-done.19.refs_1_
  51.7 0.7 %gather.1 = f32[256,256]{1,0:T(8,128)} custom-call(f32[8,128]{1,0:T(8,128)S(1)} %get-tuple-element.93.refs_0_, f32[128,256]{1,0:T(8,128)S(1)} %collective-permute-done.19.refs_1_, f32[128,256]{1,0:T(8,128)S(1)} %collective-permute-done.20.refs_2_), custom_call_target="tpu_custom_call" | custom-call | flops 8 | bytes 262144 | tf_op jit(solution)/shard_map/gather/pallas_call | solution.py:66
  (12 shorter events, 0.1 us)
Async XLA Ops:
  2.8 4.3 %collective-permute-start = (f32[128,256]{1,0:T(8,128)S(1)}, f32[128,256]{1,0:T(8,128)S(1)}, u32[]{:S(2)}, u32[]{:S(2)}) collective-permute-start(f32[128,256]{1,0:T(8,128)S(1)} %get-tuple-element.53), channel_id=1, source_target_pairs={{0,1},{1,0},{2,3},{3,2},{4,5},{5,4},{6,7},{7,6},{8,9},{9,8},{10,11... | collective-permute-start | bytes 393224 | tf_op jit(solution)/shard_map/core_swap/ppermute | solution.py:104
  6.1 1.3 %collective-permute-start.1 = (f32[128,256]{1,0:T(8,128)S(1)}, f32[128,256]{1,0:T(8,128)S(1)}, u32[]{:S(2)}, u32[]{:S(2)}) collective-permute-start(f32[128,256]{1,0:T(8,128)S(1)} %get-tuple-element.55), channel_id=1, source_target_pairs={{0,1},{1,0},{2,3},{3,2},{4,5},{5,4},{6,7},{7,6},{8,9},{9,8},{10,11... | collective-permute-start | bytes 393224 | tf_op jit(solution)/shard_map/core_swap/ppermute | solution.py:104
  7.2 7.0 %collective-permute-start.3 = (f32[128,256]{1,0:T(8,128)S(1)}, f32[128,256]{1,0:T(8,128)S(1)}, u32[]{:S(2)}, u32[]{:S(2)}) collective-permute-start(f32[128,256]{1,0:T(8,128)S(1)} %join.2.refs_0_), channel_id=1, source_target_pairs={{0,2},{1,3},{2,0},{3,1},{4,6},{5,7},{6,4},{7,5},{8,10},{9,11},{10,... | collective-permute-start | bytes 393224 | tf_op jit(solution)/shard_map/chip_swap/ppermute | solution.py:104
  7.5 9.1 %collective-permute-start.9 = (f32[128,256]{1,0:T(8,128)S(1)}, f32[128,256]{1,0:T(8,128)S(1)}, u32[]{:S(2)}, u32[]{:S(2)}) collective-permute-start(f32[128,256]{1,0:T(8,128)S(1)} %join.3.refs_1_), channel_id=1, source_target_pairs={{0,2},{1,3},{2,0},{3,1},{4,6},{5,7},{6,4},{7,5},{8,10},{9,11},{10,... | collective-permute-start | bytes 393224 | tf_op jit(solution)/shard_map/chip_swap/ppermute | solution.py:104
  11.1 3.0 %collective-permute-start.2 = (f32[128,256]{1,0:T(8,128)S(1)}, f32[128,256]{1,0:T(8,128)S(1)}, u32[]{:S(2)}, u32[]{:S(2)}) collective-permute-start(f32[128,256]{1,0:T(8,128)S(1)} %get-tuple-element.56.refs_0_), channel_id=1, source_target_pairs={{0,1},{1,0},{2,3},{3,2},{4,5},{5,4},{6,7},{7,6},{8,9},{9,8},{10,11... | collective-permute-start | bytes 393224 | tf_op jit(solution)/shard_map/core_swap/ppermute | solution.py:104
  12.1 3.8 %collective-permute-start.8 = (f32[128,256]{1,0:T(8,128)S(1)}, f32[128,256]{1,0:T(8,128)S(1)}, u32[]{:S(2)}, u32[]{:S(2)}) collective-permute-start(f32[128,256]{1,0:T(8,128)S(1)} %get-tuple-element.57.refs_1_), channel_id=1, source_target_pairs={{0,1},{1,0},{2,3},{3,2},{4,5},{5,4},{6,7},{7,6},{8,9},{9,8},{10,11... | collective-permute-start | bytes 393224 | tf_op jit(solution)/shard_map/core_swap/ppermute | solution.py:104
  13.5 12.7 %collective-permute-start.6 = (f32[512,256]{1,0:T(8,128)S(1)}, f32[512,256]{1,0:T(8,128)S(1)}, u32[]{:S(2)}, u32[]{:S(2)}) collective-permute-start(f32[512,256]{1,0:T(8,128)S(1)} %get-tuple-element.60.refs_0_), channel_id=1, source_target_pairs={{0,1},{1,0},{2,3},{3,2},{4,5},{5,4},{6,7},{7,6},{8,9},{9,8},{10,11... | collective-permute-start | bytes 1572872 | tf_op jit(solution)/shard_map/core_swap/ppermute | solution.py:104
  14.0 12.2 %collective-permute-start.7 = (f32[512,256]{1,0:T(8,128)S(1)}, f32[512,256]{1,0:T(8,128)S(1)}, u32[]{:S(2)}, u32[]{:S(2)}) collective-permute-start(f32[512,256]{1,0:T(8,128)S(1)} %get-tuple-element.73), channel_id=1, source_target_pairs={{0,1},{1,0},{2,3},{3,2},{4,5},{5,4},{6,7},{7,6},{8,9},{9,8},{10,11... | collective-permute-start | bytes 1572872 | tf_op jit(solution)/shard_map/core_swap/ppermute | solution.py:104
  14.2 12.1 %collective-permute-start.4 = (f32[128,256]{1,0:T(8,128)S(1)}, f32[128,256]{1,0:T(8,128)S(1)}, u32[]{:S(2)}, u32[]{:S(2)}) collective-permute-start(f32[128,256]{1,0:T(8,128)S(1)} %add_scaled.4.refs_0_), channel_id=1, source_target_pairs={{0,6},{1,7},{2,4},{3,5},{4,10},{5,11},{6,8},{7,9},{8,14},{9,15},{1... | collective-permute-start | bytes 393224 | tf_op jit(solution)/shard_map/onward/ppermute | solution.py:113
  15.9 10.4 %collective-permute-start.5 = (f32[256,256]{1,0:T(8,128)S(1)}, f32[256,256]{1,0:T(8,128)S(1)}, u32[]{:S(2)}, u32[]{:S(2)}) collective-permute-start(f32[256,256]{1,0:T(8,128)S(1)} %user_step.1.refs_2_.refs_0_.refs_3_.refs_4_.refs_5_), channel_id=1, source_target_pairs={{0,1},{1,0},{2,3},{3,2},{4,5},{5,4},{6,7},{7,6},{8,9},{9,8},{10,11... | collective-permute-start | bytes 786440 | tf_op jit(solution)/shard_map/core_swap/ppermute | solution.py:104
  16.7 12.4 %collective-permute-start.10 = (f32[128,256]{1,0:T(8,128)S(1)}, f32[128,256]{1,0:T(8,128)S(1)}, u32[]{:S(2)}, u32[]{:S(2)}) collective-permute-start(f32[128,256]{1,0:T(8,128)S(1)} %add_scaled.5), channel_id=1, source_target_pairs={{0,6},{1,7},{2,4},{3,5},{4,10},{5,11},{6,8},{7,9},{8,14},{9,15},{1... | collective-permute-start | bytes 393224 | tf_op jit(solution)/shard_map/onward/ppermute | solution.py:113
  26.3 5.5 %collective-permute-start.11 = (f32[128,256]{1,0:T(8,128)S(1)}, f32[128,256]{1,0:T(8,128)S(1)}, u32[]{:S(2)}, u32[]{:S(2)}) collective-permute-start(f32[128,256]{1,0:T(8,128)S(1)} %collective-permute-done.4.refs_1_.refs_9_), channel_id=1, source_target_pairs={{0,2},{1,3},{2,0},{3,1},{4,6},{5,7},{6,4},{7,5},{8,10},{9,11},{10,... | collective-permute-start | bytes 393224 | tf_op jit(solution)/shard_map/chip_swap/ppermute | solution.py:104
  27.1 8.0 %collective-permute-start.12 = (f32[128,256]{1,0:T(8,128)S(1)}, f32[128,256]{1,0:T(8,128)S(1)}, u32[]{:S(2)}, u32[]{:S(2)}) collective-permute-start(f32[128,256]{1,0:T(8,128)S(1)} %get-tuple-element.74.refs_0_), channel_id=1, source_target_pairs={{0,2},{1,3},{2,0},{3,1},{4,6},{5,7},{6,4},{7,5},{8,10},{9,11},{10,... | collective-permute-start | bytes 393224 | tf_op jit(solution)/shard_map/chip_swap/ppermute | solution.py:104
  29.1 7.9 %collective-permute-start.13 = (f32[128,256]{1,0:T(8,128)S(1)}, f32[128,256]{1,0:T(8,128)S(1)}, u32[]{:S(2)}, u32[]{:S(2)}) collective-permute-start(f32[128,256]{1,0:T(8,128)S(1)} %relay.1.refs_2_.refs_12_), channel_id=1, source_target_pairs={{0,2},{1,3},{2,0},{3,1},{4,6},{5,7},{6,4},{7,5},{8,10},{9,11},{10,... | collective-permute-start | bytes 393224 | tf_op jit(solution)/shard_map/chip_swap/ppermute | solution.py:104
  30.2 8.0 %collective-permute-start.14 = (f32[128,256]{1,0:T(8,128)S(1)}, f32[128,256]{1,0:T(8,128)S(1)}, u32[]{:S(2)}, u32[]{:S(2)}) collective-permute-start(f32[128,256]{1,0:T(8,128)S(1)} %get-tuple-element.76.refs_0_), channel_id=1, source_target_pairs={{0,2},{1,3},{2,0},{3,1},{4,6},{5,7},{6,4},{7,5},{8,10},{9,11},{10,... | collective-permute-start | bytes 393224 | tf_op jit(solution)/shard_map/chip_swap/ppermute | solution.py:104
  32.6 8.0 %collective-permute-start.17 = (f32[128,256]{1,0:T(8,128)S(1)}, f32[128,256]{1,0:T(8,128)S(1)}, u32[]{:S(2)}, u32[]{:S(2)}) collective-permute-start(f32[128,256]{1,0:T(8,128)S(1)} %get-tuple-element.90), channel_id=1, source_target_pairs={{0,1},{1,0},{2,3},{3,2},{4,5},{5,4},{6,7},{7,6},{8,9},{9,8},{10,11... | collective-permute-start | bytes 393224 | tf_op jit(solution)/shard_map/core_swap/ppermute | solution.py:104
  35.1 5.6 %collective-permute-start.16 = (f32[128,256]{1,0:T(8,128)S(1)}, f32[128,256]{1,0:T(8,128)S(1)}, u32[]{:S(2)}, u32[]{:S(2)}) collective-permute-start(f32[128,256]{1,0:T(8,128)S(1)} %get-tuple-element.89), channel_id=1, source_target_pairs={{0,1},{1,0},{2,3},{3,2},{4,5},{5,4},{6,7},{7,6},{8,9},{9,8},{10,11... | collective-permute-start | bytes 393224 | tf_op jit(solution)/shard_map/core_swap/ppermute | solution.py:104
  35.2 5.5 %collective-permute-start.15 = (f32[128,256]{1,0:T(8,128)S(1)}, f32[128,256]{1,0:T(8,128)S(1)}, u32[]{:S(2)}, u32[]{:S(2)}) collective-permute-start(f32[128,256]{1,0:T(8,128)S(1)} %get-tuple-element.88), channel_id=1, source_target_pairs={{0,1},{1,0},{2,3},{3,2},{4,5},{5,4},{6,7},{7,6},{8,9},{9,8},{10,11... | collective-permute-start | bytes 393224 | tf_op jit(solution)/shard_map/core_swap/ppermute | solution.py:104
  37.0 14.7 %collective-permute-start.19 = (f32[128,256]{1,0:T(8,128)S(1)}, f32[128,256]{1,0:T(8,128)S(1)}, u32[]{:S(2)}, u32[]{:S(2)}) collective-permute-start(f32[128,256]{1,0:T(8,128)S(1)} %add_scaled.6.refs_1_.refs_0_), channel_id=1, source_target_pairs={{0,6},{1,7},{2,4},{3,5},{4,10},{5,11},{6,8},{7,9},{8,14},{9,15},{1... | collective-permute-start | bytes 393224 | tf_op jit(solution)/shard_map/onward/ppermute | solution.py:113
  38.2 3.4 %collective-permute-start.18 = (f32[128,256]{1,0:T(8,128)S(1)}, f32[128,256]{1,0:T(8,128)S(1)}, u32[]{:S(2)}, u32[]{:S(2)}) collective-permute-start(f32[128,256]{1,0:T(8,128)S(1)} %get-tuple-element.91), channel_id=1, source_target_pairs={{0,1},{1,0},{2,3},{3,2},{4,5},{5,4},{6,7},{7,6},{8,9},{9,8},{10,11... | collective-permute-start | bytes 393224 | tf_op jit(solution)/shard_map/core_swap/ppermute | solution.py:104
  40.6 11.0 %collective-permute-start.20 = (f32[128,256]{1,0:T(8,128)S(1)}, f32[128,256]{1,0:T(8,128)S(1)}, u32[]{:S(2)}, u32[]{:S(2)}) collective-permute-start(f32[128,256]{1,0:T(8,128)S(1)} %add_scaled.7.refs_1_), channel_id=1, source_target_pairs={{0,6},{1,7},{2,4},{3,5},{4,10},{5,11},{6,8},{7,9},{8,14},{9,15},{1... | collective-permute-start | bytes 393224 | tf_op jit(solution)/shard_map/onward/ppermute | solution.py:113

commit v4 on v2

v4 whole, which is shorter than its diff:
```python
import functools
import math

import jax
import jax.numpy as jnp
from jax import lax
from jax.experimental import pallas as pl
from jax.experimental.pallas import tpu as pltpu
from jax.sharding import PartitionSpec as P

STEP_SIZE = 0.001
LIKELIHOOD = 20.0
NOISE_SCALE = math.sqrt(0.002)
GAIN = STEP_SIZE * LIKELIHOOD
AXES = ("blk", "grp")
TILE = 128
CHUNKS = 2
WEIGHT = 8
COST = {"part": 2, "join": 0, "join_2": 16, "part_2": 2, "move": (4, 4, 4, 4), "user_step": 0, "layout": 0, "near": (2, 2), "far": (2, 2), "finish": 0, "last": 0, "final": 0}
VMEM_LIMIT = 16 * 1024 * 1024

NN = (((1,), (0,)), ((), ()))
NT = (((1,), (1,)), ((), ()))
TN = (((0,), (0,)), ((), ()))


def halves(value):
    high = value.astype(jnp.bfloat16)
    low = (value - high.astype(jnp.float32)).astype(jnp.bfloat16)
    return high, low


def product(left, right, dims):
    dot = functools.partial(
        lax.dot_general, dimension_numbers=dims, preferred_element_type=jnp.float32
    )
    return dot(left[0], right[0]) + (dot(left[0], right[1]) + dot(left[1], right[0]))


def errors_of(item_halves, user_halves, rating, weight):
    predicted = product(item_halves, user_halves, NT)
    return halves(weight.astype(jnp.float32) * (rating.astype(jnp.float32) - predicted))


def stepped(now, total, noise):
    return now + STEP_SIZE * (LIKELIHOOD * total - now) + NOISE_SCALE * noise


SCALARS = pl.BlockSpec(memory_space=pltpu.SMEM)
LOCAL = pl.BlockSpec(memory_space=pltpu.VMEM)
DISTANT = pl.BlockSpec(memory_space=pltpu.HBM)
AFTER = pl.BlockSpec(memory_space=pl.ANY)


def call(body, outs, operands, cost, scratch=(), after=()):
    unread = len(after)

    def kernel(*refs):
        body(*refs[unread:])

    return pl.pallas_call(
        kernel,
        in_specs=[AFTER] * unread + [spec for spec, _ in operands],
        out_specs=[LOCAL] * len(outs),
        out_shape=[jax.ShapeDtypeStruct(shape, dtype) for shape, dtype in outs],
        scratch_shapes=list(scratch),
        compiler_params=pltpu.CompilerParams(vmem_limit_bytes=VMEM_LIMIT),
        cost_estimate=pl.CostEstimate(
            flops=WEIGHT * cost, bytes_accessed=1 << 18, transcendentals=0
        ),
        name=body.__name__ if hasattr(body, "__name__") else body.func.__name__,
    )(*after, *[held(spec, array) for spec, array in operands])


def held(spec, array):
    return pltpu.with_memory_space_constraint(array, pltpu.HBM) if spec is DISTANT else array


def local(array):
    return (LOCAL, array)


def body(users, items, noise_users, noise_items, tile_index, counts, ratings, weights):
    f32, bf16 = jnp.float32, jnp.bfloat16
    n_blk, n_grp = lax.axis_size("blk"), lax.axis_size("grp")
    owned, rank = users.shape
    slots = ratings.shape[1]
    columns = items.shape[0] // TILE
    per_quarter = columns // n_grp
    quarter = per_quarter * TILE
    chunk = quarter // CHUNKS
    place = (SCALARS, lax.axis_index("grp").astype(jnp.int32).reshape(1))

    def swap(value, other):
        pairs = [
            (b * n_grp + g, b * n_grp + (g ^ other)) for b in range(n_blk) for g in range(n_grp)
        ]
        with jax.named_scope("core_swap" if other == 1 else "chip_swap"):
            return lax.ppermute(value, AXES, pairs)

    def onward(value):
        pairs = [
            (b * n_grp + g, (b + 1) % n_blk * n_grp + (g ^ 2))
            for b in range(n_blk)
            for g in range(n_grp)
        ]
        with jax.named_scope("onward"):
            return lax.ppermute(value, AXES, pairs)

    dense = (columns, owned, TILE)
    piece = (chunk, rank)
    square = (quarter, owned)
    unit = 2 * owned * quarter * rank * 3

    def rows_of(place_ref, flip):
        return pl.ds(pl.multiple_of((place_ref[0] ^ flip) * quarter, quarter), quarter)

    def side_by_side(dense_ref, start):
        return jnp.concatenate([dense_ref[start + t] for t in range(per_quarter)], 1)

    def quarter_terms(place_ref, flip, rating_ref, weight_ref, users_ref, items_ref, high_ref, low_ref):
        start = (place_ref[0] ^ flip) * per_quarter
        user_halves = halves(users_ref[...])
        item_halves = halves(items_ref[rows_of(place_ref, flip), :])
        rating = side_by_side(rating_ref, start).astype(f32).T
        weight = side_by_side(weight_ref, start).astype(f32).T
        errors = errors_of(item_halves, user_halves, rating, weight)
        high_ref[...], low_ref[...] = errors
        return product(errors, user_halves, NN)

    def fetch(pairs, sems):
        copies = [pltpu.make_async_copy(a, b, sems.at[n]) for n, (a, b) in enumerate(pairs)]
        for copy in copies:
            copy.start()
        return copies

    live = counts.reshape(-1)
    tables = [(DISTANT, tile_index), (DISTANT, live), (DISTANT, ratings), (DISTANT, weights)]
    landing = [
        pltpu.SMEM(tile_index.shape, jnp.int32),
        pltpu.SMEM(live.shape, jnp.int32),
        pltpu.VMEM(ratings.shape[1:], bf16),
        pltpu.VMEM(weights.shape[1:], bf16),
    ]

    def first(place_ref, index_hbm, count_hbm, rating_hbm, weight_hbm, users_hbm, items_hbm, noise_hbm,
              rating_out, weight_out, users_out, items_out, noise_out, high_out, low_out, grads_out,
              index_ref, count_ref, rating_in, weight_in, sems):
        copies = fetch(
            [(index_hbm, index_ref), (count_hbm, count_ref),
             (rating_hbm.at[0], rating_in), (weight_hbm.at[0], weight_in),
             (users_hbm, users_out), (items_hbm, items_out),
             (noise_hbm.at[0, rows_of(place_ref, 2), :], noise_out.at[:quarter, :]),
             (noise_hbm.at[0, rows_of(place_ref, 0), :], noise_out.at[quarter:, :])],
            sems,
        )
        rating_out[...] = jnp.zeros_like(rating_out)
        weight_out[...] = jnp.zeros_like(weight_out)
        for copy in copies[:4]:
            copy.wait()
        for slot in range(slots):

            @pl.when(slot < count_ref[0])
            def _(slot=slot):
                tile = index_ref[0, slot]
                column = lax.rem(tile, columns)
                row = pl.multiple_of(lax.div(tile, columns) * TILE, TILE)
                rating_out[column, pl.ds(row, TILE), :] = rating_in[slot]
                weight_out[column, pl.ds(row, TILE), :] = weight_in[slot]

        copies[4].wait()
        copies[5].wait()
        grads_out[...] = quarter_terms(
            place_ref, 1, rating_out, weight_out, users_out, items_out, high_out, low_out
        )
        copies[6].wait()
        copies[7].wait()

    part_outs = [(square, bf16)] * 2 + [((quarter, rank), f32)]
    rating_0, weight_0, users_0, items_0, noise_0, *errors_1, to_sibling = call(
        first,
        [(dense, bf16)] * 2 + [(users.shape, f32), (items.shape, f32), ((2 * quarter, rank), f32)] + part_outs,
        [place] + tables + [(DISTANT, v) for v in (users, items, noise_items)],
        2 * unit,
        landing + [pltpu.SemaphoreType.DMA((8,))],
    )
    from_sibling_0 = swap(to_sibling, 1)
    stage_0 = [local(rating_0), local(weight_0), local(users_0), local(items_0)]

    def part(flip, place_ref, *refs):
        refs[-1][...] = quarter_terms(place_ref, flip, *refs[:-1])

    def quarter_part(flip, cost, after):
        high, low, grads = call(
            functools.partial(part, flip), part_outs, [place] + stage_0, cost * unit, after=after
        )
        return [high, low], grads

    def join(at, a_ref, b_ref, out):
        out[...] = a_ref[at, :] + b_ref[at, :]

    def add_scaled(at, base_ref, a_ref, out):
        out[...] = base_ref[at, :] + GAIN * a_ref[at, :]

    def rows(k):
        return slice(k * chunk, (k + 1) * chunk)

    def joined(kernel, at, a, b, cost, after):
        return call(
            functools.partial(kernel, at), [(piece, f32)], [local(a), local(b)], cost * unit,
            after=after,
        )

    errors_3, to_sibling = quarter_part(3, COST["part"], [])
    from_sibling_2 = swap(to_sibling, 1)
    errors_0, mine = quarter_part(0, COST["part"], [to_sibling])
    to_chip = []
    for k in range(CHUNKS):
        to_chip += joined(join, rows(k), mine, from_sibling_0, COST["join"], to_chip[-1:])
    from_chip = [swap(value, 2) for value in to_chip]
    errors_2, mine = quarter_part(2, COST["part_2"], to_chip)

    def user_step(place_ref, users_ref, items_ref, noise_ref, *rest):
        errors, users_out = rest[:-1], rest[-1]
        total = jnp.zeros((owned, rank), f32)
        for flip in range(n_grp):
            item_halves = halves(items_ref[rows_of(place_ref, flip), :])
            kept = (errors[2 * flip][...], errors[2 * flip + 1][...])
            total = total + product(kept, item_halves, TN)
        users_out[...] = stepped(users_ref[...], total, noise_ref[...])

    [users_1] = call(
        user_step,
        [(users.shape, f32)],
        [place, local(users_0), local(items_0), local(noise_users[0])]
        + [local(v) for v in errors_0 + errors_1 + errors_2 + errors_3],
        COST["user_step"] * unit,
    )
    flat = (columns * TILE, owned)

    def layout(place_ref, index_hbm, count_hbm, noise_hbm, rating_ref, weight_ref, users_ref,
               rating_out, weight_out, send_out, noise_out, index_ref, count_ref, sems):
        copies = fetch(
            [(index_hbm, index_ref), (count_hbm, count_ref),
             (noise_hbm.at[1, rows_of(place_ref, 2), :], noise_out)],
            sems,
        )
        rating_out[...] = jnp.zeros_like(rating_out)
        weight_out[...] = jnp.zeros_like(weight_out)
        for copy in copies[:2]:
            copy.wait()
        for slot in range(slots):

            @pl.when(slot < count_ref[1])
            def _(slot=slot):
                tile = index_ref[1, slot]
                at = pl.ds(pl.multiple_of(lax.rem(tile, columns) * TILE, TILE), TILE)
                turned = (rating_ref[slot].astype(f32).T, weight_ref[slot].astype(f32).T)
                for row in range(owned // TILE):

                    @pl.when(lax.div(tile, columns) == row)
                    def _(row=row):
                        across = slice(row * TILE, (row + 1) * TILE)
                        rating_out[at, across] = turned[0]
                        weight_out[at, across] = turned[1]

        for n, flip in enumerate((1, 3)):
            for offset, values in ((0, rating_out), (2 * quarter, weight_out)):
                at = slice(offset + n * quarter, offset + (n + 1) * quarter)
                send_out[at, :] = values[rows_of(place_ref, flip), :]
        send_out[4 * quarter :, :] = users_ref[...]
        copies[2].wait()

    rating_1, weight_1, to_sibling, noise_1 = call(
        layout,
        [(flat, f32)] * 2 + [((4 * quarter + owned, rank), f32), ((quarter, rank), f32)],
        [place] + tables[:2] + [(DISTANT, noise_items)]
        + [local(v) for v in (ratings[1], weights[1], users_1)],
        COST["layout"] * unit,
        landing[:2] + [pltpu.SemaphoreType.DMA((3,))],
        after=[users_1],
    )
    from_sibling = swap(to_sibling, 1)

    def move(n, place_ref, items_ref, noise_ref, own_ref, other_ref, out):
        flip, k = (2, 0)[n // CHUNKS], n % CHUNKS
        start = pl.multiple_of((place_ref[0] ^ flip) * quarter + k * chunk, chunk)
        total = own_ref[...] + other_ref[...]
        out[...] = stepped(items_ref[pl.ds(start, chunk), :], total, noise_ref[rows(n), :])

    moved = []
    for n in range(2 * CHUNKS):
        if n < CHUNKS:
            to_chip += joined(
                join, rows(n), mine, from_sibling_2, COST["join_2"],
                [to_sibling, from_chip[n], *moved[-1:]],
            )
            from_chip.append(swap(to_chip[-1], 2))
        terms = [local(v) for v in (items_0, noise_0, to_chip[(n + CHUNKS) % (2 * CHUNKS)], from_chip[n])]
        moved += call(
            functools.partial(move, n), [(piece, f32)], [place] + terms, COST["move"][n] * unit,
            after=moved[-1:],
        )
    ahead = [onward(value) for value in moved]

    def late(k, slot, place_ref, items_ref, users_ref, rating_ref, weight_ref, sibling_ref, *rest):
        high_out, low_out, out = rest[-3:]
        own, other = halves(users_ref[...]), halves(sibling_ref[4 * quarter :, :])
        now = items_ref[...]
        item_halves = halves(now)
        at = pl.ds(pl.multiple_of((place_ref[0] ^ (2 * slot)) * quarter + k * chunk, chunk), chunk)
        errors = errors_of(item_halves, own, rating_ref[at, :], weight_ref[at, :])
        high_out[...], low_out[...] = errors
        total = product(errors, own, NN)
        at = slot * quarter + k * chunk
        rating = sibling_ref[at : at + chunk, :]
        weight = sibling_ref[2 * quarter + at : 2 * quarter + at + chunk, :]
        errors = errors_of(item_halves, other, rating, weight)
        total = total + product(errors, other, NN)
        if slot == 1:
            total = stepped(now, total, rest[0][rows(k), :])
        out[...] = total

    common = [local(v) for v in (users_1, rating_1, weight_1, from_sibling)]
    errors_shape = (chunk, owned)
    late_outs = [(errors_shape, bf16)] * 2 + [(piece, f32)]
    def relay(value_ref, out):
        out[...] = value_ref[...]

    def relayed(value, cost, after):
        return call(relay, [(piece, f32)], [local(value)], cost * unit, after=after)

    here, there = ahead[:CHUNKS], ahead[CHUNKS:]
    errors_here, sent = [], []
    for k in range(CHUNKS):
        high, low, value = call(
            functools.partial(late, k, 0), late_outs, [place, local(here[k])] + common,
            COST["near"][k] * unit, after=sent[-1:],
        )
        errors_here.append((high, low))
        sent.append(value)
    received = [swap(value, 2) for value in sent]
    errors_there, finished = [], []
    for k in range(CHUNKS):
        high, low, value = call(
            functools.partial(late, k, 1), late_outs,
            [place, local(there[k])] + common + [local(noise_1)], COST["far"][k] * unit,
            after=[sent[-1], *finished[-1:]],
        )
        errors_there.append((high, low))
        finished += joined(add_scaled, rows(0), value, received[k], COST["finish"], [])
    final = [onward(value) for value in finished]

    def stack(*refs):
        for k in range(CHUNKS):
            refs[-1][rows(k), :] = refs[k][...]

    def paired(values, after):
        [value] = call(stack, [((quarter, rank), f32)], [local(v) for v in values], 1, after=after)
        return swap(value, 1)

    here_s, there_s = paired(here, sent[-1:]), paired(there, finished[:1])

    def last(place_ref, rating_ref, weight_ref, users_ref, noise_hbm, *rest):
        known, blocks = rest[: 6 * CHUNKS], rest[6 * CHUNKS : 6 * CHUNKS + 2]
        users_out, token, noise, sems = rest[6 * CHUNKS + 2 :]
        token[...] = jnp.zeros_like(token)
        [copy] = fetch([(noise_hbm.at[1], noise)], sems)
        user_halves = halves(users_ref[...])
        total = jnp.zeros((owned, rank), f32)
        for n in range(2 * CHUNKS):
            errors = (known[3 * n][...], known[3 * n + 1][...])
            total = total + product(errors, halves(known[3 * n + 2][...]), TN)
        for block, flip in zip(blocks, (1, 3)):
            at = rows_of(place_ref, flip)
            item_halves = halves(block[...])
            errors = errors_of(item_halves, user_halves, rating_ref[at, :], weight_ref[at, :])
            total = total + product(errors, item_halves, TN)
        copy.wait()
        users_out[...] = stepped(users_ref[...], total, noise[...])

    known = [
        local(v)
        for errors, values in zip(errors_here + errors_there, here + there)
        for v in (*errors, values)
    ]
    users_out, token = call(
        last,
        [(users.shape, f32), ((8, 128), f32)],
        [place, local(rating_1), local(weight_1), local(users_1), (DISTANT, noise_users)]
        + known + [local(here_s), local(there_s)],
        COST["last"] * unit,
        [pltpu.VMEM(users.shape, f32), pltpu.SemaphoreType.DMA((1,))],
        after=finished,
    )

    [early] = relayed(final[0], COST["final"], [token])
    [items_out] = call(stack, [((quarter, rank), f32)], [local(early), local(final[1])], 1)
    return (users_out, items_out)


def solution(mesh):
    in_specs = (
        P(("blk", "grp"), None),
        P("blk", None),
        P(None, ("blk", "grp"), None),
        P(None, "blk", None),
        P(None, ("blk", "grp")),
        P(None, ("blk", "grp")),
        P(None, ("blk", "grp"), None, None),
        P(None, ("blk", "grp"), None, None),
    )
    out_specs = (P(("blk", "grp"), None), P(("blk", "grp"), None))
    return jax.shard_map(body, mesh=mesh, in_specs=in_specs, out_specs=out_specs, check_vma=False)
```

time: 55.9 us -> 48.1 us (0.86)
  waiting for transfers between devices: 23.9 us -> 15.6 us
  Pallas kernels: 14.8 us -> 12.9 us
  starting transfers between devices: 16.1 us -> 17.9 us
  local copies, waits for them, and re-layouts: 0 us -> 0.58 us
    ppermute x4 -> x6, waiting for transfers between devices: 21.3 us -> 12.8 us  [onward(): return lax.ppermute(value, AXES, pairs)]
    ppermute x4 -> x6, starting transfers between devices: 2.45 us -> 5.32 us  [onward(): return lax.ppermute(value, AXES, pairs)]
    pallas_call x17 -> x25, Pallas kernels: 14.8 us -> 12.9 us  [call(): pl.pallas_call(kernel, in_specs=[AFTER] * unread + [spec for spec, _ in o...]
    ppermute x17 -> x11, starting transfers between devices: 13.6 us -> 12.5 us  [swap(): return lax.ppermute(value, AXES, pairs)]
    ppermute x17 -> x11, waiting for transfers between devices: 2.61 us -> 2.81 us  [swap(): return lax.ppermute(value, AXES, pairs)]
  transfers between devices with their start and end apart: 21 -> 17, of which waited for: 7 -> 8; matrix products, arithmetic and copies ran while one was open for 0% -> 0% of each run, Pallas kernels for 21% -> 21%
where the time goes in v4:
time: 48.1 us; the launch traced here: 47.9 us
  starting transfers between devices  17.9 us (37%)
  waiting for transfers between devices  15.6 us (32%)
  Pallas kernels  12.9 us (27%)
  between operations  0.87 us (2%)
  local copies, waits for them, and re-layouts  0.58 us (1%)
    pallas_call x25, Pallas kernels, call(): pl.pallas_call(kernel, in_specs=[AFTER] * unread + [spec for spec, _ in o...  12.9 us
    ppermute x6, waiting for transfers between devices, onward(): return lax.ppermute(value, AXES, pairs)  12.8 us
    ppermute x11, starting transfers between devices, swap(): return lax.ppermute(value, AXES, pairs)  12.5 us
    ppermute x6, starting transfers between devices, onward(): return lax.ppermute(value, AXES, pairs)  5.32 us
    ppermute x11, waiting for transfers between devices, swap(): return lax.ppermute(value, AXES, pairs)  2.81 us
  transfers between devices with their start and end apart: 17, of which 8 were waited for; matrix products, arithmetic and copies ran while one was open for 0% of the time, Pallas kernels for 21%

profile of v4, /device:TPU:1, one launch (start us, length us, event | category | flops | bytes accessed | tf_op | source)
XLA Modules:
  0.0 47.9 jit_solution(500576668216642040)
XLA Ops:
  0.6 2.2 %first.1 = (bf16[8,256,128]{2,1,0:T(8,128)(2,1)S(1)}, bf16[8,256,128]{2,1,0:T(8,128)(2,1)S(1)}, f32[256,256]{1,0:T(8,128)S(1)}, f32[1024,256]{1,0:T(8,128)S(1)},...) custom-call(s32[1]{0:T(128)} %bitcast.refs_0_.refs_1_.refs_2_, ...), custom_call_target="tpu_custom_call" | custom-call | flops 1610612736 | bytes 262144 | tf_op jit(solution)/shard_map/first/pallas_call | solution.py:61
  2.8 3.3 %collective-permute-start = (f32[256,256]{1,0:T(8,128)S(1)}, f32[256,256]{1,0:T(8,128)S(1)}, u32[]{:S(2)}, u32[]{:S(2)}) collective-permute-start(f32[256,256]{1,0:T(8,128)S(1)} %get-tuple-element.48), channel_id=1, source_target_pairs={{0,1},{1,0},{2,3},{3,2},{4,5},{5,4},{6,7},{7,6},{8,9},{9,8},{10,11... | collective-permute-start | bytes 786440 | tf_op jit(solution)/shard_map/core_swap/ppermute | solution.py:99
  6.2 0.6 %part.3 = (bf16[256,256]{1,0:T(8,128)(2,1)S(1)}, bf16[256,256]{1,0:T(8,128)(2,1)S(1)}, f32[256,256]{1,0:T(8,128)S(1)}) custom-call(s32[1]{0:T(128)} %bitcast.refs_0_.refs_1_.refs_2_, bf16[8,256,128]{2,1,0:T(8,128)(2,1)S(1)} %get-tuple-element.40.refs_1_.refs_2_.refs_3_, bf16[8,256,128]{2,1,0:T(8,128)(2,1)S(1)} %get-tuple-element.41.refs_2_.refs_3_.refs_4_, ...), custom_call_target="tpu_custom_call" | custom-call | flops 1610612736 | bytes 262144 | tf_op jit(solution)/shard_map/part/pallas_call | solution.py:61
  6.8 0.1 collective-permute-start.2
  7.0 0.3 copy-done.1
  7.2 0.2 copy-done.2
  7.4 0.1 copy-done
  7.5 0.6 %part.4 = (bf16[256,256]{1,0:T(8,128)(2,1)S(1)}, bf16[256,256]{1,0:T(8,128)(2,1)S(1)}, f32[256,256]{1,0:T(8,128)S(1)}) custom-call(f32[256,256]{1,0:T(8,128)S(1)} %get-tuple-element.42.refs_0_, s32[1]{0:T(128)} %bitcast.refs_0_.refs_1_.refs_2_, bf16[8,256,128]{2,1,0:T(8,128)(2,1)S(1)} %get-tuple-element.40.refs_1_.refs_2_.refs_3_, ...), custom_call_target="tpu_custom_call" | custom-call | flops 1610612736 | bytes 262144 | tf_op jit(solution)/shard_map/part/pallas_call | solution.py:61
  8.2 0.0 collective-permute-done.refs_1_.refs_2_
  8.2 0.1 collective-permute-start.1
  8.4 1.5 %collective-permute-start.5 = (f32[128,256]{1,0:T(8,128)S(1)}, f32[128,256]{1,0:T(8,128)S(1)}, u32[]{:S(2)}, u32[]{:S(2)}) collective-permute-start(f32[128,256]{1,0:T(8,128)S(1)} %join.5.refs_1_.refs_4_), channel_id=1, source_target_pairs={{0,2},{1,3},{2,0},{3,1},{4,6},{5,7},{6,4},{7,5},{8,10},{9,11},{10,... | collective-permute-start | bytes 393224 | tf_op jit(solution)/shard_map/chip_swap/ppermute | solution.py:99
  9.9 0.6 %part.5 = (bf16[256,256]{1,0:T(8,128)(2,1)S(1)}, bf16[256,256]{1,0:T(8,128)(2,1)S(1)}, f32[256,256]{1,0:T(8,128)S(1)}) custom-call(f32[128,256]{1,0:T(8,128)S(1)} %join.4.refs_0_.refs_4_, f32[128,256]{1,0:T(8,128)S(1)} %join.5.refs_1_.refs_4_, s32[1]{0:T(128)} %bitcast.refs_0_.refs_1_.refs_2_, ...), custom_call_target="tpu_custom_call" | custom-call | flops 1610612736 | bytes 262144 | tf_op jit(solution)/shard_map/part/pallas_call | solution.py:61
  10.5 0.7 %user_step.1.refs_0_.refs_7_.refs_2_.refs_3_.refs_4_.refs_5_ = f32[256,256]{1,0:T(8,128)S(1)} custom-call(s32[1]{0:T(128)} %bitcast.refs_0_.refs_1_.refs_2_, f32[256,256]{1,0:T(8,128)S(1)} %get-tuple-element.39.refs_3_.refs_4_.refs_5_.refs_1_, f32[1024,256]{1,0:T(8,128)S(1)} %get-tuple-element.37.refs_4_.refs_5_.refs_6_.refs_2_.refs_1_, ...), custom_call_target="tpu_custom_call" | custom-call | bytes 262144 | tf_op jit(solution)/shard_map/user_step/pallas_call | solution.py:61
  11.2 1.4 %layout.1 = (f32[1024,256]{1,0:T(8,128)S(1)}, f32[1024,256]{1,0:T(8,128)S(1)}, f32[1280,256]{1,0:T(8,128)S(1)}, f32[256,256]{1,0:T(8,128)S(1)}) custom-call(f32[256,256]{1,0:T(8,128)S(1)} %user_step.1.refs_0_.refs_7_.refs_2_.refs_3_.refs_4_.refs_5_, s32[1]{0:T(128)} %bitcast.refs_0_.refs_1_.refs_2_, s32[2,8]{1,0:T(2,128)} %refs_2_.1, s32[2]{0:T(128)} %bitcast.9, ...), custom_call_target="tpu_custom_call" | custom-call | bytes 262144 | tf_op jit(solution)/shard_map/layout/pallas_call | solution.py:61
  12.6 0.9 %collective-permute-start.4 = (f32[1280,256]{1,0:T(8,128)S(1)}, f32[1280,256]{1,0:T(8,128)S(1)}, u32[]{:S(2)}, u32[]{:S(2)}) collective-permute-start(f32[1280,256]{1,0:T(8,128)S(1)} %get-tuple-element.53.refs_0_), channel_id=1, source_target_pairs={{0,1},{1,0},{2,3},{3,2},{4,5},{5,4},{6,7},{7,6},{8,9},{9,8},{10,11... | collective-permute-start | bytes 3932168 | tf_op jit(solution)/shard_map/core_swap/ppermute | solution.py:99
  13.5 0.0 collective-permute-done.2.refs_3_.refs_4_
  13.5 0.0 collective-permute-done.1.refs_1_.refs_4_
  13.5 0.2 collective-permute-start.7
  13.8 1.2 %collective-permute-start.3 = (f32[128,256]{1,0:T(8,128)S(1)}, f32[128,256]{1,0:T(8,128)S(1)}, u32[]{:S(2)}, u32[]{:S(2)}) collective-permute-start(f32[128,256]{1,0:T(8,128)S(1)} %move.4.refs_2_.refs_0_), channel_id=1, source_target_pairs={{0,6},{1,7},{2,4},{3,5},{4,10},{5,11},{6,8},{7,9},{8,14},{9,15},{1... | collective-permute-start | bytes 393224 | tf_op jit(solution)/shard_map/onward/ppermute | solution.py:108
  15.0 1.3 %collective-permute-done.5.refs_1_.refs_5_ = f32[128,256]{1,0:T(8,128)S(1)} collective-permute-done((f32[128,256]{1,0:T(8,128)S(1)}, f32[128,256]{1,0:T(8,128)S(1)}, u32[]{:S(2)}, u32[]{:S(2)}) %collective-permute-start.5) | collective-permute-done | bytes 131104 | tf_op jit(solution)/shard_map/chip_swap/ppermute | solution.py:99
  16.3 0.3 collective-permute-start.10
  16.6 1.2 %collective-permute-start.6 = (f32[128,256]{1,0:T(8,128)S(1)}, f32[128,256]{1,0:T(8,128)S(1)}, u32[]{:S(2)}, u32[]{:S(2)}) collective-permute-start(f32[128,256]{1,0:T(8,128)S(1)} %move.5.refs_0_), channel_id=1, source_target_pairs={{0,6},{1,7},{2,4},{3,5},{4,10},{5,11},{6,8},{7,9},{8,14},{9,15},{1... | collective-permute-start | bytes 393224 | tf_op jit(solution)/shard_map/onward/ppermute | solution.py:108
  17.8 0.4 collective-permute-done.7.refs_5_
  18.2 1.9 %collective-permute-start.8 = (f32[128,256]{1,0:T(8,128)S(1)}, f32[128,256]{1,0:T(8,128)S(1)}, u32[]{:S(2)}, u32[]{:S(2)}) collective-permute-start(f32[128,256]{1,0:T(8,128)S(1)} %move.6.refs_0_), channel_id=1, source_target_pairs={{0,6},{1,7},{2,4},{3,5},{4,10},{5,11},{6,8},{7,9},{8,14},{9,15},{1... | collective-permute-start | bytes 393224 | tf_op jit(solution)/shard_map/onward/ppermute | solution.py:108
  20.1 1.0 %collective-permute-done.10.refs_5_ = f32[128,256]{1,0:T(8,128)S(1)} collective-permute-done((f32[128,256]{1,0:T(8,128)S(1)}, f32[128,256]{1,0:T(8,128)S(1)}, u32[]{:S(2)}, u32[]{:S(2)}) %collective-permute-start.10) | collective-permute-done | bytes 131104 | tf_op jit(solution)/shard_map/chip_swap/ppermute | solution.py:99
  21.1 0.9 %collective-permute-start.11 = (f32[128,256]{1,0:T(8,128)S(1)}, f32[128,256]{1,0:T(8,128)S(1)}, u32[]{:S(2)}, u32[]{:S(2)}) collective-permute-start(f32[128,256]{1,0:T(8,128)S(1)} %move.7), channel_id=1, source_target_pairs={{0,6},{1,7},{2,4},{3,5},{4,10},{5,11},{6,8},{7,9},{8,14},{9,15},{1... | collective-permute-start | bytes 393224 | tf_op jit(solution)/shard_map/onward/ppermute | solution.py:108
  22.0 3.0 %collective-permute-done.3.refs_1_.refs_9_ = f32[128,256]{1,0:T(8,128)S(1)} collective-permute-done((f32[128,256]{1,0:T(8,128)S(1)}, f32[128,256]{1,0:T(8,128)S(1)}, u32[]{:S(2)}, u32[]{:S(2)}) %collective-permute-start.3) | collective-permute-done | bytes 131104 | tf_op jit(solution)/shard_map/onward/ppermute | solution.py:108
  25.0 0.0 collective-permute-done.4.refs_5_.refs_6_.refs_7_
  25.1 0.9 %late.4 = (bf16[128,256]{1,0:T(8,128)(2,1)S(1)}, bf16[128,256]{1,0:T(8,128)(2,1)S(1)}, f32[128,256]{1,0:T(8,128)S(1)}) custom-call(s32[1]{0:T(128)} %bitcast.refs_0_.refs_1_.refs_2_, f32[128,256]{1,0:T(8,128)S(1)} %collective-permute-done.3.refs_1_.refs_9_, f32[256,256]{1,0:T(8,128)S(1)} %user_step.1.refs_0_.refs_7_.refs_2_.refs_3_.refs_4_.refs_5_, ...), custom_call_target="tpu_custom_call" | custom-call | flops 1610612736 | bytes 262144 | tf_op jit(solution)/shard_map/late/pallas_call | solution.py:61
  25.9 0.5 collective-permute-start.9
  26.4 2.0 %collective-permute-done.6.refs_2_.refs_12_ = f32[128,256]{1,0:T(8,128)S(1)} collective-permute-done((f32[128,256]{1,0:T(8,128)S(1)}, f32[128,256]{1,0:T(8,128)S(1)}, u32[]{:S(2)}, u32[]{:S(2)}) %collective-permute-start.6) | collective-permute-done | bytes 131104 | tf_op jit(solution)/shard_map/onward/ppermute | solution.py:108
  28.4 0.9 %late.5 = (bf16[128,256]{1,0:T(8,128)(2,1)S(1)}, bf16[128,256]{1,0:T(8,128)(2,1)S(1)}, f32[128,256]{1,0:T(8,128)S(1)}) custom-call(f32[128,256]{1,0:T(8,128)S(1)} %get-tuple-element.57.refs_0_, s32[1]{0:T(128)} %bitcast.refs_0_.refs_1_.refs_2_, f32[128,256]{1,0:T(8,128)S(1)} %collective-permute-done.6.refs_2_.refs_12_, ...), custom_call_target="tpu_custom_call" | custom-call | flops 1610612736 | bytes 262144 | tf_op jit(solution)/shard_map/late/pallas_call | solution.py:61
  29.3 0.6 %collective-permute-start.12 = (f32[128,256]{1,0:T(8,128)S(1)}, f32[128,256]{1,0:T(8,128)S(1)}, u32[]{:S(2)}, u32[]{:S(2)}) collective-permute-start(f32[128,256]{1,0:T(8,128)S(1)} %get-tuple-element.58.refs_0_), channel_id=1, source_target_pairs={{0,2},{1,3},{2,0},{3,1},{4,6},{5,7},{6,4},{7,5},{8,10},{9,11},{10,... | collective-permute-start | bytes 393224 | tf_op jit(solution)/shard_map/chip_swap/ppermute | solution.py:99
  29.9 3.4 %collective-permute-start.13 = (f32[256,256]{1,0:T(8,128)S(1)}, f32[256,256]{1,0:T(8,128)S(1)}, u32[]{:S(2)}, u32[]{:S(2)}) collective-permute-start(f32[256,256]{1,0:T(8,128)S(1)} %stack.3), channel_id=1, source_target_pairs={{0,1},{1,0},{2,3},{3,2},{4,5},{5,4},{6,7},{7,6},{8,9},{9,8},{10,11... | collective-permute-start | bytes 786440 | tf_op jit(solution)/shard_map/core_swap/ppermute | solution.py:99
  33.4 0.0 collective-permute-done.8.refs_2_.refs_1_.refs_15_
  33.4 0.9 %late.6 = (bf16[128,256]{1,0:T(8,128)(2,1)S(1)}, bf16[128,256]{1,0:T(8,128)(2,1)S(1)}, f32[128,256]{1,0:T(8,128)S(1)}) custom-call(f32[128,256]{1,0:T(8,128)S(1)} %get-tuple-element.58.refs_0_, s32[1]{0:T(128)} %bitcast.refs_0_.refs_1_.refs_2_, f32[128,256]{1,0:T(8,128)S(1)} %collective-permute-done.8.refs_2_.refs_1_.refs_15_, ...), custom_call_target="tpu_custom_call" | custom-call | flops 1610612736 | bytes 262144 | tf_op jit(solution)/shard_map/late/pallas_call | solution.py:61
  34.2 0.0 collective-permute-done.9.refs_1_
  34.3 0.1 collective-permute-start.15
  34.4 1.5 %collective-permute-start.14 = (f32[256,256]{1,0:T(8,128)S(1)}, f32[256,256]{1,0:T(8,128)S(1)}, u32[]{:S(2)}, u32[]{:S(2)}) collective-permute-start(f32[256,256]{1,0:T(8,128)S(1)} %stack.4), channel_id=1, source_target_pairs={{0,1},{1,0},{2,3},{3,2},{4,5},{5,4},{6,7},{7,6},{8,9},{9,8},{10,11... | collective-permute-start | bytes 786440 | tf_op jit(solution)/shard_map/core_swap/ppermute | solution.py:99
  35.9 0.9 %late.7 = (bf16[128,256]{1,0:T(8,128)(2,1)S(1)}, bf16[128,256]{1,0:T(8,128)(2,1)S(1)}, f32[128,256]{1,0:T(8,128)S(1)}) custom-call(f32[128,256]{1,0:T(8,128)S(1)} %get-tuple-element.58.refs_0_, f32[128,256]{1,0:T(8,128)S(1)} %add_scaled.2.refs_1_.refs_0_, s32[1]{0:T(128)} %bitcast.refs_0_.refs_1_.refs_2_, ...), custom_call_target="tpu_custom_call" | custom-call | flops 1610612736 | bytes 262144 | tf_op jit(solution)/shard_map/late/pallas_call | solution.py:61
  36.8 0.0 collective-permute-done.12.refs_1_
  36.8 0.1 collective-permute-start.16
  36.9 0.0 collective-permute-done.13.refs_19_
  36.9 0.1 collective-permute-done.14.refs_20_
  37.1 2.3 %last.1 = (f32[256,256]{1,0:T(8,128)}, f32[8,128]{1,0:T(8,128)S(1)}) custom-call(f32[128,256]{1,0:T(8,128)S(1)} %add_scaled.2.refs_1_.refs_0_, f32[128,256]{1,0:T(8,128)S(1)} %add_scaled.3.refs_1_, s32[1]{0:T(128)} %bitcast.refs_0_.refs_1_.refs_2_, f32[1024,256]{1,0:T(8,128)S(1)} %get-tuple-element.55.refs_3_.refs_4_.refs_5_, ...), custom_call_target="tpu_custom_call" | custom-call | bytes 262144 | tf_op jit(solution)/shard_map/last/pallas_call | solution.py:61
  39.4 4.2 %collective-permute-done.15.refs_1_ = f32[128,256]{1,0:T(8,128)S(1)} collective-permute-done((f32[128,256]{1,0:T(8,128)S(1)}, f32[128,256]{1,0:T(8,128)S(1)}, u32[]{:S(2)}, u32[]{:S(2)}) %collective-permute-start.15) | collective-permute-done | bytes 131104 | tf_op jit(solution)/shard_map/onward/ppermute | solution.py:108
  43.6 3.5 %collective-permute-done.16.refs_1_ = f32[128,256]{1,0:T(8,128)S(1)} collective-permute-done((f32[128,256]{1,0:T(8,128)S(1)}, f32[128,256]{1,0:T(8,128)S(1)}, u32[]{:S(2)}, u32[]{:S(2)}) %collective-permute-start.16) | collective-permute-done | bytes 131104 | tf_op jit(solution)/shard_map/onward/ppermute | solution.py:108
  47.2 0.7 %stack.5 = f32[256,256]{1,0:T(8,128)} custom-call(f32[128,256]{1,0:T(8,128)S(1)} %relay.1.refs_0_, f32[128,256]{1,0:T(8,128)S(1)} %collective-permute-done.16.refs_1_), custom_call_target="tpu_custom_call" | custom-call | flops 8 | bytes 262144 | tf_op jit(solution)/shard_map/stack/pallas_call | solution.py:61
  (19 shorter events, 0.4 us)
Async XLA Ops:
  2.8 5.4 %collective-permute-start = (f32[256,256]{1,0:T(8,128)S(1)}, f32[256,256]{1,0:T(8,128)S(1)}, u32[]{:S(2)}, u32[]{:S(2)}) collective-permute-start(f32[256,256]{1,0:T(8,128)S(1)} %get-tuple-element.48), channel_id=1, source_target_pairs={{0,1},{1,0},{2,3},{3,2},{4,5},{5,4},{6,7},{7,6},{8,9},{9,8},{10,11... | collective-permute-start | bytes 786440 | tf_op jit(solution)/shard_map/core_swap/ppermute | solution.py:99
  6.2 1.0 %copy-start.1 = (bf16[2,8,128,128]{3,2,1,0:T(8,128)(2,1)S(1)}, bf16[2,8,128,128]{3,2,1,0:T(8,128)(2,1)}, u32[]{:S(2)}) copy-start(bf16[2,8,128,128]{3,2,1,0:T(8,128)(2,1)} %refs_3_.1) | copy-start | bytes 1572868
  6.2 1.2 %copy-start.2 = (bf16[2,8,128,128]{3,2,1,0:T(8,128)(2,1)S(1)}, bf16[2,8,128,128]{3,2,1,0:T(8,128)(2,1)}, u32[]{:S(2)}) copy-start(bf16[2,8,128,128]{3,2,1,0:T(8,128)(2,1)} %refs_4_.2) | copy-start | bytes 1572868
  6.2 1.4 %copy-start = (f32[2,256,256]{2,1,0:T(8,128)S(1)}, f32[2,256,256]{2,1,0:T(8,128)}, u32[]{:S(2)}) copy-start(f32[2,256,256]{2,1,0:T(8,128)} %refs_6_.3) | copy-start | bytes 1572868
  6.8 6.7 %collective-permute-start.2 = (f32[256,256]{1,0:T(8,128)S(1)}, f32[256,256]{1,0:T(8,128)S(1)}, u32[]{:S(2)}, u32[]{:S(2)}) collective-permute-start(f32[256,256]{1,0:T(8,128)S(1)} %get-tuple-element.42.refs_0_), channel_id=1, source_target_pairs={{0,1},{1,0},{2,3},{3,2},{4,5},{5,4},{6,7},{7,6},{8,9},{9,8},{10,11... | collective-permute-start | bytes 786440 | tf_op jit(solution)/shard_map/core_swap/ppermute | solution.py:99
  8.2 5.3 %collective-permute-start.1 = (f32[128,256]{1,0:T(8,128)S(1)}, f32[128,256]{1,0:T(8,128)S(1)}, u32[]{:S(2)}, u32[]{:S(2)}) collective-permute-start(f32[128,256]{1,0:T(8,128)S(1)} %join.4.refs_0_.refs_4_), channel_id=1, source_target_pairs={{0,2},{1,3},{2,0},{3,1},{4,6},{5,7},{6,4},{7,5},{8,10},{9,11},{10,... | collective-permute-start | bytes 393224 | tf_op jit(solution)/shard_map/chip_swap/ppermute | solution.py:99
  8.4 7.9 %collective-permute-start.5 = (f32[128,256]{1,0:T(8,128)S(1)}, f32[128,256]{1,0:T(8,128)S(1)}, u32[]{:S(2)}, u32[]{:S(2)}) collective-permute-start(f32[128,256]{1,0:T(8,128)S(1)} %join.5.refs_1_.refs_4_), channel_id=1, source_target_pairs={{0,2},{1,3},{2,0},{3,1},{4,6},{5,7},{6,4},{7,5},{8,10},{9,11},{10,... | collective-permute-start | bytes 393224 | tf_op jit(solution)/shard_map/chip_swap/ppermute | solution.py:99
  12.6 12.4 %collective-permute-start.4 = (f32[1280,256]{1,0:T(8,128)S(1)}, f32[1280,256]{1,0:T(8,128)S(1)}, u32[]{:S(2)}, u32[]{:S(2)}) collective-permute-start(f32[1280,256]{1,0:T(8,128)S(1)} %get-tuple-element.53.refs_0_), channel_id=1, source_target_pairs={{0,1},{1,0},{2,3},{3,2},{4,5},{5,4},{6,7},{7,6},{8,9},{9,8},{10,11... | collective-permute-start | bytes 3932168 | tf_op jit(solution)/shard_map/core_swap/ppermute | solution.py:99
  13.5 4.6 %collective-permute-start.7 = (f32[128,256]{1,0:T(8,128)S(1)}, f32[128,256]{1,0:T(8,128)S(1)}, u32[]{:S(2)}, u32[]{:S(2)}) collective-permute-start(f32[128,256]{1,0:T(8,128)S(1)} %join.6.refs_3_), channel_id=1, source_target_pairs={{0,2},{1,3},{2,0},{3,1},{4,6},{5,7},{6,4},{7,5},{8,10},{9,11},{10,... | collective-permute-start | bytes 393224 | tf_op jit(solution)/shard_map/chip_swap/ppermute | solution.py:99
  13.8 11.3 %collective-permute-start.3 = (f32[128,256]{1,0:T(8,128)S(1)}, f32[128,256]{1,0:T(8,128)S(1)}, u32[]{:S(2)}, u32[]{:S(2)}) collective-permute-start(f32[128,256]{1,0:T(8,128)S(1)} %move.4.refs_2_.refs_0_), channel_id=1, source_target_pairs={{0,6},{1,7},{2,4},{3,5},{4,10},{5,11},{6,8},{7,9},{8,14},{9,15},{1... | collective-permute-start | bytes 393224 | tf_op jit(solution)/shard_map/onward/ppermute | solution.py:108
  16.3 4.8 %collective-permute-start.10 = (f32[128,256]{1,0:T(8,128)S(1)}, f32[128,256]{1,0:T(8,128)S(1)}, u32[]{:S(2)}, u32[]{:S(2)}) collective-permute-start(f32[128,256]{1,0:T(8,128)S(1)} %join.7.refs_4_), channel_id=1, source_target_pairs={{0,2},{1,3},{2,0},{3,1},{4,6},{5,7},{6,4},{7,5},{8,10},{9,11},{10,... | collective-permute-start | bytes 393224 | tf_op jit(solution)/shard_map/chip_swap/ppermute | solution.py:99
  16.6 11.8 %collective-permute-start.6 = (f32[128,256]{1,0:T(8,128)S(1)}, f32[128,256]{1,0:T(8,128)S(1)}, u32[]{:S(2)}, u32[]{:S(2)}) collective-permute-start(f32[128,256]{1,0:T(8,128)S(1)} %move.5.refs_0_), channel_id=1, source_target_pairs={{0,6},{1,7},{2,4},{3,5},{4,10},{5,11},{6,8},{7,9},{8,14},{9,15},{1... | collective-permute-start | bytes 393224 | tf_op jit(solution)/shard_map/onward/ppermute | solution.py:108
  18.2 15.2 %collective-permute-start.8 = (f32[128,256]{1,0:T(8,128)S(1)}, f32[128,256]{1,0:T(8,128)S(1)}, u32[]{:S(2)}, u32[]{:S(2)}) collective-permute-start(f32[128,256]{1,0:T(8,128)S(1)} %move.6.refs_0_), channel_id=1, source_target_pairs={{0,6},{1,7},{2,4},{3,5},{4,10},{5,11},{6,8},{7,9},{8,14},{9,15},{1... | collective-permute-start | bytes 393224 | tf_op jit(solution)/shard_map/onward/ppermute | solution.py:108
  21.1 13.3 %collective-permute-start.11 = (f32[128,256]{1,0:T(8,128)S(1)}, f32[128,256]{1,0:T(8,128)S(1)}, u32[]{:S(2)}, u32[]{:S(2)}) collective-permute-start(f32[128,256]{1,0:T(8,128)S(1)} %move.7), channel_id=1, source_target_pairs={{0,6},{1,7},{2,4},{3,5},{4,10},{5,11},{6,8},{7,9},{8,14},{9,15},{1... | collective-permute-start | bytes 393224 | tf_op jit(solution)/shard_map/onward/ppermute | solution.py:108
  25.9 8.3 %collective-permute-start.9 = (f32[128,256]{1,0:T(8,128)S(1)}, f32[128,256]{1,0:T(8,128)S(1)}, u32[]{:S(2)}, u32[]{:S(2)}) collective-permute-start(f32[128,256]{1,0:T(8,128)S(1)} %get-tuple-element.57.refs_0_), channel_id=1, source_target_pairs={{0,2},{1,3},{2,0},{3,1},{4,6},{5,7},{6,4},{7,5},{8,10},{9,11},{10,... | collective-permute-start | bytes 393224 | tf_op jit(solution)/shard_map/chip_swap/ppermute | solution.py:99
  29.3 7.5 %collective-permute-start.12 = (f32[128,256]{1,0:T(8,128)S(1)}, f32[128,256]{1,0:T(8,128)S(1)}, u32[]{:S(2)}, u32[]{:S(2)}) collective-permute-start(f32[128,256]{1,0:T(8,128)S(1)} %get-tuple-element.58.refs_0_), channel_id=1, source_target_pairs={{0,2},{1,3},{2,0},{3,1},{4,6},{5,7},{6,4},{7,5},{8,10},{9,11},{10,... | collective-permute-start | bytes 393224 | tf_op jit(solution)/shard_map/chip_swap/ppermute | solution.py:99
  29.9 7.0 %collective-permute-start.13 = (f32[256,256]{1,0:T(8,128)S(1)}, f32[256,256]{1,0:T(8,128)S(1)}, u32[]{:S(2)}, u32[]{:S(2)}) collective-permute-start(f32[256,256]{1,0:T(8,128)S(1)} %stack.3), channel_id=1, source_target_pairs={{0,1},{1,0},{2,3},{3,2},{4,5},{5,4},{6,7},{7,6},{8,9},{9,8},{10,11... | collective-permute-start | bytes 786440 | tf_op jit(solution)/shard_map/core_swap/ppermute | solution.py:99
  34.3 9.3 %collective-permute-start.15 = (f32[128,256]{1,0:T(8,128)S(1)}, f32[128,256]{1,0:T(8,128)S(1)}, u32[]{:S(2)}, u32[]{:S(2)}) collective-permute-start(f32[128,256]{1,0:T(8,128)S(1)} %add_scaled.2.refs_1_.refs_0_), channel_id=1, source_target_pairs={{0,6},{1,7},{2,4},{3,5},{4,10},{5,11},{6,8},{7,9},{8,14},{9,15},{1... | collective-permute-start | bytes 393224 | tf_op jit(solution)/shard_map/onward/ppermute | solution.py:108
  34.4 2.7 %collective-permute-start.14 = (f32[256,256]{1,0:T(8,128)S(1)}, f32[256,256]{1,0:T(8,128)S(1)}, u32[]{:S(2)}, u32[]{:S(2)}) collective-permute-start(f32[256,256]{1,0:T(8,128)S(1)} %stack.4), channel_id=1, source_target_pairs={{0,1},{1,0},{2,3},{3,2},{4,5},{5,4},{6,7},{7,6},{8,9},{9,8},{10,11... | collective-permute-start | bytes 786440 | tf_op jit(solution)/shard_map/core_swap/ppermute | solution.py:99
  36.8 10.3 %collective-permute-start.16 = (f32[128,256]{1,0:T(8,128)S(1)}, f32[128,256]{1,0:T(8,128)S(1)}, u32[]{:S(2)}, u32[]{:S(2)}) collective-permute-start(f32[128,256]{1,0:T(8,128)S(1)} %add_scaled.3.refs_1_), channel_id=1, source_target_pairs={{0,6},{1,7},{2,4},{3,5},{4,10},{5,11},{6,8},{7,9},{8,14},{9,15},{1... | collective-permute-start | bytes 393224 | tf_op jit(solution)/shard_map/onward/ppermute | solution.py:108

commit v5 on v4

--- a/solution.py
+++ b/solution.py
@@ -15,8 +15,9 @@
 AXES = ("blk", "grp")
 TILE = 128
 CHUNKS = 2
+SHARES = 3
 WEIGHT = 8
-COST = {"part": 2, "join": 0, "join_2": 16, "part_2": 2, "move": (4, 4, 4, 4), "user_step": 0, "layout": 0, "near": (2, 2), "far": (2, 2), "finish": 0, "last": 0, "final": 0}
+COST = {"part": 2, "join": 0, "join_2": 16, "part_2": 2, "move": (4, 4, 4, 4), "user_step": 0, "layout": 0, "near": (2, 2), "far": (2, 2), "finish": 0, "user_sums": 64, "last": 0, "final": 0}
 VMEM_LIMIT = 16 * 1024 * 1024
 
 NN = (((1,), (0,)), ((), ()))
@@ -148,10 +149,11 @@
               index_ref, count_ref, rating_in, weight_in, sems):
         copies = fetch(
             [(index_hbm, index_ref), (count_hbm, count_ref),
-             (rating_hbm.at[0], rating_in), (weight_hbm.at[0], weight_in),
-             (users_hbm, users_out), (items_hbm, items_out),
-             (noise_hbm.at[0, rows_of(place_ref, 2), :], noise_out.at[:quarter, :]),
-             (noise_hbm.at[0, rows_of(place_ref, 0), :], noise_out.at[quarter:, :])],
+             (rating_hbm.at[0], rating_in), (weight_hbm.at[0], weight_in), (users_hbm, users_out)]
+            + [(items_hbm.at[rows_of(place_ref, flip), :], items_out.at[rows_of(place_ref, flip), :])
+               for flip in (1, 0, 3, 2)]
+            + [(noise_hbm.at[0, rows_of(place_ref, 2), :], noise_out.at[:quarter, :]),
+               (noise_hbm.at[0, rows_of(place_ref, 0), :], noise_out.at[quarter:, :])],
             sems,
         )
         rating_out[...] = jnp.zeros_like(rating_out)
@@ -173,8 +175,8 @@
         grads_out[...] = quarter_terms(
             place_ref, 1, rating_out, weight_out, users_out, items_out, high_out, low_out
         )
-        copies[6].wait()
-        copies[7].wait()
+        for copy in copies[6:]:
+            copy.wait()
 
     part_outs = [(square, bf16)] * 2 + [((quarter, rank), f32)]
     rating_0, weight_0, users_0, items_0, noise_0, *errors_1, to_sibling = call(
@@ -182,7 +184,7 @@
         [(dense, bf16)] * 2 + [(users.shape, f32), (items.shape, f32), ((2 * quarter, rank), f32)] + part_outs,
         [place] + tables + [(DISTANT, v) for v in (users, items, noise_items)],
         2 * unit,
-        landing + [pltpu.SemaphoreType.DMA((8,))],
+        landing + [pltpu.SemaphoreType.DMA((11,))],
     )
     from_sibling_0 = swap(to_sibling, 1)
     stage_0 = [local(rating_0), local(weight_0), local(users_0), local(items_0)]
@@ -304,7 +306,7 @@
     ahead = [onward(value) for value in moved]
 
     def late(k, slot, place_ref, items_ref, users_ref, rating_ref, weight_ref, sibling_ref, *rest):
-        high_out, low_out, out = rest[-3:]
+        high_out, low_out, high_s_out, low_s_out, out = rest[-5:]
         own, other = halves(users_ref[...]), halves(sibling_ref[4 * quarter :, :])
         now = items_ref[...]
         item_halves = halves(now)
@@ -316,6 +318,7 @@
         rating = sibling_ref[at : at + chunk, :]
         weight = sibling_ref[2 * quarter + at : 2 * quarter + at + chunk, :]
         errors = errors_of(item_halves, other, rating, weight)
+        high_s_out[...], low_s_out[...] = errors
         total = total + product(errors, other, NN)
         if slot == 1:
             total = stepped(now, total, rest[0][rows(k), :])
@@ -323,7 +326,7 @@
 
     common = [local(v) for v in (users_1, rating_1, weight_1, from_sibling)]
     errors_shape = (chunk, owned)
-    late_outs = [(errors_shape, bf16)] * 2 + [(piece, f32)]
+    late_outs = [(errors_shape, bf16)] * 4 + [(piece, f32)]
     def relay(value_ref, out):
         out[...] = value_ref[...]
 
@@ -333,65 +336,66 @@
     here, there = ahead[:CHUNKS], ahead[CHUNKS:]
     errors_here, sent = [], []
     for k in range(CHUNKS):
-        high, low, value = call(
+        *errors, value = call(
             functools.partial(late, k, 0), late_outs, [place, local(here[k])] + common,
             COST["near"][k] * unit, after=sent[-1:],
         )
-        errors_here.append((high, low))
+        errors_here.append(errors)
         sent.append(value)
     received = [swap(value, 2) for value in sent]
     errors_there, finished = [], []
     for k in range(CHUNKS):
-        high, low, value = call(
+        *errors, value = call(
             functools.partial(late, k, 1), late_outs,
             [place, local(there[k])] + common + [local(noise_1)], COST["far"][k] * unit,
             after=[sent[-1], *finished[-1:]],
         )
-        errors_there.append((high, low))
+        errors_there.append(errors)
         finished += joined(add_scaled, rows(0), value, received[k], COST["finish"], [])
     final = [onward(value) for value in finished]
 
     def stack(*refs):
         for k in range(CHUNKS):
             refs[-1][rows(k), :] = refs[k][...]
-
-    def paired(values, after):
-        [value] = call(stack, [((quarter, rank), f32)], [local(v) for v in values], 1, after=after)
-        return swap(value, 1)
-
-    here_s, there_s = paired(here, sent[-1:]), paired(there, finished[:1])
-
-    def last(place_ref, rating_ref, weight_ref, users_ref, noise_hbm, *rest):
-        known, blocks = rest[: 6 * CHUNKS], rest[6 * CHUNKS : 6 * CHUNKS + 2]
-        users_out, token, noise, sems = rest[6 * CHUNKS + 2 :]
-        token[...] = jnp.zeros_like(token)
-        [copy] = fetch([(noise_hbm.at[1], noise)], sems)
-        user_halves = halves(users_ref[...])
-        total = jnp.zeros((owned, rank), f32)
-        for n in range(2 * CHUNKS):
-            errors = (known[3 * n][...], known[3 * n + 1][...])
-            total = total + product(errors, halves(known[3 * n + 2][...]), TN)
-        for block, flip in zip(blocks, (1, 3)):
-            at = rows_of(place_ref, flip)
-            item_halves = halves(block[...])
-            errors = errors_of(item_halves, user_halves, rating_ref[at, :], weight_ref[at, :])
-            total = total + product(errors, item_halves, TN)
-        copy.wait()
-        users_out[...] = stepped(users_ref[...], total, noise[...])
 
     known = [
         local(v)
         for errors, values in zip(errors_here + errors_there, here + there)
         for v in (*errors, values)
     ]
+    step = -(-owned // (8 * SHARES)) * 8
+    shares_at = [slice(n * step, min((n + 1) * step, owned)) for n in range(SHARES)]
+
+    def user_sums(*refs):
+        own = other = jnp.zeros((owned, rank), f32)
+        for n in range(2 * CHUNKS):
+            high, low, high_s, low_s, values = (ref[...] for ref in refs[5 * n : 5 * n + 5])
+            item_halves = halves(values)
+            own = own + product((high, low), item_halves, TN)
+            other = other + product((high_s, low_s), item_halves, TN)
+        refs[10 * CHUNKS][...] = own
+        for n, ref in enumerate(refs[10 * CHUNKS + 1 :]):
+            ref[...] = other[shares_at[n], :]
+
+    sums, *to_sibling = call(
+        user_sums, [(users.shape, f32)] + [((at.stop - at.start, rank), f32) for at in shares_at],
+        known, COST["user_sums"] * unit,
+        after=finished,
+    )
+    from_sibling = [swap(value, 1) for value in to_sibling]
+
+    def last(users_ref, sums_ref, noise_ref, *rest):
+        shares, (users_out, token) = rest[:SHARES], rest[SHARES:]
+        token[...] = jnp.zeros_like(token)
+        for at, ref in zip(shares_at, shares):
+            total = sums_ref[at, :] + ref[...]
+            users_out[at, :] = stepped(users_ref[at, :], total, noise_ref[at, :])
+
     users_out, token = call(
         last,
         [(users.shape, f32), ((8, 128), f32)],
-        [place, local(rating_1), local(weight_1), local(users_1), (DISTANT, noise_users)]
-        + known + [local(here_s), local(there_s)],
+        [local(users_1), local(sums), local(noise_users[1])] + [local(v) for v in from_sibling],
         COST["last"] * unit,
-        [pltpu.VMEM(users.shape, f32), pltpu.SemaphoreType.DMA((1,))],
-        after=finished,
     )
 
     [early] = relayed(final[0], COST["final"], [token])

time: 48.1 us -> 46.3 us (0.963)
  starting transfers between devices: 17.9 us -> 15.7 us
  waiting for transfers between devices: 15.6 us -> 16.6 us
  Pallas kernels: 12.9 us -> 12.2 us
    ppermute x11 -> x12, starting transfers between devices: 12.5 us -> 10.2 us  [swap(): return lax.ppermute(value, AXES, pairs)]
    pallas_call x25 -> x24, Pallas kernels: 12.9 us -> 12.2 us  [call(): pl.pallas_call(kernel, in_specs=[AFTER] * unread + [spec for spec, _ in o...]
    ppermute x11 -> x12, waiting for transfers between devices: 2.81 us -> 3.39 us  [swap(): return lax.ppermute(value, AXES, pairs)]
  transfers between devices with their start and end apart: 17 -> 18, of which waited for: 8 -> 10; matrix products, arithmetic and copies ran while one was open for 0% -> 0% of each run, Pallas kernels for 21% -> 21%
where the time goes in v5:
time: 46.3 us
  waiting for transfers between devices  16.6 us (36%)
  starting transfers between devices  15.7 us (34%)
  Pallas kernels  12.2 us (26%)
  local copies, waits for them, and re-layouts  1.02 us (2%)
  between operations  0.86 us (2%)
    ppermute x6, waiting for transfers between devices, onward(): return lax.ppermute(value, AXES, pairs)  13.2 us
    pallas_call x24, Pallas kernels, call(): pl.pallas_call(kernel, in_specs=[AFTER] * unread + [spec for spec, _ in o...  12.2 us
    ppermute x12, starting transfers between devices, swap(): return lax.ppermute(value, AXES, pairs)  10.2 us
    ppermute x6, starting transfers between devices, onward(): return lax.ppermute(value, AXES, pairs)  5.52 us
    ppermute x12, waiting for transfers between devices, swap(): return lax.ppermute(value, AXES, pairs)  3.39 us
    unnamed x6, local copies, waits for them, and re-layouts  0.94 us
  transfers between devices with their start and end apart: 18, of which 10 were waited for; matrix products, arithmetic and copies ran while one was open for 0% of the time, Pallas kernels for 21%

profile of v5, /device:TPU:1, one launch (start us, length us, event | category | flops | bytes accessed | tf_op | source)
XLA Modules:
  0.0 46.3 jit_solution(13995629513016853637)
XLA Ops:
  0.6 1.9 %first.1 = (bf16[8,256,128]{2,1,0:T(8,128)(2,1)S(1)}, bf16[8,256,128]{2,1,0:T(8,128)(2,1)S(1)}, f32[256,256]{1,0:T(8,128)S(1)}, f32[1024,256]{1,0:T(8,128)S(1)},...) custom-call(s32[1]{0:T(128)} %bitcast.refs_0_.refs_1_.refs_2_, ...), custom_call_target="tpu_custom_call" | custom-call | flops 1610612736 | bytes 262144 | tf_op jit(solution)/shard_map/first/pallas_call | solution.py:62
  2.6 3.3 %collective-permute-start = (f32[256,256]{1,0:T(8,128)S(1)}, f32[256,256]{1,0:T(8,128)S(1)}, u32[]{:S(2)}, u32[]{:S(2)}) collective-permute-start(f32[256,256]{1,0:T(8,128)S(1)} %get-tuple-element.59), channel_id=1, source_target_pairs={{0,1},{1,0},{2,3},{3,2},{4,5},{5,4},{6,7},{7,6},{8,9},{9,8},{10,11... | collective-permute-start | bytes 786440 | tf_op jit(solution)/shard_map/core_swap/ppermute | solution.py:100
  5.9 0.6 %part.3 = (bf16[256,256]{1,0:T(8,128)(2,1)S(1)}, bf16[256,256]{1,0:T(8,128)(2,1)S(1)}, f32[256,256]{1,0:T(8,128)S(1)}) custom-call(s32[1]{0:T(128)} %bitcast.refs_0_.refs_1_.refs_2_, bf16[8,256,128]{2,1,0:T(8,128)(2,1)S(1)} %get-tuple-element.51.refs_1_.refs_2_.refs_3_, bf16[8,256,128]{2,1,0:T(8,128)(2,1)S(1)} %get-tuple-element.52.refs_2_.refs_3_.refs_4_, ...), custom_call_target="tpu_custom_call" | custom-call | flops 1610612736 | bytes 262144 | tf_op jit(solution)/shard_map/part/pallas_call | solution.py:62
  6.6 0.0 copy-start
  6.6 0.1 collective-permute-start.2
  6.7 0.3 copy-done.1
  7.0 0.2 copy-done.2
  7.2 0.5 %copy-done = f32[2,256,256]{2,1,0:T(8,128)S(1)} copy-done((f32[2,256,256]{2,1,0:T(8,128)S(1)}, f32[2,256,256]{2,1,0:T(8,128)}, u32[]{:S(2)}) %copy-start) | copy-done | bytes 524312
  7.7 0.6 %part.4 = (bf16[256,256]{1,0:T(8,128)(2,1)S(1)}, bf16[256,256]{1,0:T(8,128)(2,1)S(1)}, f32[256,256]{1,0:T(8,128)S(1)}) custom-call(f32[256,256]{1,0:T(8,128)S(1)} %get-tuple-element.53.refs_0_, s32[1]{0:T(128)} %bitcast.refs_0_.refs_1_.refs_2_, bf16[8,256,128]{2,1,0:T(8,128)(2,1)S(1)} %get-tuple-element.51.refs_1_.refs_2_.refs_3_, ...), custom_call_target="tpu_custom_call" | custom-call | flops 1610612736 | bytes 262144 | tf_op jit(solution)/shard_map/part/pallas_call | solution.py:62
  8.4 0.0 collective-permute-done.refs_1_.refs_2_
  8.4 0.1 collective-permute-start.1
  8.5 1.5 %collective-permute-start.5 = (f32[128,256]{1,0:T(8,128)S(1)}, f32[128,256]{1,0:T(8,128)S(1)}, u32[]{:S(2)}, u32[]{:S(2)}) collective-permute-start(f32[128,256]{1,0:T(8,128)S(1)} %join.5.refs_1_.refs_4_), channel_id=1, source_target_pairs={{0,2},{1,3},{2,0},{3,1},{4,6},{5,7},{6,4},{7,5},{8,10},{9,11},{10,... | collective-permute-start | bytes 393224 | tf_op jit(solution)/shard_map/chip_swap/ppermute | solution.py:100
  10.1 0.6 %part.5 = (bf16[256,256]{1,0:T(8,128)(2,1)S(1)}, bf16[256,256]{1,0:T(8,128)(2,1)S(1)}, f32[256,256]{1,0:T(8,128)S(1)}) custom-call(f32[128,256]{1,0:T(8,128)S(1)} %join.4.refs_0_.refs_4_, f32[128,256]{1,0:T(8,128)S(1)} %join.5.refs_1_.refs_4_, s32[1]{0:T(128)} %bitcast.refs_0_.refs_1_.refs_2_, ...), custom_call_target="tpu_custom_call" | custom-call | flops 1610612736 | bytes 262144 | tf_op jit(solution)/shard_map/part/pallas_call | solution.py:62
  10.7 0.7 %user_step.1.refs_0_.refs_7_.refs_2_.refs_3_.refs_4_ = f32[256,256]{1,0:T(8,128)S(1)} custom-call(s32[1]{0:T(128)} %bitcast.refs_0_.refs_1_.refs_2_, f32[256,256]{1,0:T(8,128)S(1)} %get-tuple-element.49.refs_3_.refs_4_.refs_5_.refs_1_, f32[1024,256]{1,0:T(8,128)S(1)} %get-tuple-element.50.refs_4_.refs_5_.refs_6_.refs_2_.refs_1_, ...), custom_call_target="tpu_custom_call" | custom-call | bytes 262144 | tf_op jit(solution)/shard_map/user_step/pallas_call | solution.py:62
  11.4 1.4 %layout.1 = (f32[1024,256]{1,0:T(8,128)S(1)}, f32[1024,256]{1,0:T(8,128)S(1)}, f32[1280,256]{1,0:T(8,128)S(1)}, f32[256,256]{1,0:T(8,128)S(1)}) custom-call(f32[256,256]{1,0:T(8,128)S(1)} %user_step.1.refs_0_.refs_7_.refs_2_.refs_3_.refs_4_, s32[1]{0:T(128)} %bitcast.refs_0_.refs_1_.refs_2_, s32[2,8]{1,0:T(2,128)} %refs_2_.1, s32[2]{0:T(128)} %bitcast.11, ...), custom_call_target="tpu_custom_call" | custom-call | bytes 262144 | tf_op jit(solution)/shard_map/layout/pallas_call | solution.py:62
  12.8 0.8 %collective-permute-start.4 = (f32[1280,256]{1,0:T(8,128)S(1)}, f32[1280,256]{1,0:T(8,128)S(1)}, u32[]{:S(2)}, u32[]{:S(2)}) collective-permute-start(f32[1280,256]{1,0:T(8,128)S(1)} %get-tuple-element.65.refs_0_), channel_id=1, source_target_pairs={{0,1},{1,0},{2,3},{3,2},{4,5},{5,4},{6,7},{7,6},{8,9},{9,8},{10,11... | collective-permute-start | bytes 3932168 | tf_op jit(solution)/shard_map/core_swap/ppermute | solution.py:100
  13.6 0.0 collective-permute-done.2.refs_3_.refs_4_
  13.6 0.0 collective-permute-done.1.refs_1_.refs_4_
  13.6 0.3 collective-permute-start.7
  13.9 1.3 %collective-permute-start.3 = (f32[128,256]{1,0:T(8,128)S(1)}, f32[128,256]{1,0:T(8,128)S(1)}, u32[]{:S(2)}, u32[]{:S(2)}) collective-permute-start(f32[128,256]{1,0:T(8,128)S(1)} %move.4.refs_2_.refs_0_), channel_id=1, source_target_pairs={{0,6},{1,7},{2,4},{3,5},{4,10},{5,11},{6,8},{7,9},{8,14},{9,15},{1... | collective-permute-start | bytes 393224 | tf_op jit(solution)/shard_map/onward/ppermute | solution.py:109
  15.2 1.2 %collective-permute-done.5.refs_1_.refs_5_ = f32[128,256]{1,0:T(8,128)S(1)} collective-permute-done((f32[128,256]{1,0:T(8,128)S(1)}, f32[128,256]{1,0:T(8,128)S(1)}, u32[]{:S(2)}, u32[]{:S(2)}) %collective-permute-start.5) | collective-permute-done | bytes 131104 | tf_op jit(solution)/shard_map/chip_swap/ppermute | solution.py:100
  16.4 0.3 collective-permute-start.10
  16.8 1.2 %collective-permute-start.6 = (f32[128,256]{1,0:T(8,128)S(1)}, f32[128,256]{1,0:T(8,128)S(1)}, u32[]{:S(2)}, u32[]{:S(2)}) collective-permute-start(f32[128,256]{1,0:T(8,128)S(1)} %move.5.refs_0_), channel_id=1, source_target_pairs={{0,6},{1,7},{2,4},{3,5},{4,10},{5,11},{6,8},{7,9},{8,14},{9,15},{1... | collective-permute-start | bytes 393224 | tf_op jit(solution)/shard_map/onward/ppermute | solution.py:109
  17.9 0.4 collective-permute-done.7.refs_5_
  18.3 1.9 %collective-permute-start.8 = (f32[128,256]{1,0:T(8,128)S(1)}, f32[128,256]{1,0:T(8,128)S(1)}, u32[]{:S(2)}, u32[]{:S(2)}) collective-permute-start(f32[128,256]{1,0:T(8,128)S(1)} %move.6.refs_0_), channel_id=1, source_target_pairs={{0,6},{1,7},{2,4},{3,5},{4,10},{5,11},{6,8},{7,9},{8,14},{9,15},{1... | collective-permute-start | bytes 393224 | tf_op jit(solution)/shard_map/onward/ppermute | solution.py:109
  20.3 0.9 %collective-permute-done.10.refs_5_ = f32[128,256]{1,0:T(8,128)S(1)} collective-permute-done((f32[128,256]{1,0:T(8,128)S(1)}, f32[128,256]{1,0:T(8,128)S(1)}, u32[]{:S(2)}, u32[]{:S(2)}) %collective-permute-start.10) | collective-permute-done | bytes 131104 | tf_op jit(solution)/shard_map/chip_swap/ppermute | solution.py:100
  21.2 1.0 %collective-permute-start.11 = (f32[128,256]{1,0:T(8,128)S(1)}, f32[128,256]{1,0:T(8,128)S(1)}, u32[]{:S(2)}, u32[]{:S(2)}) collective-permute-start(f32[128,256]{1,0:T(8,128)S(1)} %move.7), channel_id=1, source_target_pairs={{0,6},{1,7},{2,4},{3,5},{4,10},{5,11},{6,8},{7,9},{8,14},{9,15},{1... | collective-permute-start | bytes 393224 | tf_op jit(solution)/shard_map/onward/ppermute | solution.py:109
  22.2 3.1 %collective-permute-done.3.refs_1_.refs_6_ = f32[128,256]{1,0:T(8,128)S(1)} collective-permute-done((f32[128,256]{1,0:T(8,128)S(1)}, f32[128,256]{1,0:T(8,128)S(1)}, u32[]{:S(2)}, u32[]{:S(2)}) %collective-permute-start.3) | collective-permute-done | bytes 131104 | tf_op jit(solution)/shard_map/onward/ppermute | solution.py:109
  25.3 0.9 %late.4 = (bf16[128,256]{1,0:T(8,128)(2,1)S(1)}, bf16[128,256]{1,0:T(8,128)(2,1)S(1)}, bf16[128,256]{1,0:T(8,128)(2,1)S(1)}, bf16[128,256]{1,0:T(8,128)(2,1)S(1)}, f32[128,256]{1,0:T(8,128)S(1)}) custom-call(s32[1]{0:T(128)} %bitcast.refs_0_.refs_1_.refs_2_, f32[128,256]{1,0:T(8,128)S(1)} %collective-permute-done.3.refs_1_.refs_6_, ...), custom_call_target="tpu_custom_call" | custom-call | flops 1610612736 | bytes 262144 | tf_op jit(solution)/shard_map/late/pallas_call | solution.py:62
  26.2 0.3 collective-permute-start.9
  26.5 2.2 %collective-permute-done.6.refs_2_.refs_11_ = f32[128,256]{1,0:T(8,128)S(1)} collective-permute-done((f32[128,256]{1,0:T(8,128)S(1)}, f32[128,256]{1,0:T(8,128)S(1)}, u32[]{:S(2)}, u32[]{:S(2)}) %collective-permute-start.6) | collective-permute-done | bytes 131104 | tf_op jit(solution)/shard_map/onward/ppermute | solution.py:109
  28.7 0.9 %late.5 = (bf16[128,256]{1,0:T(8,128)(2,1)S(1)}, bf16[128,256]{1,0:T(8,128)(2,1)S(1)}, bf16[128,256]{1,0:T(8,128)(2,1)S(1)}, bf16[128,256]{1,0:T(8,128)(2,1)S(1)}, f32[128,256]{1,0:T(8,128)S(1)}) custom-call(f32[128,256]{1,0:T(8,128)S(1)} %get-tuple-element.69.refs_0_, s32[1]{0:T(128)} %bitcast.refs_0_.refs_1_.refs_2_, ...), custom_call_target="tpu_custom_call" | custom-call | flops 1610612736 | bytes 262144 | tf_op jit(solution)/shard_map/late/pallas_call | solution.py:62
  29.6 0.3 collective-permute-start.12
  29.8 1.7 %collective-permute-done.8.refs_2_.refs_16_ = f32[128,256]{1,0:T(8,128)S(1)} collective-permute-done((f32[128,256]{1,0:T(8,128)S(1)}, f32[128,256]{1,0:T(8,128)S(1)}, u32[]{:S(2)}, u32[]{:S(2)}) %collective-permute-start.8) | collective-permute-done | bytes 131104 | tf_op jit(solution)/shard_map/onward/ppermute | solution.py:109
  31.5 0.9 %late.6 = (bf16[128,256]{1,0:T(8,128)(2,1)S(1)}, bf16[128,256]{1,0:T(8,128)(2,1)S(1)}, bf16[128,256]{1,0:T(8,128)(2,1)S(1)}, bf16[128,256]{1,0:T(8,128)(2,1)S(1)}, f32[128,256]{1,0:T(8,128)S(1)}) custom-call(f32[128,256]{1,0:T(8,128)S(1)} %get-tuple-element.70.refs_0_, s32[1]{0:T(128)} %bitcast.refs_0_.refs_1_.refs_2_, ...), custom_call_target="tpu_custom_call" | custom-call | flops 1610612736 | bytes 262144 | tf_op jit(solution)/shard_map/late/pallas_call | solution.py:62
  32.4 0.1 collective-permute-start.16
  32.5 1.8 %collective-permute-done.11.refs_3_.refs_21_ = f32[128,256]{1,0:T(8,128)S(1)} collective-permute-done((f32[128,256]{1,0:T(8,128)S(1)}, f32[128,256]{1,0:T(8,128)S(1)}, u32[]{:S(2)}, u32[]{:S(2)}) %collective-permute-start.11) | collective-permute-done | bytes 131104 | tf_op jit(solution)/shard_map/onward/ppermute | solution.py:109
  34.3 0.9 %late.7 = (bf16[128,256]{1,0:T(8,128)(2,1)S(1)}, bf16[128,256]{1,0:T(8,128)(2,1)S(1)}, bf16[128,256]{1,0:T(8,128)(2,1)S(1)}, bf16[128,256]{1,0:T(8,128)(2,1)S(1)}, f32[128,256]{1,0:T(8,128)S(1)}) custom-call(f32[128,256]{1,0:T(8,128)S(1)} %get-tuple-element.70.refs_0_, f32[128,256]{1,0:T(8,128)S(1)} %add_scaled.2.refs_1_.refs_0_, ...), custom_call_target="tpu_custom_call" | custom-call | flops 1610612736 | bytes 262144 | tf_op jit(solution)/shard_map/late/pallas_call | solution.py:62
  35.2 0.1 collective-permute-start.17
  35.3 1.0 %user_sums.1 = (f32[256,256]{1,0:T(8,128)S(1)}, f32[88,256]{1,0:T(8,128)S(1)}, f32[88,256]{1,0:T(8,128)S(1)}, f32[80,256]{1,0:T(8,128)S(1)}) custom-call(f32[128,256]{1,0:T(8,128)S(1)} %add_scaled.2.refs_1_.refs_0_, f32[128,256]{1,0:T(8,128)S(1)} %add_scaled.3.refs_1_, bf16[128,256]{1,0:T(8,128)(2,1)S(1)} %get-tuple-element.74.refs_2_, ...), custom_call_target="tpu_custom_call" | custom-call | flops 51539607552 | bytes 262144 | tf_op jit(solution)/shard_map/user_sums/pallas_call | solution.py:62
  36.3 2.7 %collective-permute-start.13 = (f32[88,256]{1,0:T(8,128)S(1)}, f32[88,256]{1,0:T(8,128)S(1)}, u32[]{:S(2)}, u32[]{:S(2)}) collective-permute-start(f32[88,256]{1,0:T(8,128)S(1)} %get-tuple-element.91), channel_id=1, source_target_pairs={{0,1},{1,0},{2,3},{3,2},{4,5},{5,4},{6,7},{7,6},{8,9},{9,8},{10,11... | collective-permute-start | bytes 270344 | tf_op jit(solution)/shard_map/core_swap/ppermute | solution.py:100
  39.0 0.1 collective-permute-start.14
  39.1 0.4 collective-permute-start.15
  39.5 0.9 %collective-permute-done.15.refs_5_ = f32[80,256]{1,0:T(8,128)S(1)} collective-permute-done((f32[80,256]{1,0:T(8,128)S(1)}, f32[80,256]{1,0:T(8,128)S(1)}, u32[]{:S(2)}, u32[]{:S(2)}) %collective-permute-start.15) | collective-permute-done | bytes 81952 | tf_op jit(solution)/shard_map/core_swap/ppermute | solution.py:100
  40.5 0.8 %last.1 = (f32[256,256]{1,0:T(8,128)}, f32[8,128]{1,0:T(8,128)S(1)}) custom-call(f32[256,256]{1,0:T(8,128)S(1)} %user_step.1.refs_0_.refs_7_.refs_2_.refs_3_.refs_4_, f32[256,256]{1,0:T(8,128)S(1)} %get-tuple-element.90.refs_1_, f32[256,256]{1,0:T(8,128)S(1)} %get-tuple-element.96.refs_2_, f32[88,256]{1,0:T(8,128)S(1)} %collective-permute-done.13.refs_3_, ...), custom_call_target="tpu_custom_call" | custom-call | bytes 262144 | tf_op jit(solution)/shard_map/last/pallas_call | solution.py:62
  41.2 0.5 %collective-permute-done.16.refs_1_ = f32[128,256]{1,0:T(8,128)S(1)} collective-permute-done((f32[128,256]{1,0:T(8,128)S(1)}, f32[128,256]{1,0:T(8,128)S(1)}, u32[]{:S(2)}, u32[]{:S(2)}) %collective-permute-start.16) | collective-permute-done | bytes 131104 | tf_op jit(solution)/shard_map/onward/ppermute | solution.py:109
  41.8 3.9 %collective-permute-done.17.refs_1_ = f32[128,256]{1,0:T(8,128)S(1)} collective-permute-done((f32[128,256]{1,0:T(8,128)S(1)}, f32[128,256]{1,0:T(8,128)S(1)}, u32[]{:S(2)}, u32[]{:S(2)}) %collective-permute-start.17) | collective-permute-done | bytes 131104 | tf_op jit(solution)/shard_map/onward/ppermute | solution.py:109
  45.6 0.7 %stack.1 = f32[256,256]{1,0:T(8,128)} custom-call(f32[128,256]{1,0:T(8,128)S(1)} %relay.1.refs_0_, f32[128,256]{1,0:T(8,128)S(1)} %collective-permute-done.17.refs_1_), custom_call_target="tpu_custom_call" | custom-call | flops 8 | bytes 262144 | tf_op jit(solution)/shard_map/stack/pallas_call | solution.py:62
  (20 shorter events, 0.4 us)
Async XLA Ops:
  2.6 5.8 %collective-permute-start = (f32[256,256]{1,0:T(8,128)S(1)}, f32[256,256]{1,0:T(8,128)S(1)}, u32[]{:S(2)}, u32[]{:S(2)}) collective-permute-start(f32[256,256]{1,0:T(8,128)S(1)} %get-tuple-element.59), channel_id=1, source_target_pairs={{0,1},{1,0},{2,3},{3,2},{4,5},{5,4},{6,7},{7,6},{8,9},{9,8},{10,11... | collective-permute-start | bytes 786440 | tf_op jit(solution)/shard_map/core_swap/ppermute | solution.py:100
  5.9 1.0 %copy-start.1 = (bf16[2,8,128,128]{3,2,1,0:T(8,128)(2,1)S(1)}, bf16[2,8,128,128]{3,2,1,0:T(8,128)(2,1)}, u32[]{:S(2)}) copy-start(bf16[2,8,128,128]{3,2,1,0:T(8,128)(2,1)} %refs_3_.1) | copy-start | bytes 1572868
  5.9 1.2 %copy-start.2 = (bf16[2,8,128,128]{3,2,1,0:T(8,128)(2,1)S(1)}, bf16[2,8,128,128]{3,2,1,0:T(8,128)(2,1)}, u32[]{:S(2)}) copy-start(bf16[2,8,128,128]{3,2,1,0:T(8,128)(2,1)} %refs_4_.2) | copy-start | bytes 1572868
  6.6 1.1 %copy-start = (f32[2,256,256]{2,1,0:T(8,128)S(1)}, f32[2,256,256]{2,1,0:T(8,128)}, u32[]{:S(2)}) copy-start(f32[2,256,256]{2,1,0:T(8,128)} %param.10) | copy-start | bytes 1572868
  6.6 7.0 %collective-permute-start.2 = (f32[256,256]{1,0:T(8,128)S(1)}, f32[256,256]{1,0:T(8,128)S(1)}, u32[]{:S(2)}, u32[]{:S(2)}) collective-permute-start(f32[256,256]{1,0:T(8,128)S(1)} %get-tuple-element.53.refs_0_), channel_id=1, source_target_pairs={{0,1},{1,0},{2,3},{3,2},{4,5},{5,4},{6,7},{7,6},{8,9},{9,8},{10,11... | collective-permute-start | bytes 786440 | tf_op jit(solution)/shard_map/core_swap/ppermute | solution.py:100
  8.4 5.2 %collective-permute-start.1 = (f32[128,256]{1,0:T(8,128)S(1)}, f32[128,256]{1,0:T(8,128)S(1)}, u32[]{:S(2)}, u32[]{:S(2)}) collective-permute-start(f32[128,256]{1,0:T(8,128)S(1)} %join.4.refs_0_.refs_4_), channel_id=1, source_target_pairs={{0,2},{1,3},{2,0},{3,1},{4,6},{5,7},{6,4},{7,5},{8,10},{9,11},{10,... | collective-permute-start | bytes 393224 | tf_op jit(solution)/shard_map/chip_swap/ppermute | solution.py:100
  8.5 7.9 %collective-permute-start.5 = (f32[128,256]{1,0:T(8,128)S(1)}, f32[128,256]{1,0:T(8,128)S(1)}, u32[]{:S(2)}, u32[]{:S(2)}) collective-permute-start(f32[128,256]{1,0:T(8,128)S(1)} %join.5.refs_1_.refs_4_), channel_id=1, source_target_pairs={{0,2},{1,3},{2,0},{3,1},{4,6},{5,7},{6,4},{7,5},{8,10},{9,11},{10,... | collective-permute-start | bytes 393224 | tf_op jit(solution)/shard_map/chip_swap/ppermute | solution.py:100
  12.8 12.5 %collective-permute-start.4 = (f32[1280,256]{1,0:T(8,128)S(1)}, f32[1280,256]{1,0:T(8,128)S(1)}, u32[]{:S(2)}, u32[]{:S(2)}) collective-permute-start(f32[1280,256]{1,0:T(8,128)S(1)} %get-tuple-element.65.refs_0_), channel_id=1, source_target_pairs={{0,1},{1,0},{2,3},{3,2},{4,5},{5,4},{6,7},{7,6},{8,9},{9,8},{10,11... | collective-permute-start | bytes 3932168 | tf_op jit(solution)/shard_map/core_swap/ppermute | solution.py:100
  13.6 4.7 %collective-permute-start.7 = (f32[128,256]{1,0:T(8,128)S(1)}, f32[128,256]{1,0:T(8,128)S(1)}, u32[]{:S(2)}, u32[]{:S(2)}) collective-permute-start(f32[128,256]{1,0:T(8,128)S(1)} %join.6.refs_3_), channel_id=1, source_target_pairs={{0,2},{1,3},{2,0},{3,1},{4,6},{5,7},{6,4},{7,5},{8,10},{9,11},{10,... | collective-permute-start | bytes 393224 | tf_op jit(solution)/shard_map/chip_swap/ppermute | solution.py:100
  13.9 11.4 %collective-permute-start.3 = (f32[128,256]{1,0:T(8,128)S(1)}, f32[128,256]{1,0:T(8,128)S(1)}, u32[]{:S(2)}, u32[]{:S(2)}) collective-permute-start(f32[128,256]{1,0:T(8,128)S(1)} %move.4.refs_2_.refs_0_), channel_id=1, source_target_pairs={{0,6},{1,7},{2,4},{3,5},{4,10},{5,11},{6,8},{7,9},{8,14},{9,15},{1... | collective-permute-start | bytes 393224 | tf_op jit(solution)/shard_map/onward/ppermute | solution.py:109
  16.4 4.8 %collective-permute-start.10 = (f32[128,256]{1,0:T(8,128)S(1)}, f32[128,256]{1,0:T(8,128)S(1)}, u32[]{:S(2)}, u32[]{:S(2)}) collective-permute-start(f32[128,256]{1,0:T(8,128)S(1)} %join.7.refs_4_), channel_id=1, source_target_pairs={{0,2},{1,3},{2,0},{3,1},{4,6},{5,7},{6,4},{7,5},{8,10},{9,11},{10,... | collective-permute-start | bytes 393224 | tf_op jit(solution)/shard_map/chip_swap/ppermute | solution.py:100
  16.8 11.9 %collective-permute-start.6 = (f32[128,256]{1,0:T(8,128)S(1)}, f32[128,256]{1,0:T(8,128)S(1)}, u32[]{:S(2)}, u32[]{:S(2)}) collective-permute-start(f32[128,256]{1,0:T(8,128)S(1)} %move.5.refs_0_), channel_id=1, source_target_pairs={{0,6},{1,7},{2,4},{3,5},{4,10},{5,11},{6,8},{7,9},{8,14},{9,15},{1... | collective-permute-start | bytes 393224 | tf_op jit(solution)/shard_map/onward/ppermute | solution.py:109
  18.3 13.2 %collective-permute-start.8 = (f32[128,256]{1,0:T(8,128)S(1)}, f32[128,256]{1,0:T(8,128)S(1)}, u32[]{:S(2)}, u32[]{:S(2)}) collective-permute-start(f32[128,256]{1,0:T(8,128)S(1)} %move.6.refs_0_), channel_id=1, source_target_pairs={{0,6},{1,7},{2,4},{3,5},{4,10},{5,11},{6,8},{7,9},{8,14},{9,15},{1... | collective-permute-start | bytes 393224 | tf_op jit(solution)/shard_map/onward/ppermute | solution.py:109
  21.2 13.1 %collective-permute-start.11 = (f32[128,256]{1,0:T(8,128)S(1)}, f32[128,256]{1,0:T(8,128)S(1)}, u32[]{:S(2)}, u32[]{:S(2)}) collective-permute-start(f32[128,256]{1,0:T(8,128)S(1)} %move.7), channel_id=1, source_target_pairs={{0,6},{1,7},{2,4},{3,5},{4,10},{5,11},{6,8},{7,9},{8,14},{9,15},{1... | collective-permute-start | bytes 393224 | tf_op jit(solution)/shard_map/onward/ppermute | solution.py:109
  26.2 6.2 %collective-permute-start.9 = (f32[128,256]{1,0:T(8,128)S(1)}, f32[128,256]{1,0:T(8,128)S(1)}, u32[]{:S(2)}, u32[]{:S(2)}) collective-permute-start(f32[128,256]{1,0:T(8,128)S(1)} %get-tuple-element.69.refs_0_), channel_id=1, source_target_pairs={{0,2},{1,3},{2,0},{3,1},{4,6},{5,7},{6,4},{7,5},{8,10},{9,11},{10,... | collective-permute-start | bytes 393224 | tf_op jit(solution)/shard_map/chip_swap/ppermute | solution.py:100
  29.6 5.6 %collective-permute-start.12 = (f32[128,256]{1,0:T(8,128)S(1)}, f32[128,256]{1,0:T(8,128)S(1)}, u32[]{:S(2)}, u32[]{:S(2)}) collective-permute-start(f32[128,256]{1,0:T(8,128)S(1)} %get-tuple-element.70.refs_0_), channel_id=1, source_target_pairs={{0,2},{1,3},{2,0},{3,1},{4,6},{5,7},{6,4},{7,5},{8,10},{9,11},{10,... | collective-permute-start | bytes 393224 | tf_op jit(solution)/shard_map/chip_swap/ppermute | solution.py:100
  32.4 9.3 %collective-permute-start.16 = (f32[128,256]{1,0:T(8,128)S(1)}, f32[128,256]{1,0:T(8,128)S(1)}, u32[]{:S(2)}, u32[]{:S(2)}) collective-permute-start(f32[128,256]{1,0:T(8,128)S(1)} %add_scaled.2.refs_1_.refs_0_), channel_id=1, source_target_pairs={{0,6},{1,7},{2,4},{3,5},{4,10},{5,11},{6,8},{7,9},{8,14},{9,15},{1... | collective-permute-start | bytes 393224 | tf_op jit(solution)/shard_map/onward/ppermute | solution.py:109
  35.2 10.4 %collective-permute-start.17 = (f32[128,256]{1,0:T(8,128)S(1)}, f32[128,256]{1,0:T(8,128)S(1)}, u32[]{:S(2)}, u32[]{:S(2)}) collective-permute-start(f32[128,256]{1,0:T(8,128)S(1)} %add_scaled.3.refs_1_), channel_id=1, source_target_pairs={{0,6},{1,7},{2,4},{3,5},{4,10},{5,11},{6,8},{7,9},{8,14},{9,15},{1... | collective-permute-start | bytes 393224 | tf_op jit(solution)/shard_map/onward/ppermute | solution.py:109
  36.3 4.1 %collective-permute-start.13 = (f32[88,256]{1,0:T(8,128)S(1)}, f32[88,256]{1,0:T(8,128)S(1)}, u32[]{:S(2)}, u32[]{:S(2)}) collective-permute-start(f32[88,256]{1,0:T(8,128)S(1)} %get-tuple-element.91), channel_id=1, source_target_pairs={{0,1},{1,0},{2,3},{3,2},{4,5},{5,4},{6,7},{7,6},{8,9},{9,8},{10,11... | collective-permute-start | bytes 270344 | tf_op jit(solution)/shard_map/core_swap/ppermute | solution.py:100
  39.0 1.4 %collective-permute-start.14 = (f32[88,256]{1,0:T(8,128)S(1)}, f32[88,256]{1,0:T(8,128)S(1)}, u32[]{:S(2)}, u32[]{:S(2)}) collective-permute-start(f32[88,256]{1,0:T(8,128)S(1)} %get-tuple-element.92), channel_id=1, source_target_pairs={{0,1},{1,0},{2,3},{3,2},{4,5},{5,4},{6,7},{7,6},{8,9},{9,8},{10,11... | collective-permute-start | bytes 270344 | tf_op jit(solution)/shard_map/core_swap/ppermute | solution.py:100
  39.1 1.3 %collective-permute-start.15 = (f32[80,256]{1,0:T(8,128)S(1)}, f32[80,256]{1,0:T(8,128)S(1)}, u32[]{:S(2)}, u32[]{:S(2)}) collective-permute-start(f32[80,256]{1,0:T(8,128)S(1)} %get-tuple-element.93), channel_id=1, source_target_pairs={{0,1},{1,0},{2,3},{3,2},{4,5},{5,4},{6,7},{7,6},{8,9},{9,8},{10,11... | collective-permute-start | bytes 245768 | tf_op jit(solution)/shard_map/core_swap/ppermute | solution.py:100

commit v6 on v5

--- a/solution.py
+++ b/solution.py
@@ -17,7 +17,7 @@
 CHUNKS = 2
 SHARES = 3
 WEIGHT = 8
-COST = {"part": 2, "join": 0, "join_2": 16, "part_2": 2, "move": (4, 4, 4, 4), "user_step": 0, "layout": 0, "near": (2, 2), "far": (2, 2), "finish": 0, "user_sums": 64, "last": 0, "final": 0}
+COST = {"part": 2, "join": 0, "join_2": 4, "relay": 1, "part_2": 2, "move": (4, 4, 4, 4), "user_step": 0, "layout": 0, "near": (2, 2), "far": (2, 2), "finish": 0, "user_sums": 64, "last": 0, "final": 0}
 VMEM_LIMIT = 16 * 1024 * 1024
 
 NN = (((1,), (0,)), ((), ()))
@@ -229,12 +229,12 @@
             item_halves = halves(items_ref[rows_of(place_ref, flip), :])
             kept = (errors[2 * flip][...], errors[2 * flip + 1][...])
             total = total + product(kept, item_halves, TN)
-        users_out[...] = stepped(users_ref[...], total, noise_ref[...])
+        users_out[...] = stepped(users_ref[...], total, noise_ref[0])
 
     [users_1] = call(
         user_step,
         [(users.shape, f32)],
-        [place, local(users_0), local(items_0), local(noise_users[0])]
+        [place, local(users_0), local(items_0), local(noise_users)]
         + [local(v) for v in errors_0 + errors_1 + errors_2 + errors_3],
         COST["user_step"] * unit,
     )
@@ -257,7 +257,7 @@
             def _(slot=slot):
                 tile = index_ref[1, slot]
                 at = pl.ds(pl.multiple_of(lax.rem(tile, columns) * TILE, TILE), TILE)
-                turned = (rating_ref[slot].astype(f32).T, weight_ref[slot].astype(f32).T)
+                turned = (rating_ref[1, slot].astype(f32).T, weight_ref[1, slot].astype(f32).T)
                 for row in range(owned // TILE):
 
                     @pl.when(lax.div(tile, columns) == row)
@@ -277,7 +277,7 @@
         layout,
         [(flat, f32)] * 2 + [((4 * quarter + owned, rank), f32), ((quarter, rank), f32)],
         [place] + tables[:2] + [(DISTANT, noise_items)]
-        + [local(v) for v in (ratings[1], weights[1], users_1)],
+        + [local(v) for v in (ratings, weights, users_1)],
         COST["layout"] * unit,
         landing[:2] + [pltpu.SemaphoreType.DMA((3,))],
         after=[users_1],
@@ -289,6 +289,12 @@
         start = pl.multiple_of((place_ref[0] ^ flip) * quarter + k * chunk, chunk)
         total = own_ref[...] + other_ref[...]
         out[...] = stepped(items_ref[pl.ds(start, chunk), :], total, noise_ref[rows(n), :])
+
+    def relay(value_ref, out):
+        out[...] = value_ref[...]
+
+    def relayed(value, cost, after):
+        return call(relay, [(piece, f32)], [local(value)], cost * unit, after=after)
 
     moved = []
     for n in range(2 * CHUNKS):
@@ -297,12 +303,14 @@
                 join, rows(n), mine, from_sibling_2, COST["join_2"],
                 [to_sibling, from_chip[n], *moved[-1:]],
             )
-            from_chip.append(swap(to_chip[-1], 2))
         terms = [local(v) for v in (items_0, noise_0, to_chip[(n + CHUNKS) % (2 * CHUNKS)], from_chip[n])]
         moved += call(
             functools.partial(move, n), [(piece, f32)], [place] + terms, COST["move"][n] * unit,
             after=moved[-1:],
         )
+        if n < CHUNKS:
+            [value] = relayed(to_chip[-1], COST["relay"], moved[-1:])
+            from_chip.append(swap(value, 2))
     ahead = [onward(value) for value in moved]
 
     def late(k, slot, place_ref, items_ref, users_ref, rating_ref, weight_ref, sibling_ref, *rest):
@@ -327,12 +335,6 @@
     common = [local(v) for v in (users_1, rating_1, weight_1, from_sibling)]
     errors_shape = (chunk, owned)
     late_outs = [(errors_shape, bf16)] * 4 + [(piece, f32)]
-    def relay(value_ref, out):
-        out[...] = value_ref[...]
-
-    def relayed(value, cost, after):
-        return call(relay, [(piece, f32)], [local(value)], cost * unit, after=after)
-
     here, there = ahead[:CHUNKS], ahead[CHUNKS:]
     errors_here, sent = [], []
     for k in range(CHUNKS):
@@ -389,12 +391,12 @@
         token[...] = jnp.zeros_like(token)
         for at, ref in zip(shares_at, shares):
             total = sums_ref[at, :] + ref[...]
-            users_out[at, :] = stepped(users_ref[at, :], total, noise_ref[at, :])
+            users_out[at, :] = stepped(users_ref[at, :], total, noise_ref[1, at, :])
 
     users_out, token = call(
         last,
         [(users.shape, f32), ((8, 128), f32)],
-        [local(users_1), local(sums), local(noise_users[1])] + [local(v) for v in from_sibling],
+        [local(users_1), local(sums), local(noise_users)] + [local(v) for v in from_sibling],
         COST["last"] * unit,
     )
 

time: 46.3 us -> 45.6 us (0.985)
  waiting for transfers between devices: 16.6 us -> 14.8 us
  starting transfers between devices: 15.7 us -> 17.1 us
  local copies, waits for them, and re-layouts: 1.02 us -> 0.5 us
    ppermute x6, waiting for transfers between devices: 13.2 us -> 10.3 us  [onward(): return lax.ppermute(value, AXES, pairs)]
    ppermute x12, waiting for transfers between devices: 3.39 us -> 4.5 us  [swap(): return lax.ppermute(value, AXES, pairs)]
    ppermute x6, starting transfers between devices: 5.52 us -> 6.28 us  [onward(): return lax.ppermute(value, AXES, pairs)]
    ppermute x12, starting transfers between devices: 10.2 us -> 10.8 us  [swap(): return lax.ppermute(value, AXES, pairs)]
    pallas_call x24 -> x26, Pallas kernels: 12.2 us -> 12.2 us  [call(): pl.pallas_call(kernel, in_specs=[AFTER] * unread + [spec for spec, _ in o...]
where the time goes in v6:
time: 45.6 us; the launch traced here: 45.4 us
  starting transfers between devices  17.1 us (38%)
  waiting for transfers between devices  14.8 us (32%)
  Pallas kernels  12.2 us (27%)
  between operations  0.87 us (2%)
  local copies, waits for them, and re-layouts  0.5 us (1%)
    pallas_call x26, Pallas kernels, call(): pl.pallas_call(kernel, in_specs=[AFTER] * unread + [spec for spec, _ in o...  12.2 us
    ppermute x12, starting transfers between devices, swap(): return lax.ppermute(value, AXES, pairs)  10.8 us
    ppermute x6, waiting for transfers between devices, onward(): return lax.ppermute(value, AXES, pairs)  10.3 us
    ppermute x6, starting transfers between devices, onward(): return lax.ppermute(value, AXES, pairs)  6.28 us
    ppermute x12, waiting for transfers between devices, swap(): return lax.ppermute(value, AXES, pairs)  4.5 us
  transfers between devices with their start and end apart: 18, of which 10 were waited for; matrix products, arithmetic and copies ran while one was open for 0% of the time, Pallas kernels for 21%

profile of v6, /device:TPU:1, one launch (start us, length us, event | category | flops | bytes accessed | tf_op | source)
XLA Modules:
  0.0 45.4 jit_solution(11196160061129366316)
XLA Ops:
  0.6 1.9 %first.1 = (bf16[8,256,128]{2,1,0:T(8,128)(2,1)S(1)}, bf16[8,256,128]{2,1,0:T(8,128)(2,1)S(1)}, f32[256,256]{1,0:T(8,128)S(1)}, f32[1024,256]{1,0:T(8,128)S(1)},...) custom-call(s32[1]{0:T(128)} %bitcast.refs_0_.refs_1_.refs_2_, ...), custom_call_target="tpu_custom_call" | custom-call | flops 1610612736 | bytes 262144 | tf_op jit(solution)/shard_map/first/pallas_call | solution.py:62
  2.6 3.3 %collective-permute-start = (f32[256,256]{1,0:T(8,128)S(1)}, f32[256,256]{1,0:T(8,128)S(1)}, u32[]{:S(2)}, u32[]{:S(2)}) collective-permute-start(f32[256,256]{1,0:T(8,128)S(1)} %get-tuple-element.59), channel_id=1, source_target_pairs={{0,1},{1,0},{2,3},{3,2},{4,5},{5,4},{6,7},{7,6},{8,9},{9,8},{10,11... | collective-permute-start | bytes 786440 | tf_op jit(solution)/shard_map/core_swap/ppermute | solution.py:100
  5.9 0.6 %part.3 = (bf16[256,256]{1,0:T(8,128)(2,1)S(1)}, bf16[256,256]{1,0:T(8,128)(2,1)S(1)}, f32[256,256]{1,0:T(8,128)S(1)}) custom-call(s32[1]{0:T(128)} %bitcast.refs_0_.refs_1_.refs_2_, bf16[8,256,128]{2,1,0:T(8,128)(2,1)S(1)} %get-tuple-element.51.refs_1_.refs_2_.refs_3_, bf16[8,256,128]{2,1,0:T(8,128)(2,1)S(1)} %get-tuple-element.52.refs_2_.refs_3_.refs_4_, ...), custom_call_target="tpu_custom_call" | custom-call | flops 1610612736 | bytes 262144 | tf_op jit(solution)/shard_map/part/pallas_call | solution.py:62
  6.6 0.1 collective-permute-start.2
  6.7 0.6 %part.4 = (bf16[256,256]{1,0:T(8,128)(2,1)S(1)}, bf16[256,256]{1,0:T(8,128)(2,1)S(1)}, f32[256,256]{1,0:T(8,128)S(1)}) custom-call(f32[256,256]{1,0:T(8,128)S(1)} %get-tuple-element.53.refs_0_, s32[1]{0:T(128)} %bitcast.refs_0_.refs_1_.refs_2_, bf16[8,256,128]{2,1,0:T(8,128)(2,1)S(1)} %get-tuple-element.51.refs_1_.refs_2_.refs_3_, ...), custom_call_target="tpu_custom_call" | custom-call | flops 1610612736 | bytes 262144 | tf_op jit(solution)/shard_map/part/pallas_call | solution.py:62
  7.3 0.1 collective-permute-start.1
  7.5 0.0 copy-start
  7.5 1.5 %collective-permute-start.5 = (f32[128,256]{1,0:T(8,128)S(1)}, f32[128,256]{1,0:T(8,128)S(1)}, u32[]{:S(2)}, u32[]{:S(2)}) collective-permute-start(f32[128,256]{1,0:T(8,128)S(1)} %join.5.refs_1_.refs_4_), channel_id=1, source_target_pairs={{0,2},{1,3},{2,0},{3,1},{4,6},{5,7},{6,4},{7,5},{8,10},{9,11},{10,... | collective-permute-start | bytes 393224 | tf_op jit(solution)/shard_map/chip_swap/ppermute | solution.py:100
  9.0 0.6 %part.5 = (bf16[256,256]{1,0:T(8,128)(2,1)S(1)}, bf16[256,256]{1,0:T(8,128)(2,1)S(1)}, f32[256,256]{1,0:T(8,128)S(1)}) custom-call(f32[128,256]{1,0:T(8,128)S(1)} %join.4.refs_0_.refs_4_, f32[128,256]{1,0:T(8,128)S(1)} %join.5.refs_1_.refs_4_, s32[1]{0:T(128)} %bitcast.refs_0_.refs_1_.refs_2_, ...), custom_call_target="tpu_custom_call" | custom-call | flops 1610612736 | bytes 262144 | tf_op jit(solution)/shard_map/part/pallas_call | solution.py:62
  9.7 0.0 copy-start.1
  9.7 0.0 copy-start.2
  9.7 0.7 %user_step.1.refs_0_.refs_7_.refs_2_.refs_3_.refs_4_ = f32[256,256]{1,0:T(8,128)S(1)} custom-call(s32[1]{0:T(128)} %bitcast.refs_0_.refs_1_.refs_2_, f32[256,256]{1,0:T(8,128)S(1)} %get-tuple-element.49.refs_3_.refs_4_.refs_5_.refs_1_, f32[1024,256]{1,0:T(8,128)S(1)} %get-tuple-element.50.refs_4_.refs_5_.refs_6_.refs_2_.refs_1_, f32[2,256,256]{2,1,0:T(8,128)S(1)} %copy-done, ...), custom_call_target="tpu_custom_call" | custom-call | bytes 262144 | tf_op jit(solution)/shard_map/user_step/pallas_call | solution.py:62
  10.4 0.3 copy-done.1
  10.7 0.2 copy-done.2
  10.9 1.4 %layout.1 = (f32[1024,256]{1,0:T(8,128)S(1)}, f32[1024,256]{1,0:T(8,128)S(1)}, f32[1280,256]{1,0:T(8,128)S(1)}, f32[256,256]{1,0:T(8,128)S(1)}) custom-call(f32[256,256]{1,0:T(8,128)S(1)} %user_step.1.refs_0_.refs_7_.refs_2_.refs_3_.refs_4_, s32[1]{0:T(128)} %bitcast.refs_0_.refs_1_.refs_2_, s32[2,8]{1,0:T(2,128)} %refs_2_.2, s32[2]{0:T(128)} %bitcast.3, ...), custom_call_target="tpu_custom_call" | custom-call | bytes 262144 | tf_op jit(solution)/shard_map/layout/pallas_call | solution.py:62
  12.3 1.4 %collective-permute-start.4 = (f32[1280,256]{1,0:T(8,128)S(1)}, f32[1280,256]{1,0:T(8,128)S(1)}, u32[]{:S(2)}, u32[]{:S(2)}) collective-permute-start(f32[1280,256]{1,0:T(8,128)S(1)} %get-tuple-element.65.refs_0_), channel_id=1, source_target_pairs={{0,1},{1,0},{2,3},{3,2},{4,5},{5,4},{6,7},{7,6},{8,9},{9,8},{10,11... | collective-permute-start | bytes 3932168 | tf_op jit(solution)/shard_map/core_swap/ppermute | solution.py:100
  13.7 0.0 collective-permute-done.1.refs_1_.refs_4_
  13.8 0.5 %collective-permute-start.3 = (f32[128,256]{1,0:T(8,128)S(1)}, f32[128,256]{1,0:T(8,128)S(1)}, u32[]{:S(2)}, u32[]{:S(2)}) collective-permute-start(f32[128,256]{1,0:T(8,128)S(1)} %move.4.refs_2_.refs_0_), channel_id=1, source_target_pairs={{0,6},{1,7},{2,4},{3,5},{4,10},{5,11},{6,8},{7,9},{8,14},{9,15},{1... | collective-permute-start | bytes 393224 | tf_op jit(solution)/shard_map/onward/ppermute | solution.py:109
  14.3 0.5 %collective-permute-done.5.refs_1_.refs_5_ = f32[128,256]{1,0:T(8,128)S(1)} collective-permute-done((f32[128,256]{1,0:T(8,128)S(1)}, f32[128,256]{1,0:T(8,128)S(1)}, u32[]{:S(2)}, u32[]{:S(2)}) %collective-permute-start.5) | collective-permute-done | bytes 131104 | tf_op jit(solution)/shard_map/chip_swap/ppermute | solution.py:100
  14.8 0.1 move.5.refs_0_
  14.9 1.8 %collective-permute-start.6 = (f32[128,256]{1,0:T(8,128)S(1)}, f32[128,256]{1,0:T(8,128)S(1)}, u32[]{:S(2)}, u32[]{:S(2)}) collective-permute-start(f32[128,256]{1,0:T(8,128)S(1)} %move.5.refs_0_), channel_id=1, source_target_pairs={{0,6},{1,7},{2,4},{3,5},{4,10},{5,11},{6,8},{7,9},{8,14},{9,15},{1... | collective-permute-start | bytes 393224 | tf_op jit(solution)/shard_map/onward/ppermute | solution.py:109
  16.7 0.3 collective-permute-start.10
  17.0 1.2 %collective-permute-done.7.refs_5_ = f32[128,256]{1,0:T(8,128)S(1)} collective-permute-done((f32[128,256]{1,0:T(8,128)S(1)}, f32[128,256]{1,0:T(8,128)S(1)}, u32[]{:S(2)}, u32[]{:S(2)}) %collective-permute-start.7) | collective-permute-done | bytes 131104 | tf_op jit(solution)/shard_map/chip_swap/ppermute | solution.py:100
  18.2 1.9 %collective-permute-start.8 = (f32[128,256]{1,0:T(8,128)S(1)}, f32[128,256]{1,0:T(8,128)S(1)}, u32[]{:S(2)}, u32[]{:S(2)}) collective-permute-start(f32[128,256]{1,0:T(8,128)S(1)} %move.6.refs_0_), channel_id=1, source_target_pairs={{0,6},{1,7},{2,4},{3,5},{4,10},{5,11},{6,8},{7,9},{8,14},{9,15},{1... | collective-permute-start | bytes 393224 | tf_op jit(solution)/shard_map/onward/ppermute | solution.py:109
  20.1 1.1 %collective-permute-done.10.refs_5_ = f32[128,256]{1,0:T(8,128)S(1)} collective-permute-done((f32[128,256]{1,0:T(8,128)S(1)}, f32[128,256]{1,0:T(8,128)S(1)}, u32[]{:S(2)}, u32[]{:S(2)}) %collective-permute-start.10) | collective-permute-done | bytes 131104 | tf_op jit(solution)/shard_map/chip_swap/ppermute | solution.py:100
  21.2 1.9 %collective-permute-start.11 = (f32[128,256]{1,0:T(8,128)S(1)}, f32[128,256]{1,0:T(8,128)S(1)}, u32[]{:S(2)}, u32[]{:S(2)}) collective-permute-start(f32[128,256]{1,0:T(8,128)S(1)} %move.7), channel_id=1, source_target_pairs={{0,6},{1,7},{2,4},{3,5},{4,10},{5,11},{6,8},{7,9},{8,14},{9,15},{1... | collective-permute-start | bytes 393224 | tf_op jit(solution)/shard_map/onward/ppermute | solution.py:109
  23.1 1.9 %collective-permute-done.3.refs_1_.refs_6_ = f32[128,256]{1,0:T(8,128)S(1)} collective-permute-done((f32[128,256]{1,0:T(8,128)S(1)}, f32[128,256]{1,0:T(8,128)S(1)}, u32[]{:S(2)}, u32[]{:S(2)}) %collective-permute-start.3) | collective-permute-done | bytes 131104 | tf_op jit(solution)/shard_map/onward/ppermute | solution.py:109
  25.0 0.9 %late.4 = (bf16[128,256]{1,0:T(8,128)(2,1)S(1)}, bf16[128,256]{1,0:T(8,128)(2,1)S(1)}, bf16[128,256]{1,0:T(8,128)(2,1)S(1)}, bf16[128,256]{1,0:T(8,128)(2,1)S(1)}, f32[128,256]{1,0:T(8,128)S(1)}) custom-call(s32[1]{0:T(128)} %bitcast.refs_0_.refs_1_.refs_2_, f32[128,256]{1,0:T(8,128)S(1)} %collective-permute-done.3.refs_1_.refs_6_, ...), custom_call_target="tpu_custom_call" | custom-call | flops 1610612736 | bytes 262144 | tf_op jit(solution)/shard_map/late/pallas_call | solution.py:62
  25.9 0.2 collective-permute-start.9
  26.1 1.7 %collective-permute-done.6.refs_2_.refs_11_ = f32[128,256]{1,0:T(8,128)S(1)} collective-permute-done((f32[128,256]{1,0:T(8,128)S(1)}, f32[128,256]{1,0:T(8,128)S(1)}, u32[]{:S(2)}, u32[]{:S(2)}) %collective-permute-start.6) | collective-permute-done | bytes 131104 | tf_op jit(solution)/shard_map/onward/ppermute | solution.py:109
  27.8 0.9 %late.5 = (bf16[128,256]{1,0:T(8,128)(2,1)S(1)}, bf16[128,256]{1,0:T(8,128)(2,1)S(1)}, bf16[128,256]{1,0:T(8,128)(2,1)S(1)}, bf16[128,256]{1,0:T(8,128)(2,1)S(1)}, f32[128,256]{1,0:T(8,128)S(1)}) custom-call(f32[128,256]{1,0:T(8,128)S(1)} %get-tuple-element.69.refs_0_, s32[1]{0:T(128)} %bitcast.refs_0_.refs_1_.refs_2_, ...), custom_call_target="tpu_custom_call" | custom-call | flops 1610612736 | bytes 262144 | tf_op jit(solution)/shard_map/late/pallas_call | solution.py:62
  28.7 0.4 collective-permute-start.12
  29.1 0.9 %collective-permute-done.8.refs_2_.refs_16_ = f32[128,256]{1,0:T(8,128)S(1)} collective-permute-done((f32[128,256]{1,0:T(8,128)S(1)}, f32[128,256]{1,0:T(8,128)S(1)}, u32[]{:S(2)}, u32[]{:S(2)}) %collective-permute-start.8) | collective-permute-done | bytes 131104 | tf_op jit(solution)/shard_map/onward/ppermute | solution.py:109
  30.0 0.9 %late.6 = (bf16[128,256]{1,0:T(8,128)(2,1)S(1)}, bf16[128,256]{1,0:T(8,128)(2,1)S(1)}, bf16[128,256]{1,0:T(8,128)(2,1)S(1)}, bf16[128,256]{1,0:T(8,128)(2,1)S(1)}, f32[128,256]{1,0:T(8,128)S(1)}) custom-call(f32[128,256]{1,0:T(8,128)S(1)} %get-tuple-element.70.refs_0_, s32[1]{0:T(128)} %bitcast.refs_0_.refs_1_.refs_2_, ...), custom_call_target="tpu_custom_call" | custom-call | flops 1610612736 | bytes 262144 | tf_op jit(solution)/shard_map/late/pallas_call | solution.py:62
  30.9 0.0 collective-permute-done.9.refs_1_
  30.9 0.1 collective-permute-start.16
  31.0 1.7 %collective-permute-done.11.refs_3_.refs_21_ = f32[128,256]{1,0:T(8,128)S(1)} collective-permute-done((f32[128,256]{1,0:T(8,128)S(1)}, f32[128,256]{1,0:T(8,128)S(1)}, u32[]{:S(2)}, u32[]{:S(2)}) %collective-permute-start.11) | collective-permute-done | bytes 131104 | tf_op jit(solution)/shard_map/onward/ppermute | solution.py:109
  32.8 0.9 %late.7 = (bf16[128,256]{1,0:T(8,128)(2,1)S(1)}, bf16[128,256]{1,0:T(8,128)(2,1)S(1)}, bf16[128,256]{1,0:T(8,128)(2,1)S(1)}, bf16[128,256]{1,0:T(8,128)(2,1)S(1)}, f32[128,256]{1,0:T(8,128)S(1)}) custom-call(f32[128,256]{1,0:T(8,128)S(1)} %get-tuple-element.70.refs_0_, f32[128,256]{1,0:T(8,128)S(1)} %add_scaled.2.refs_1_.refs_0_, ...), custom_call_target="tpu_custom_call" | custom-call | flops 1610612736 | bytes 262144 | tf_op jit(solution)/shard_map/late/pallas_call | solution.py:62
  33.7 0.8 %collective-permute-done.12.refs_1_ = f32[128,256]{1,0:T(8,128)S(1)} collective-permute-done((f32[128,256]{1,0:T(8,128)S(1)}, f32[128,256]{1,0:T(8,128)S(1)}, u32[]{:S(2)}, u32[]{:S(2)}) %collective-permute-start.12) | collective-permute-done | bytes 131104 | tf_op jit(solution)/shard_map/chip_swap/ppermute | solution.py:100
  34.5 0.1 collective-permute-start.17
  34.6 1.0 %user_sums.1 = (f32[256,256]{1,0:T(8,128)S(1)}, f32[88,256]{1,0:T(8,128)S(1)}, f32[88,256]{1,0:T(8,128)S(1)}, f32[80,256]{1,0:T(8,128)S(1)}) custom-call(f32[128,256]{1,0:T(8,128)S(1)} %add_scaled.2.refs_1_.refs_0_, f32[128,256]{1,0:T(8,128)S(1)} %add_scaled.3.refs_1_, bf16[128,256]{1,0:T(8,128)(2,1)S(1)} %get-tuple-element.74.refs_2_, ...), custom_call_target="tpu_custom_call" | custom-call | flops 51539607552 | bytes 262144 | tf_op jit(solution)/shard_map/user_sums/pallas_call | solution.py:62
  35.6 2.9 %collective-permute-start.13 = (f32[88,256]{1,0:T(8,128)S(1)}, f32[88,256]{1,0:T(8,128)S(1)}, u32[]{:S(2)}, u32[]{:S(2)}) collective-permute-start(f32[88,256]{1,0:T(8,128)S(1)} %get-tuple-element.91), channel_id=1, source_target_pairs={{0,1},{1,0},{2,3},{3,2},{4,5},{5,4},{6,7},{7,6},{8,9},{9,8},{10,11... | collective-permute-start | bytes 270344 | tf_op jit(solution)/shard_map/core_swap/ppermute | solution.py:100
  38.5 0.1 collective-permute-start.14
  38.6 0.4 collective-permute-start.15
  39.0 0.9 %collective-permute-done.15.refs_5_ = f32[80,256]{1,0:T(8,128)S(1)} collective-permute-done((f32[80,256]{1,0:T(8,128)S(1)}, f32[80,256]{1,0:T(8,128)S(1)}, u32[]{:S(2)}, u32[]{:S(2)}) %collective-permute-start.15) | collective-permute-done | bytes 81952 | tf_op jit(solution)/shard_map/core_swap/ppermute | solution.py:100
  39.9 0.8 %last.1 = (f32[256,256]{1,0:T(8,128)}, f32[8,128]{1,0:T(8,128)S(1)}) custom-call(f32[256,256]{1,0:T(8,128)S(1)} %user_step.1.refs_0_.refs_7_.refs_2_.refs_3_.refs_4_, f32[256,256]{1,0:T(8,128)S(1)} %get-tuple-element.90.refs_1_, f32[2,256,256]{2,1,0:T(8,128)S(1)} %copy-done, f32[88,256]{1,0:T(8,128)S(1)} %collective-permute-done.13.refs_3_, ...), custom_call_target="tpu_custom_call" | custom-call | bytes 262144 | tf_op jit(solution)/shard_map/last/pallas_call | solution.py:62
  40.7 4.0 %collective-permute-done.17.refs_1_ = f32[128,256]{1,0:T(8,128)S(1)} collective-permute-done((f32[128,256]{1,0:T(8,128)S(1)}, f32[128,256]{1,0:T(8,128)S(1)}, u32[]{:S(2)}, u32[]{:S(2)}) %collective-permute-start.17) | collective-permute-done | bytes 131104 | tf_op jit(solution)/shard_map/onward/ppermute | solution.py:109
  44.7 0.7 %stack.1 = f32[256,256]{1,0:T(8,128)} custom-call(f32[128,256]{1,0:T(8,128)S(1)} %relay.5.refs_0_, f32[128,256]{1,0:T(8,128)S(1)} %collective-permute-done.17.refs_1_), custom_call_target="tpu_custom_call" | custom-call | flops 8 | bytes 262144 | tf_op jit(solution)/shard_map/stack/pallas_call | solution.py:62
  (20 shorter events, 0.3 us)
Async XLA Ops:
  2.6 4.7 %collective-permute-start = (f32[256,256]{1,0:T(8,128)S(1)}, f32[256,256]{1,0:T(8,128)S(1)}, u32[]{:S(2)}, u32[]{:S(2)}) collective-permute-start(f32[256,256]{1,0:T(8,128)S(1)} %get-tuple-element.59), channel_id=1, source_target_pairs={{0,1},{1,0},{2,3},{3,2},{4,5},{5,4},{6,7},{7,6},{8,9},{9,8},{10,11... | collective-permute-start | bytes 786440 | tf_op jit(solution)/shard_map/core_swap/ppermute | solution.py:100
  6.6 7.1 %collective-permute-start.2 = (f32[256,256]{1,0:T(8,128)S(1)}, f32[256,256]{1,0:T(8,128)S(1)}, u32[]{:S(2)}, u32[]{:S(2)}) collective-permute-start(f32[256,256]{1,0:T(8,128)S(1)} %get-tuple-element.53.refs_0_), channel_id=1, source_target_pairs={{0,1},{1,0},{2,3},{3,2},{4,5},{5,4},{6,7},{7,6},{8,9},{9,8},{10,11... | collective-permute-start | bytes 786440 | tf_op jit(solution)/shard_map/core_swap/ppermute | solution.py:100
  7.3 6.4 %collective-permute-start.1 = (f32[128,256]{1,0:T(8,128)S(1)}, f32[128,256]{1,0:T(8,128)S(1)}, u32[]{:S(2)}, u32[]{:S(2)}) collective-permute-start(f32[128,256]{1,0:T(8,128)S(1)} %join.4.refs_0_.refs_4_), channel_id=1, source_target_pairs={{0,2},{1,3},{2,0},{3,1},{4,6},{5,7},{6,4},{7,5},{8,10},{9,11},{10,... | collective-permute-start | bytes 393224 | tf_op jit(solution)/shard_map/chip_swap/ppermute | solution.py:100
  7.5 2.2 %copy-start = (f32[2,256,256]{2,1,0:T(8,128)S(1)}, f32[2,256,256]{2,1,0:T(8,128)}, u32[]{:S(2)}) copy-start(f32[2,256,256]{2,1,0:T(8,128)} %refs_2_.3) | copy-start | bytes 1572868
  7.5 7.3 %collective-permute-start.5 = (f32[128,256]{1,0:T(8,128)S(1)}, f32[128,256]{1,0:T(8,128)S(1)}, u32[]{:S(2)}, u32[]{:S(2)}) collective-permute-start(f32[128,256]{1,0:T(8,128)S(1)} %join.5.refs_1_.refs_4_), channel_id=1, source_target_pairs={{0,2},{1,3},{2,0},{3,1},{4,6},{5,7},{6,4},{7,5},{8,10},{9,11},{10,... | collective-permute-start | bytes 393224 | tf_op jit(solution)/shard_map/chip_swap/ppermute | solution.py:100
  9.7 1.0 %copy-start.1 = (bf16[2,8,128,128]{3,2,1,0:T(8,128)(2,1)S(1)}, bf16[2,8,128,128]{3,2,1,0:T(8,128)(2,1)}, u32[]{:S(2)}) copy-start(bf16[2,8,128,128]{3,2,1,0:T(8,128)(2,1)} %refs_5_.3) | copy-start | bytes 1572868
  9.7 1.2 %copy-start.2 = (bf16[2,8,128,128]{3,2,1,0:T(8,128)(2,1)S(1)}, bf16[2,8,128,128]{3,2,1,0:T(8,128)(2,1)}, u32[]{:S(2)}) copy-start(bf16[2,8,128,128]{3,2,1,0:T(8,128)(2,1)} %refs_6_.3) | copy-start | bytes 1572868
  12.3 12.8 %collective-permute-start.4 = (f32[1280,256]{1,0:T(8,128)S(1)}, f32[1280,256]{1,0:T(8,128)S(1)}, u32[]{:S(2)}, u32[]{:S(2)}) collective-permute-start(f32[1280,256]{1,0:T(8,128)S(1)} %get-tuple-element.65.refs_0_), channel_id=1, source_target_pairs={{0,1},{1,0},{2,3},{3,2},{4,5},{5,4},{6,7},{7,6},{8,9},{9,8},{10,11... | collective-permute-start | bytes 3932168 | tf_op jit(solution)/shard_map/core_swap/ppermute | solution.py:100
  13.8 11.2 %collective-permute-start.3 = (f32[128,256]{1,0:T(8,128)S(1)}, f32[128,256]{1,0:T(8,128)S(1)}, u32[]{:S(2)}, u32[]{:S(2)}) collective-permute-start(f32[128,256]{1,0:T(8,128)S(1)} %move.4.refs_2_.refs_0_), channel_id=1, source_target_pairs={{0,6},{1,7},{2,4},{3,5},{4,10},{5,11},{6,8},{7,9},{8,14},{9,15},{1... | collective-permute-start | bytes 393224 | tf_op jit(solution)/shard_map/onward/ppermute | solution.py:109
  14.3 3.8 %collective-permute-start.7 = (f32[128,256]{1,0:T(8,128)S(1)}, f32[128,256]{1,0:T(8,128)S(1)}, u32[]{:S(2)}, u32[]{:S(2)}) collective-permute-start(f32[128,256]{1,0:T(8,128)S(1)} %relay.3), channel_id=1, source_target_pairs={{0,2},{1,3},{2,0},{3,1},{4,6},{5,7},{6,4},{7,5},{8,10},{9,11},{10,... | collective-permute-start | bytes 393224 | tf_op jit(solution)/shard_map/chip_swap/ppermute | solution.py:100
  14.9 13.0 %collective-permute-start.6 = (f32[128,256]{1,0:T(8,128)S(1)}, f32[128,256]{1,0:T(8,128)S(1)}, u32[]{:S(2)}, u32[]{:S(2)}) collective-permute-start(f32[128,256]{1,0:T(8,128)S(1)} %move.5.refs_0_), channel_id=1, source_target_pairs={{0,6},{1,7},{2,4},{3,5},{4,10},{5,11},{6,8},{7,9},{8,14},{9,15},{1... | collective-permute-start | bytes 393224 | tf_op jit(solution)/shard_map/onward/ppermute | solution.py:109
  16.7 4.5 %collective-permute-start.10 = (f32[128,256]{1,0:T(8,128)S(1)}, f32[128,256]{1,0:T(8,128)S(1)}, u32[]{:S(2)}, u32[]{:S(2)}) collective-permute-start(f32[128,256]{1,0:T(8,128)S(1)} %relay.4), channel_id=1, source_target_pairs={{0,2},{1,3},{2,0},{3,1},{4,6},{5,7},{6,4},{7,5},{8,10},{9,11},{10,... | collective-permute-start | bytes 393224 | tf_op jit(solution)/shard_map/chip_swap/ppermute | solution.py:100
  18.2 11.8 %collective-permute-start.8 = (f32[128,256]{1,0:T(8,128)S(1)}, f32[128,256]{1,0:T(8,128)S(1)}, u32[]{:S(2)}, u32[]{:S(2)}) collective-permute-start(f32[128,256]{1,0:T(8,128)S(1)} %move.6.refs_0_), channel_id=1, source_target_pairs={{0,6},{1,7},{2,4},{3,5},{4,10},{5,11},{6,8},{7,9},{8,14},{9,15},{1... | collective-permute-start | bytes 393224 | tf_op jit(solution)/shard_map/onward/ppermute | solution.py:109
  21.2 11.6 %collective-permute-start.11 = (f32[128,256]{1,0:T(8,128)S(1)}, f32[128,256]{1,0:T(8,128)S(1)}, u32[]{:S(2)}, u32[]{:S(2)}) collective-permute-start(f32[128,256]{1,0:T(8,128)S(1)} %move.7), channel_id=1, source_target_pairs={{0,6},{1,7},{2,4},{3,5},{4,10},{5,11},{6,8},{7,9},{8,14},{9,15},{1... | collective-permute-start | bytes 393224 | tf_op jit(solution)/shard_map/onward/ppermute | solution.py:109
  25.9 5.0 %collective-permute-start.9 = (f32[128,256]{1,0:T(8,128)S(1)}, f32[128,256]{1,0:T(8,128)S(1)}, u32[]{:S(2)}, u32[]{:S(2)}) collective-permute-start(f32[128,256]{1,0:T(8,128)S(1)} %get-tuple-element.69.refs_0_), channel_id=1, source_target_pairs={{0,2},{1,3},{2,0},{3,1},{4,6},{5,7},{6,4},{7,5},{8,10},{9,11},{10,... | collective-permute-start | bytes 393224 | tf_op jit(solution)/shard_map/chip_swap/ppermute | solution.py:100
  28.7 5.8 %collective-permute-start.12 = (f32[128,256]{1,0:T(8,128)S(1)}, f32[128,256]{1,0:T(8,128)S(1)}, u32[]{:S(2)}, u32[]{:S(2)}) collective-permute-start(f32[128,256]{1,0:T(8,128)S(1)} %get-tuple-element.70.refs_0_), channel_id=1, source_target_pairs={{0,2},{1,3},{2,0},{3,1},{4,6},{5,7},{6,4},{7,5},{8,10},{9,11},{10,... | collective-permute-start | bytes 393224 | tf_op jit(solution)/shard_map/chip_swap/ppermute | solution.py:100
  30.9 9.8 %collective-permute-start.16 = (f32[128,256]{1,0:T(8,128)S(1)}, f32[128,256]{1,0:T(8,128)S(1)}, u32[]{:S(2)}, u32[]{:S(2)}) collective-permute-start(f32[128,256]{1,0:T(8,128)S(1)} %add_scaled.2.refs_1_.refs_0_), channel_id=1, source_target_pairs={{0,6},{1,7},{2,4},{3,5},{4,10},{5,11},{6,8},{7,9},{8,14},{9,15},{1... | collective-permute-start | bytes 393224 | tf_op jit(solution)/shard_map/onward/ppermute | solution.py:109
  34.5 10.2 %collective-permute-start.17 = (f32[128,256]{1,0:T(8,128)S(1)}, f32[128,256]{1,0:T(8,128)S(1)}, u32[]{:S(2)}, u32[]{:S(2)}) collective-permute-start(f32[128,256]{1,0:T(8,128)S(1)} %add_scaled.3.refs_1_), channel_id=1, source_target_pairs={{0,6},{1,7},{2,4},{3,5},{4,10},{5,11},{6,8},{7,9},{8,14},{9,15},{1... | collective-permute-start | bytes 393224 | tf_op jit(solution)/shard_map/onward/ppermute | solution.py:109
  35.6 4.3 %collective-permute-start.13 = (f32[88,256]{1,0:T(8,128)S(1)}, f32[88,256]{1,0:T(8,128)S(1)}, u32[]{:S(2)}, u32[]{:S(2)}) collective-permute-start(f32[88,256]{1,0:T(8,128)S(1)} %get-tuple-element.91), channel_id=1, source_target_pairs={{0,1},{1,0},{2,3},{3,2},{4,5},{5,4},{6,7},{7,6},{8,9},{9,8},{10,11... | collective-permute-start | bytes 270344 | tf_op jit(solution)/shard_map/core_swap/ppermute | solution.py:100
  38.5 1.4 %collective-permute-start.14 = (f32[88,256]{1,0:T(8,128)S(1)}, f32[88,256]{1,0:T(8,128)S(1)}, u32[]{:S(2)}, u32[]{:S(2)}) collective-permute-start(f32[88,256]{1,0:T(8,128)S(1)} %get-tuple-element.92), channel_id=1, source_target_pairs={{0,1},{1,0},{2,3},{3,2},{4,5},{5,4},{6,7},{7,6},{8,9},{9,8},{10,11... | collective-permute-start | bytes 270344 | tf_op jit(solution)/shard_map/core_swap/ppermute | solution.py:100
  38.6 1.3 %collective-permute-start.15 = (f32[80,256]{1,0:T(8,128)S(1)}, f32[80,256]{1,0:T(8,128)S(1)}, u32[]{:S(2)}, u32[]{:S(2)}) collective-permute-start(f32[80,256]{1,0:T(8,128)S(1)} %get-tuple-element.93), channel_id=1, source_target_pairs={{0,1},{1,0},{2,3},{3,2},{4,5},{5,4},{6,7},{7,6},{8,9},{9,8},{10,11... | collective-permute-start | bytes 245768 | tf_op jit(solution)/shard_map/core_swap/ppermute | solution.py:100

commit v7 on v6

--- a/solution.py
+++ b/solution.py
@@ -315,19 +315,18 @@
 
     def late(k, slot, place_ref, items_ref, users_ref, rating_ref, weight_ref, sibling_ref, *rest):
         high_out, low_out, high_s_out, low_s_out, out = rest[-5:]
-        own, other = halves(users_ref[...]), halves(sibling_ref[4 * quarter :, :])
+        both = halves(jnp.concatenate([users_ref[...], sibling_ref[4 * quarter :, :]], 0))
         now = items_ref[...]
         item_halves = halves(now)
         at = pl.ds(pl.multiple_of((place_ref[0] ^ (2 * slot)) * quarter + k * chunk, chunk), chunk)
-        errors = errors_of(item_halves, own, rating_ref[at, :], weight_ref[at, :])
-        high_out[...], low_out[...] = errors
-        total = product(errors, own, NN)
-        at = slot * quarter + k * chunk
-        rating = sibling_ref[at : at + chunk, :]
-        weight = sibling_ref[2 * quarter + at : 2 * quarter + at + chunk, :]
-        errors = errors_of(item_halves, other, rating, weight)
-        high_s_out[...], low_s_out[...] = errors
-        total = total + product(errors, other, NN)
+        there_at = slice(slot * quarter + k * chunk, slot * quarter + (k + 1) * chunk)
+        weights_at = slice(2 * quarter + there_at.start, 2 * quarter + there_at.stop)
+        rating = jnp.concatenate([rating_ref[at, :], sibling_ref[there_at, :]], 1)
+        weight = jnp.concatenate([weight_ref[at, :], sibling_ref[weights_at, :]], 1)
+        high, low = errors_of(item_halves, both, rating, weight)
+        high_out[...], low_out[...] = high[:, :owned], low[:, :owned]
+        high_s_out[...], low_s_out[...] = high[:, owned:], low[:, owned:]
+        total = product((high, low), both, NN)
         if slot == 1:
             total = stepped(now, total, rest[0][rows(k), :])
         out[...] = total

time: 45.6 us -> 45.5 us (level)
  Pallas kernels: 12.2 us -> 11.6 us
  waiting for transfers between devices: 14.8 us -> 15.3 us
    ppermute x6, waiting for transfers between devices: 10.3 us -> 11.5 us  [onward(): return lax.ppermute(value, AXES, pairs)]
    ppermute x12, waiting for transfers between devices: 4.5 us -> 3.84 us  [swap(): return lax.ppermute(value, AXES, pairs)]
    pallas_call x26, Pallas kernels: 12.2 us -> 11.6 us  [call(): pl.pallas_call(kernel, in_specs=[AFTER] * unread + [spec for spec, _ in o...]
  transfers between devices with their start and end apart: 18 -> 18, of which waited for: 10 -> 10; matrix products, arithmetic and copies ran while one was open for 0% -> 0% of each run, Pallas kernels for 21% -> 20%
where the time goes in v7:
time: 45.5 us; the launch traced here: 45.4 us
  starting transfers between devices  17.1 us (38%)
  waiting for transfers between devices  15.3 us (34%)
  Pallas kernels  11.6 us (25%)
  between operations  0.88 us (2%)
  local copies, waits for them, and re-layouts  0.5 us (1%)
    pallas_call x26, Pallas kernels, call(): pl.pallas_call(kernel, in_specs=[AFTER] * unread + [spec for spec, _ in o...  11.6 us
    ppermute x6, waiting for transfers between devices, onward(): return lax.ppermute(value, AXES, pairs)  11.5 us
    ppermute x12, starting transfers between devices, swap(): return lax.ppermute(value, AXES, pairs)  10.4 us
    ppermute x6, starting transfers between devices, onward(): return lax.ppermute(value, AXES, pairs)  6.7 us
    ppermute x12, waiting for transfers between devices, swap(): return lax.ppermute(value, AXES, pairs)  3.84 us
  transfers between devices with their start and end apart: 18, of which 10 were waited for; matrix products, arithmetic and copies ran while one was open for 0% of the time, Pallas kernels for 20%

profile of v7, /device:TPU:1, one launch (start us, length us, event | category | flops | bytes accessed | tf_op | source)
XLA Modules:
  0.0 45.4 jit_solution(17722289319419967652)
XLA Ops:
  0.6 1.9 %first.1 = (bf16[8,256,128]{2,1,0:T(8,128)(2,1)S(1)}, bf16[8,256,128]{2,1,0:T(8,128)(2,1)S(1)}, f32[256,256]{1,0:T(8,128)S(1)}, f32[1024,256]{1,0:T(8,128)S(1)},...) custom-call(s32[1]{0:T(128)} %bitcast.refs_0_.refs_1_.refs_2_, ...), custom_call_target="tpu_custom_call" | custom-call | flops 1610612736 | bytes 262144 | tf_op jit(solution)/shard_map/first/pallas_call | solution.py:62
  2.6 3.3 %collective-permute-start = (f32[256,256]{1,0:T(8,128)S(1)}, f32[256,256]{1,0:T(8,128)S(1)}, u32[]{:S(2)}, u32[]{:S(2)}) collective-permute-start(f32[256,256]{1,0:T(8,128)S(1)} %get-tuple-element.59), channel_id=1, source_target_pairs={{0,1},{1,0},{2,3},{3,2},{4,5},{5,4},{6,7},{7,6},{8,9},{9,8},{10,11... | collective-permute-start | bytes 786440 | tf_op jit(solution)/shard_map/core_swap/ppermute | solution.py:100
  5.9 0.6 %part.3 = (bf16[256,256]{1,0:T(8,128)(2,1)S(1)}, bf16[256,256]{1,0:T(8,128)(2,1)S(1)}, f32[256,256]{1,0:T(8,128)S(1)}) custom-call(s32[1]{0:T(128)} %bitcast.refs_0_.refs_1_.refs_2_, bf16[8,256,128]{2,1,0:T(8,128)(2,1)S(1)} %get-tuple-element.51.refs_1_.refs_2_.refs_3_, bf16[8,256,128]{2,1,0:T(8,128)(2,1)S(1)} %get-tuple-element.52.refs_2_.refs_3_.refs_4_, ...), custom_call_target="tpu_custom_call" | custom-call | flops 1610612736 | bytes 262144 | tf_op jit(solution)/shard_map/part/pallas_call | solution.py:62
  6.6 0.1 collective-permute-start.2
  6.7 0.6 %part.4 = (bf16[256,256]{1,0:T(8,128)(2,1)S(1)}, bf16[256,256]{1,0:T(8,128)(2,1)S(1)}, f32[256,256]{1,0:T(8,128)S(1)}) custom-call(f32[256,256]{1,0:T(8,128)S(1)} %get-tuple-element.53.refs_0_, s32[1]{0:T(128)} %bitcast.refs_0_.refs_1_.refs_2_, bf16[8,256,128]{2,1,0:T(8,128)(2,1)S(1)} %get-tuple-element.51.refs_1_.refs_2_.refs_3_, ...), custom_call_target="tpu_custom_call" | custom-call | flops 1610612736 | bytes 262144 | tf_op jit(solution)/shard_map/part/pallas_call | solution.py:62
  7.3 0.0 collective-permute-done.refs_1_.refs_2_
  7.3 0.1 collective-permute-start.1
  7.5 0.0 copy-start
  7.5 1.5 %collective-permute-start.5 = (f32[128,256]{1,0:T(8,128)S(1)}, f32[128,256]{1,0:T(8,128)S(1)}, u32[]{:S(2)}, u32[]{:S(2)}) collective-permute-start(f32[128,256]{1,0:T(8,128)S(1)} %join.5.refs_1_.refs_4_), channel_id=1, source_target_pairs={{0,2},{1,3},{2,0},{3,1},{4,6},{5,7},{6,4},{7,5},{8,10},{9,11},{10,... | collective-permute-start | bytes 393224 | tf_op jit(solution)/shard_map/chip_swap/ppermute | solution.py:100
  9.0 0.6 %part.5 = (bf16[256,256]{1,0:T(8,128)(2,1)S(1)}, bf16[256,256]{1,0:T(8,128)(2,1)S(1)}, f32[256,256]{1,0:T(8,128)S(1)}) custom-call(f32[128,256]{1,0:T(8,128)S(1)} %join.4.refs_0_.refs_4_, f32[128,256]{1,0:T(8,128)S(1)} %join.5.refs_1_.refs_4_, s32[1]{0:T(128)} %bitcast.refs_0_.refs_1_.refs_2_, ...), custom_call_target="tpu_custom_call" | custom-call | flops 1610612736 | bytes 262144 | tf_op jit(solution)/shard_map/part/pallas_call | solution.py:62
  9.7 0.0 copy-start.1
  9.7 0.0 copy-start.2
  9.7 0.7 %user_step.1.refs_0_.refs_7_.refs_2_.refs_3_.refs_4_ = f32[256,256]{1,0:T(8,128)S(1)} custom-call(s32[1]{0:T(128)} %bitcast.refs_0_.refs_1_.refs_2_, f32[256,256]{1,0:T(8,128)S(1)} %get-tuple-element.49.refs_3_.refs_4_.refs_5_.refs_1_, f32[1024,256]{1,0:T(8,128)S(1)} %get-tuple-element.50.refs_4_.refs_5_.refs_6_.refs_2_.refs_1_, f32[2,256,256]{2,1,0:T(8,128)S(1)} %copy-done, ...), custom_call_target="tpu_custom_call" | custom-call | bytes 262144 | tf_op jit(solution)/shard_map/user_step/pallas_call | solution.py:62
  10.4 0.3 copy-done.1
  10.7 0.2 copy-done.2
  10.9 1.4 %layout.1 = (f32[1024,256]{1,0:T(8,128)S(1)}, f32[1024,256]{1,0:T(8,128)S(1)}, f32[1280,256]{1,0:T(8,128)S(1)}, f32[256,256]{1,0:T(8,128)S(1)}) custom-call(f32[256,256]{1,0:T(8,128)S(1)} %user_step.1.refs_0_.refs_7_.refs_2_.refs_3_.refs_4_, s32[1]{0:T(128)} %bitcast.refs_0_.refs_1_.refs_2_, s32[2,8]{1,0:T(2,128)} %refs_2_.2, s32[2]{0:T(128)} %bitcast.3, ...), custom_call_target="tpu_custom_call" | custom-call | bytes 262144 | tf_op jit(solution)/shard_map/layout/pallas_call | solution.py:62
  12.3 1.2 %collective-permute-start.4 = (f32[1280,256]{1,0:T(8,128)S(1)}, f32[1280,256]{1,0:T(8,128)S(1)}, u32[]{:S(2)}, u32[]{:S(2)}) collective-permute-start(f32[1280,256]{1,0:T(8,128)S(1)} %get-tuple-element.65.refs_0_), channel_id=1, source_target_pairs={{0,1},{1,0},{2,3},{3,2},{4,5},{5,4},{6,7},{7,6},{8,9},{9,8},{10,11... | collective-permute-start | bytes 3932168 | tf_op jit(solution)/shard_map/core_swap/ppermute | solution.py:100
  13.6 0.9 %collective-permute-start.3 = (f32[128,256]{1,0:T(8,128)S(1)}, f32[128,256]{1,0:T(8,128)S(1)}, u32[]{:S(2)}, u32[]{:S(2)}) collective-permute-start(f32[128,256]{1,0:T(8,128)S(1)} %move.4.refs_2_.refs_0_), channel_id=1, source_target_pairs={{0,6},{1,7},{2,4},{3,5},{4,10},{5,11},{6,8},{7,9},{8,14},{9,15},{1... | collective-permute-start | bytes 393224 | tf_op jit(solution)/shard_map/onward/ppermute | solution.py:109
  14.5 0.1 collective-permute-start.7
  14.6 0.2 collective-permute-done.5.refs_1_.refs_5_
  14.8 0.1 move.5.refs_0_
  14.9 1.9 %collective-permute-start.6 = (f32[128,256]{1,0:T(8,128)S(1)}, f32[128,256]{1,0:T(8,128)S(1)}, u32[]{:S(2)}, u32[]{:S(2)}) collective-permute-start(f32[128,256]{1,0:T(8,128)S(1)} %move.5.refs_0_), channel_id=1, source_target_pairs={{0,6},{1,7},{2,4},{3,5},{4,10},{5,11},{6,8},{7,9},{8,14},{9,15},{1... | collective-permute-start | bytes 393224 | tf_op jit(solution)/shard_map/onward/ppermute | solution.py:109
  16.8 0.3 collective-permute-start.10
  17.1 1.3 %collective-permute-done.7.refs_5_ = f32[128,256]{1,0:T(8,128)S(1)} collective-permute-done((f32[128,256]{1,0:T(8,128)S(1)}, f32[128,256]{1,0:T(8,128)S(1)}, u32[]{:S(2)}, u32[]{:S(2)}) %collective-permute-start.7) | collective-permute-done | bytes 131104 | tf_op jit(solution)/shard_map/chip_swap/ppermute | solution.py:100
  18.4 1.8 %collective-permute-start.8 = (f32[128,256]{1,0:T(8,128)S(1)}, f32[128,256]{1,0:T(8,128)S(1)}, u32[]{:S(2)}, u32[]{:S(2)}) collective-permute-start(f32[128,256]{1,0:T(8,128)S(1)} %move.6.refs_0_), channel_id=1, source_target_pairs={{0,6},{1,7},{2,4},{3,5},{4,10},{5,11},{6,8},{7,9},{8,14},{9,15},{1... | collective-permute-start | bytes 393224 | tf_op jit(solution)/shard_map/onward/ppermute | solution.py:109
  20.2 1.0 %collective-permute-done.10.refs_5_ = f32[128,256]{1,0:T(8,128)S(1)} collective-permute-done((f32[128,256]{1,0:T(8,128)S(1)}, f32[128,256]{1,0:T(8,128)S(1)}, u32[]{:S(2)}, u32[]{:S(2)}) %collective-permute-start.10) | collective-permute-done | bytes 131104 | tf_op jit(solution)/shard_map/chip_swap/ppermute | solution.py:100
  21.2 1.9 %collective-permute-start.11 = (f32[128,256]{1,0:T(8,128)S(1)}, f32[128,256]{1,0:T(8,128)S(1)}, u32[]{:S(2)}, u32[]{:S(2)}) collective-permute-start(f32[128,256]{1,0:T(8,128)S(1)} %move.7), channel_id=1, source_target_pairs={{0,6},{1,7},{2,4},{3,5},{4,10},{5,11},{6,8},{7,9},{8,14},{9,15},{1... | collective-permute-start | bytes 393224 | tf_op jit(solution)/shard_map/onward/ppermute | solution.py:109
  23.1 2.1 %collective-permute-done.3.refs_1_.refs_6_ = f32[128,256]{1,0:T(8,128)S(1)} collective-permute-done((f32[128,256]{1,0:T(8,128)S(1)}, f32[128,256]{1,0:T(8,128)S(1)}, u32[]{:S(2)}, u32[]{:S(2)}) %collective-permute-start.3) | collective-permute-done | bytes 131104 | tf_op jit(solution)/shard_map/onward/ppermute | solution.py:109
  25.3 0.7 %late.4 = (bf16[128,256]{1,0:T(8,128)(2,1)S(1)}, bf16[128,256]{1,0:T(8,128)(2,1)S(1)}, bf16[128,256]{1,0:T(8,128)(2,1)S(1)}, bf16[128,256]{1,0:T(8,128)(2,1)S(1)}, f32[128,256]{1,0:T(8,128)S(1)}) custom-call(s32[1]{0:T(128)} %bitcast.refs_0_.refs_1_.refs_2_, f32[128,256]{1,0:T(8,128)S(1)} %collective-permute-done.3.refs_1_.refs_6_, ...), custom_call_target="tpu_custom_call" | custom-call | flops 1610612736 | bytes 262144 | tf_op jit(solution)/shard_map/late/pallas_call | solution.py:62
  26.0 0.1 collective-permute-start.9
  26.1 2.0 %collective-permute-done.6.refs_2_.refs_11_ = f32[128,256]{1,0:T(8,128)S(1)} collective-permute-done((f32[128,256]{1,0:T(8,128)S(1)}, f32[128,256]{1,0:T(8,128)S(1)}, u32[]{:S(2)}, u32[]{:S(2)}) %collective-permute-start.6) | collective-permute-done | bytes 131104 | tf_op jit(solution)/shard_map/onward/ppermute | solution.py:109
  28.1 0.7 %late.5 = (bf16[128,256]{1,0:T(8,128)(2,1)S(1)}, bf16[128,256]{1,0:T(8,128)(2,1)S(1)}, bf16[128,256]{1,0:T(8,128)(2,1)S(1)}, bf16[128,256]{1,0:T(8,128)(2,1)S(1)}, f32[128,256]{1,0:T(8,128)S(1)}) custom-call(f32[128,256]{1,0:T(8,128)S(1)} %get-tuple-element.69.refs_0_, s32[1]{0:T(128)} %bitcast.refs_0_.refs_1_.refs_2_, ...), custom_call_target="tpu_custom_call" | custom-call | flops 1610612736 | bytes 262144 | tf_op jit(solution)/shard_map/late/pallas_call | solution.py:62
  28.8 0.3 collective-permute-start.12
  29.1 1.1 %collective-permute-done.8.refs_2_.refs_16_ = f32[128,256]{1,0:T(8,128)S(1)} collective-permute-done((f32[128,256]{1,0:T(8,128)S(1)}, f32[128,256]{1,0:T(8,128)S(1)}, u32[]{:S(2)}, u32[]{:S(2)}) %collective-permute-start.8) | collective-permute-done | bytes 131104 | tf_op jit(solution)/shard_map/onward/ppermute | solution.py:109
  30.1 0.7 %late.6 = (bf16[128,256]{1,0:T(8,128)(2,1)S(1)}, bf16[128,256]{1,0:T(8,128)(2,1)S(1)}, bf16[128,256]{1,0:T(8,128)(2,1)S(1)}, bf16[128,256]{1,0:T(8,128)(2,1)S(1)}, f32[128,256]{1,0:T(8,128)S(1)}) custom-call(f32[128,256]{1,0:T(8,128)S(1)} %get-tuple-element.70.refs_0_, s32[1]{0:T(128)} %bitcast.refs_0_.refs_1_.refs_2_, ...), custom_call_target="tpu_custom_call" | custom-call | flops 1610612736 | bytes 262144 | tf_op jit(solution)/shard_map/late/pallas_call | solution.py:62
  30.9 0.1 collective-permute-start.16
  31.0 2.2 %collective-permute-done.11.refs_3_.refs_21_ = f32[128,256]{1,0:T(8,128)S(1)} collective-permute-done((f32[128,256]{1,0:T(8,128)S(1)}, f32[128,256]{1,0:T(8,128)S(1)}, u32[]{:S(2)}, u32[]{:S(2)}) %collective-permute-start.11) | collective-permute-done | bytes 131104 | tf_op jit(solution)/shard_map/onward/ppermute | solution.py:109
  33.2 0.7 %late.7 = (bf16[128,256]{1,0:T(8,128)(2,1)S(1)}, bf16[128,256]{1,0:T(8,128)(2,1)S(1)}, bf16[128,256]{1,0:T(8,128)(2,1)S(1)}, bf16[128,256]{1,0:T(8,128)(2,1)S(1)}, f32[128,256]{1,0:T(8,128)S(1)}) custom-call(f32[128,256]{1,0:T(8,128)S(1)} %get-tuple-element.70.refs_0_, f32[128,256]{1,0:T(8,128)S(1)} %add_scaled.2.refs_1_.refs_0_, ...), custom_call_target="tpu_custom_call" | custom-call | flops 1610612736 | bytes 262144 | tf_op jit(solution)/shard_map/late/pallas_call | solution.py:62
  33.9 0.5 collective-permute-done.12.refs_1_
  34.4 0.1 collective-permute-start.17
  34.5 1.0 %user_sums.1 = (f32[256,256]{1,0:T(8,128)S(1)}, f32[88,256]{1,0:T(8,128)S(1)}, f32[88,256]{1,0:T(8,128)S(1)}, f32[80,256]{1,0:T(8,128)S(1)}) custom-call(f32[128,256]{1,0:T(8,128)S(1)} %add_scaled.2.refs_1_.refs_0_, f32[128,256]{1,0:T(8,128)S(1)} %add_scaled.3.refs_1_, bf16[128,256]{1,0:T(8,128)(2,1)S(1)} %get-tuple-element.74.refs_2_, ...), custom_call_target="tpu_custom_call" | custom-call | flops 51539607552 | bytes 262144 | tf_op jit(solution)/shard_map/user_sums/pallas_call | solution.py:62
  35.5 2.8 %collective-permute-start.13 = (f32[88,256]{1,0:T(8,128)S(1)}, f32[88,256]{1,0:T(8,128)S(1)}, u32[]{:S(2)}, u32[]{:S(2)}) collective-permute-start(f32[88,256]{1,0:T(8,128)S(1)} %get-tuple-element.91), channel_id=1, source_target_pairs={{0,1},{1,0},{2,3},{3,2},{4,5},{5,4},{6,7},{7,6},{8,9},{9,8},{10,11... | collective-permute-start | bytes 270344 | tf_op jit(solution)/shard_map/core_swap/ppermute | solution.py:100
  38.3 0.1 collective-permute-start.14
  38.4 0.4 collective-permute-start.15
  38.8 0.9 %collective-permute-done.15.refs_5_ = f32[80,256]{1,0:T(8,128)S(1)} collective-permute-done((f32[80,256]{1,0:T(8,128)S(1)}, f32[80,256]{1,0:T(8,128)S(1)}, u32[]{:S(2)}, u32[]{:S(2)}) %collective-permute-start.15) | collective-permute-done | bytes 81952 | tf_op jit(solution)/shard_map/core_swap/ppermute | solution.py:100
  39.7 0.8 %last.1 = (f32[256,256]{1,0:T(8,128)}, f32[8,128]{1,0:T(8,128)S(1)}) custom-call(f32[256,256]{1,0:T(8,128)S(1)} %user_step.1.refs_0_.refs_7_.refs_2_.refs_3_.refs_4_, f32[256,256]{1,0:T(8,128)S(1)} %get-tuple-element.90.refs_1_, f32[2,256,256]{2,1,0:T(8,128)S(1)} %copy-done, f32[88,256]{1,0:T(8,128)S(1)} %collective-permute-done.13.refs_3_, ...), custom_call_target="tpu_custom_call" | custom-call | bytes 262144 | tf_op jit(solution)/shard_map/last/pallas_call | solution.py:62
  40.5 4.1 %collective-permute-done.17.refs_1_ = f32[128,256]{1,0:T(8,128)S(1)} collective-permute-done((f32[128,256]{1,0:T(8,128)S(1)}, f32[128,256]{1,0:T(8,128)S(1)}, u32[]{:S(2)}, u32[]{:S(2)}) %collective-permute-start.17) | collective-permute-done | bytes 131104 | tf_op jit(solution)/shard_map/onward/ppermute | solution.py:109
  44.7 0.7 %stack.1 = f32[256,256]{1,0:T(8,128)} custom-call(f32[128,256]{1,0:T(8,128)S(1)} %relay.5.refs_0_, f32[128,256]{1,0:T(8,128)S(1)} %collective-permute-done.17.refs_1_), custom_call_target="tpu_custom_call" | custom-call | flops 8 | bytes 262144 | tf_op jit(solution)/shard_map/stack/pallas_call | solution.py:62
  (20 shorter events, 0.3 us)
Async XLA Ops:
  2.6 4.7 %collective-permute-start = (f32[256,256]{1,0:T(8,128)S(1)}, f32[256,256]{1,0:T(8,128)S(1)}, u32[]{:S(2)}, u32[]{:S(2)}) collective-permute-start(f32[256,256]{1,0:T(8,128)S(1)} %get-tuple-element.59), channel_id=1, source_target_pairs={{0,1},{1,0},{2,3},{3,2},{4,5},{5,4},{6,7},{7,6},{8,9},{9,8},{10,11... | collective-permute-start | bytes 786440 | tf_op jit(solution)/shard_map/core_swap/ppermute | solution.py:100
  6.6 6.9 %collective-permute-start.2 = (f32[256,256]{1,0:T(8,128)S(1)}, f32[256,256]{1,0:T(8,128)S(1)}, u32[]{:S(2)}, u32[]{:S(2)}) collective-permute-start(f32[256,256]{1,0:T(8,128)S(1)} %get-tuple-element.53.refs_0_), channel_id=1, source_target_pairs={{0,1},{1,0},{2,3},{3,2},{4,5},{5,4},{6,7},{7,6},{8,9},{9,8},{10,11... | collective-permute-start | bytes 786440 | tf_op jit(solution)/shard_map/core_swap/ppermute | solution.py:100
  7.3 6.2 %collective-permute-start.1 = (f32[128,256]{1,0:T(8,128)S(1)}, f32[128,256]{1,0:T(8,128)S(1)}, u32[]{:S(2)}, u32[]{:S(2)}) collective-permute-start(f32[128,256]{1,0:T(8,128)S(1)} %join.4.refs_0_.refs_4_), channel_id=1, source_target_pairs={{0,2},{1,3},{2,0},{3,1},{4,6},{5,7},{6,4},{7,5},{8,10},{9,11},{10,... | collective-permute-start | bytes 393224 | tf_op jit(solution)/shard_map/chip_swap/ppermute | solution.py:100
  7.5 2.2 %copy-start = (f32[2,256,256]{2,1,0:T(8,128)S(1)}, f32[2,256,256]{2,1,0:T(8,128)}, u32[]{:S(2)}) copy-start(f32[2,256,256]{2,1,0:T(8,128)} %refs_2_.3) | copy-start | bytes 1572868
  7.5 7.3 %collective-permute-start.5 = (f32[128,256]{1,0:T(8,128)S(1)}, f32[128,256]{1,0:T(8,128)S(1)}, u32[]{:S(2)}, u32[]{:S(2)}) collective-permute-start(f32[128,256]{1,0:T(8,128)S(1)} %join.5.refs_1_.refs_4_), channel_id=1, source_target_pairs={{0,2},{1,3},{2,0},{3,1},{4,6},{5,7},{6,4},{7,5},{8,10},{9,11},{10,... | collective-permute-start | bytes 393224 | tf_op jit(solution)/shard_map/chip_swap/ppermute | solution.py:100
  9.7 1.0 %copy-start.1 = (bf16[2,8,128,128]{3,2,1,0:T(8,128)(2,1)S(1)}, bf16[2,8,128,128]{3,2,1,0:T(8,128)(2,1)}, u32[]{:S(2)}) copy-start(bf16[2,8,128,128]{3,2,1,0:T(8,128)(2,1)} %refs_5_.3) | copy-start | bytes 1572868
  9.7 1.2 %copy-start.2 = (bf16[2,8,128,128]{3,2,1,0:T(8,128)(2,1)S(1)}, bf16[2,8,128,128]{3,2,1,0:T(8,128)(2,1)}, u32[]{:S(2)}) copy-start(bf16[2,8,128,128]{3,2,1,0:T(8,128)(2,1)} %refs_6_.3) | copy-start | bytes 1572868
  12.3 13.0 %collective-permute-start.4 = (f32[1280,256]{1,0:T(8,128)S(1)}, f32[1280,256]{1,0:T(8,128)S(1)}, u32[]{:S(2)}, u32[]{:S(2)}) collective-permute-start(f32[1280,256]{1,0:T(8,128)S(1)} %get-tuple-element.65.refs_0_), channel_id=1, source_target_pairs={{0,1},{1,0},{2,3},{3,2},{4,5},{5,4},{6,7},{7,6},{8,9},{9,8},{10,11... | collective-permute-start | bytes 3932168 | tf_op jit(solution)/shard_map/core_swap/ppermute | solution.py:100
  13.6 11.7 %collective-permute-start.3 = (f32[128,256]{1,0:T(8,128)S(1)}, f32[128,256]{1,0:T(8,128)S(1)}, u32[]{:S(2)}, u32[]{:S(2)}) collective-permute-start(f32[128,256]{1,0:T(8,128)S(1)} %move.4.refs_2_.refs_0_), channel_id=1, source_target_pairs={{0,6},{1,7},{2,4},{3,5},{4,10},{5,11},{6,8},{7,9},{8,14},{9,15},{1... | collective-permute-start | bytes 393224 | tf_op jit(solution)/shard_map/onward/ppermute | solution.py:109
  14.5 3.8 %collective-permute-start.7 = (f32[128,256]{1,0:T(8,128)S(1)}, f32[128,256]{1,0:T(8,128)S(1)}, u32[]{:S(2)}, u32[]{:S(2)}) collective-permute-start(f32[128,256]{1,0:T(8,128)S(1)} %relay.3), channel_id=1, source_target_pairs={{0,2},{1,3},{2,0},{3,1},{4,6},{5,7},{6,4},{7,5},{8,10},{9,11},{10,... | collective-permute-start | bytes 393224 | tf_op jit(solution)/shard_map/chip_swap/ppermute | solution.py:100
  14.9 13.2 %collective-permute-start.6 = (f32[128,256]{1,0:T(8,128)S(1)}, f32[128,256]{1,0:T(8,128)S(1)}, u32[]{:S(2)}, u32[]{:S(2)}) collective-permute-start(f32[128,256]{1,0:T(8,128)S(1)} %move.5.refs_0_), channel_id=1, source_target_pairs={{0,6},{1,7},{2,4},{3,5},{4,10},{5,11},{6,8},{7,9},{8,14},{9,15},{1... | collective-permute-start | bytes 393224 | tf_op jit(solution)/shard_map/onward/ppermute | solution.py:109
  16.8 4.4 %collective-permute-start.10 = (f32[128,256]{1,0:T(8,128)S(1)}, f32[128,256]{1,0:T(8,128)S(1)}, u32[]{:S(2)}, u32[]{:S(2)}) collective-permute-start(f32[128,256]{1,0:T(8,128)S(1)} %relay.4), channel_id=1, source_target_pairs={{0,2},{1,3},{2,0},{3,1},{4,6},{5,7},{6,4},{7,5},{8,10},{9,11},{10,... | collective-permute-start | bytes 393224 | tf_op jit(solution)/shard_map/chip_swap/ppermute | solution.py:100
  18.4 11.7 %collective-permute-start.8 = (f32[128,256]{1,0:T(8,128)S(1)}, f32[128,256]{1,0:T(8,128)S(1)}, u32[]{:S(2)}, u32[]{:S(2)}) collective-permute-start(f32[128,256]{1,0:T(8,128)S(1)} %move.6.refs_0_), channel_id=1, source_target_pairs={{0,6},{1,7},{2,4},{3,5},{4,10},{5,11},{6,8},{7,9},{8,14},{9,15},{1... | collective-permute-start | bytes 393224 | tf_op jit(solution)/shard_map/onward/ppermute | solution.py:109
  21.2 12.0 %collective-permute-start.11 = (f32[128,256]{1,0:T(8,128)S(1)}, f32[128,256]{1,0:T(8,128)S(1)}, u32[]{:S(2)}, u32[]{:S(2)}) collective-permute-start(f32[128,256]{1,0:T(8,128)S(1)} %move.7), channel_id=1, source_target_pairs={{0,6},{1,7},{2,4},{3,5},{4,10},{5,11},{6,8},{7,9},{8,14},{9,15},{1... | collective-permute-start | bytes 393224 | tf_op jit(solution)/shard_map/onward/ppermute | solution.py:109
  26.0 4.9 %collective-permute-start.9 = (f32[128,256]{1,0:T(8,128)S(1)}, f32[128,256]{1,0:T(8,128)S(1)}, u32[]{:S(2)}, u32[]{:S(2)}) collective-permute-start(f32[128,256]{1,0:T(8,128)S(1)} %get-tuple-element.69.refs_0_), channel_id=1, source_target_pairs={{0,2},{1,3},{2,0},{3,1},{4,6},{5,7},{6,4},{7,5},{8,10},{9,11},{10,... | collective-permute-start | bytes 393224 | tf_op jit(solution)/shard_map/chip_swap/ppermute | solution.py:100
  28.8 5.6 %collective-permute-start.12 = (f32[128,256]{1,0:T(8,128)S(1)}, f32[128,256]{1,0:T(8,128)S(1)}, u32[]{:S(2)}, u32[]{:S(2)}) collective-permute-start(f32[128,256]{1,0:T(8,128)S(1)} %get-tuple-element.70.refs_0_), channel_id=1, source_target_pairs={{0,2},{1,3},{2,0},{3,1},{4,6},{5,7},{6,4},{7,5},{8,10},{9,11},{10,... | collective-permute-start | bytes 393224 | tf_op jit(solution)/shard_map/chip_swap/ppermute | solution.py:100
  30.9 9.6 %collective-permute-start.16 = (f32[128,256]{1,0:T(8,128)S(1)}, f32[128,256]{1,0:T(8,128)S(1)}, u32[]{:S(2)}, u32[]{:S(2)}) collective-permute-start(f32[128,256]{1,0:T(8,128)S(1)} %add_scaled.2.refs_1_.refs_0_), channel_id=1, source_target_pairs={{0,6},{1,7},{2,4},{3,5},{4,10},{5,11},{6,8},{7,9},{8,14},{9,15},{1... | collective-permute-start | bytes 393224 | tf_op jit(solution)/shard_map/onward/ppermute | solution.py:109
  34.4 10.3 %collective-permute-start.17 = (f32[128,256]{1,0:T(8,128)S(1)}, f32[128,256]{1,0:T(8,128)S(1)}, u32[]{:S(2)}, u32[]{:S(2)}) collective-permute-start(f32[128,256]{1,0:T(8,128)S(1)} %add_scaled.3.refs_1_), channel_id=1, source_target_pairs={{0,6},{1,7},{2,4},{3,5},{4,10},{5,11},{6,8},{7,9},{8,14},{9,15},{1... | collective-permute-start | bytes 393224 | tf_op jit(solution)/shard_map/onward/ppermute | solution.py:109
  35.5 4.3 %collective-permute-start.13 = (f32[88,256]{1,0:T(8,128)S(1)}, f32[88,256]{1,0:T(8,128)S(1)}, u32[]{:S(2)}, u32[]{:S(2)}) collective-permute-start(f32[88,256]{1,0:T(8,128)S(1)} %get-tuple-element.91), channel_id=1, source_target_pairs={{0,1},{1,0},{2,3},{3,2},{4,5},{5,4},{6,7},{7,6},{8,9},{9,8},{10,11... | collective-permute-start | bytes 270344 | tf_op jit(solution)/shard_map/core_swap/ppermute | solution.py:100
  38.3 1.4 %collective-permute-start.14 = (f32[88,256]{1,0:T(8,128)S(1)}, f32[88,256]{1,0:T(8,128)S(1)}, u32[]{:S(2)}, u32[]{:S(2)}) collective-permute-start(f32[88,256]{1,0:T(8,128)S(1)} %get-tuple-element.92), channel_id=1, source_target_pairs={{0,1},{1,0},{2,3},{3,2},{4,5},{5,4},{6,7},{7,6},{8,9},{9,8},{10,11... | collective-permute-start | bytes 270344 | tf_op jit(solution)/shard_map/core_swap/ppermute | solution.py:100
  38.4 1.3 %collective-permute-start.15 = (f32[80,256]{1,0:T(8,128)S(1)}, f32[80,256]{1,0:T(8,128)S(1)}, u32[]{:S(2)}, u32[]{:S(2)}) collective-permute-start(f32[80,256]{1,0:T(8,128)S(1)} %get-tuple-element.93), channel_id=1, source_target_pairs={{0,1},{1,0},{2,3},{3,2},{4,5},{5,4},{6,7},{7,6},{8,9},{9,8},{10,11... | collective-permute-start | bytes 245768 | tf_op jit(solution)/shard_map/core_swap/ppermute | solution.py:100
